TPU v7x, 32 devices: a whole 2x2x4 slice. The times are simulated.
32 devices in a mesh: traj: 4 (over y, core), grid: 8 (over z, x).
Axes of the slice: x: 2, y: 2, z: 4, core: 2. Of those that a mesh axis runs over, the one named last changes fastest.
Arguments:
- state: bfloat16 [16, 24, 640, 1280], P('traj', None, 'grid'), may hold values from -6 to 6
- counts: int32 [16], replicated, may hold values from 0 to 4, as said below
- slot_perm: int32 [16], replicated, may hold values from 0 to 15, each once
- legendre: bfloat16 [640, 2, 320, 320], P(('traj', 'grid')), may hold values from -0.3125 to 0.3125
- quad_weight: float32 [320], replicated, may hold values from 0.5 to 1.5
- diffusion: float32 [24], replicated, may hold values from 0.5 to 20
Outputs:
- smoothed: bfloat16 [16, 24, 640, 1280], P('traj', None, 'grid')
Inputs may be any that keep to these rules, and one draw needn't show every extreme that they name: Offspring counts of the 16 trajectories; they sum to 16, at least one trajectory has 4 copies, and at least one has none. `slot_perm`: each of the 16 slots appears once.
All inputs are finite; a program needn't handle non-finite values.
Results may differ from a plain program's by a relative error of at most 0.0077.
Values may be sent and summed in bfloat16 or wider, within the bound.
No kernel may reach another device: no remote copies, remote signals or barrier semaphores. Data moves between devices by JAX's collectives and lax.ppermute only.
A program may use at most 256 MiB of HBM per device.

v0:
```python
import math

import jax
import jax.numpy as jnp
from jax import lax
from jax.sharding import PartitionSpec as P


def parent_slots(counts, slot_perm):
    member_count = counts.shape[0]
    position = jnp.arange(member_count, dtype=jnp.int32)
    copy_end = jnp.cumsum(counts)
    copy_parent = jnp.sum((copy_end[None, :] <= position[:, None]).astype(jnp.int32), axis=1)
    landing = (slot_perm[:, None] == position[None, :]).astype(jnp.int32)
    return jnp.sum(landing * copy_parent[:, None], axis=0)


def trig_pair(wave_order, lon_count):
    lon_points = jnp.arange(lon_count, dtype=jnp.int32)
    phase_angle = (wave_order[:, None] * lon_points[None, :] % lon_count).astype(jnp.float32) * (
        2.0 * math.pi / lon_count
    )
    return jnp.stack([jnp.cos(phase_angle), -jnp.sin(phase_angle)], axis=1)


def forward_table(wave_order, lon_count):
    return (trig_pair(wave_order, lon_count) / lon_count).astype(jnp.bfloat16)


def inverse_table(wave_order, lon_count):
    doubled = jnp.where(wave_order == 0, 1.0, 2.0).astype(jnp.float32)
    return (trig_pair(wave_order, lon_count) * doubled[:, None, None]).astype(jnp.bfloat16)


def gathered_order(wave_count, group_count, slab_count):
    per_device = wave_count // (group_count * slab_count)
    per_slab = wave_count // slab_count
    position = jnp.arange(wave_count, dtype=jnp.int32)
    lat_slab = position // per_slab
    within = position % per_slab
    return (within // per_device * slab_count + lat_slab) * per_device + within % per_device


def spectral_filter(wave_rows, legendre_table, wave_ids, quad_weight, rate_cols):
    wave_here, slot_count, lat_count, col_count = wave_rows.shape
    hemisphere = lat_count // 2
    weight_col = quad_weight[:, None]
    north_rows = wave_rows[:, :, :hemisphere].astype(jnp.float32)
    south_rows = jnp.flip(wave_rows[:, :, hemisphere:], axis=2).astype(jnp.float32)
    even_sum = ((north_rows + south_rows) * weight_col).astype(jnp.bfloat16)
    odd_diff = ((north_rows - south_rows) * weight_col).astype(jnp.bfloat16)
    paired = jnp.stack([even_sum, odd_diff], axis=1)
    spectrum = jnp.einsum(
        "mpkl,mpslc->mpksc", legendre_table, paired, preferred_element_type=jnp.float32
    )
    parity = jnp.arange(2, dtype=jnp.int32)
    degree = (
        2 * jnp.arange(hemisphere, dtype=jnp.int32)[None, None, :]
        + (wave_ids[:, None, None] + parity[None, :, None]) % 2
    )
    degree_ratio = (degree * (degree + 1)).astype(jnp.float32) / float(lat_count * (lat_count - 1))
    damping = 1.0 / (
        1.0 + rate_cols[None, None, None, None, :] * (degree_ratio * degree_ratio)[..., None, None]
    )
    retained = (degree >= wave_ids[:, None, None])[..., None, None]
    filtered = jnp.where(retained, spectrum * damping, 0.0).astype(jnp.bfloat16)
    returned = jnp.einsum(
        "mpkl,mpksc->mpslc", legendre_table, filtered, preferred_element_type=jnp.float32
    )
    north_out = returned[:, 0] + returned[:, 1]
    south_out = returned[:, 0] - returned[:, 1]
    lat_rows = jnp.concatenate([north_out, jnp.flip(south_out, axis=2)], axis=2)
    return lat_rows.astype(jnp.bfloat16)


def on_device(state, counts, slot_perm, legendre, quad_weight, diffusion):
    parents = parent_slots(counts, slot_perm)
    group_count = lax.axis_size("traj")
    slab_count = lax.axis_size("grid")
    group_index = lax.axis_index("traj")
    slab_index = lax.axis_index("grid")
    member_here, field_count, lat_here, lon_count = state.shape
    wave_count = lon_count // 2
    per_device = wave_count // (group_count * slab_count)
    regrouped = gathered_order(wave_count, group_count, slab_count)
    natural = jnp.arange(wave_count, dtype=jnp.int32)
    wave_rows = jnp.einsum(
        "tflj,mrj->mtlrf",
        state,
        forward_table(natural, lon_count),
        preferred_element_type=jnp.float32,
    )
    wave_rows = wave_rows.astype(jnp.bfloat16).reshape(
        wave_count, member_here, lat_here, 2 * field_count
    )
    spread_rows = lax.all_to_all(
        lax.all_to_all(wave_rows, "traj", split_axis=0, concat_axis=1, tiled=True),
        "grid",
        split_axis=0,
        concat_axis=2,
        tiled=True,
    )
    cloned = jnp.take(spread_rows, parents, axis=1)
    wave_ids = (group_index * slab_count + slab_index) * per_device + jnp.arange(
        per_device, dtype=jnp.int32
    )
    rate_cols = jnp.broadcast_to(diffusion, (2, field_count)).reshape(-1)
    filtered = spectral_filter(cloned, legendre, wave_ids, quad_weight, rate_cols)
    returned = lax.all_to_all(
        lax.all_to_all(filtered, "traj", split_axis=1, concat_axis=0, tiled=True),
        "grid",
        split_axis=2,
        concat_axis=0,
        tiled=True,
    )
    returned = returned.reshape(wave_count, member_here, lat_here, 2, field_count)
    inverse = inverse_table(regrouped, lon_count)
    smoothed = jnp.einsum("mtlrf,mrj->tflj", returned, inverse, preferred_element_type=jnp.float32)
    return smoothed.astype(jnp.bfloat16)


def solution(mesh):
    return jax.shard_map(
        on_device,
        mesh=mesh,
        in_specs=(
            P("traj", None, "grid", None),
            P(),
            P(),
            P(("traj", "grid"), None, None, None),
            P(),
            P(),
        ),
        out_specs=P("traj", None, "grid", None),
        check_vma=False,
    )
```

profile of v0, /device:TPU:17, one launch (start us, length us, event | category | flops | bytes accessed | tf_op | source)
XLA Modules:
  0.0 2720.6 jit_solution(9948043184061403408)
XLA Ops:
  0.0 14.5 sine_negate_fusion
  14.5 30.8 %convert_bitcast_fusion = bf16[640,4,80,2,24]{0,2,4,1,3:T(8,128)(2,1)S(1)} fusion(bf16[4,24,80,1280]{3,2,1,0:T(8,128)(2,1)} %param.6, f32[640,1,1280]{2,0,1:T(8,128)} %get-tuple-element.9, f32[640,1,1280]{2,0,1:T(8,128)} %get-tuple-element.10), kind=kOutput, calls=%fused_computation.30 | convolution fusion | flops 25180569600 | bytes 45875200 | tf_op jit(solution)/shard_map/tflj,mrj->mtlrf/dot_general | solution.py:87
  45.3 11.1 copy.68
  56.3 40.1 %copy.69 = bf16[640,4,80,48]{2,3,1,0:T(8,128)(2,1)} copy(bf16[640,4,80,48]{0,3,2,1:T(8,128)(2,1)} %bitcast.107) | data formatting | bytes 39321600 | tf_op jit(solution)/shard_map/reshape | solution.py:93
  96.4 357.2 %all_to_all.69 = bf16[640,4,80,48]{2,3,1,0:T(8,128)(2,1)} all-to-all(bf16[640,4,80,48]{2,3,1,0:T(8,128)(2,1)} %copy.69), channel_id=1, replica_groups=mesh['traj'=4,'grid'=8] {'traj'}, dimensions={0} | all-to-all | bytes 39321600 | tf_op jit(solution)/shard_map/all_to_all | solution.py:97
  453.6 69.2 %copy.88 = bf16[4,160,4,80,48]{1,0,4,3,2:T(4,128)(2,1)} copy(bf16[4,160,4,80,48]{3,4,2,1,0:T(8,128)(2,1)} %bitcast.103) | data formatting | bytes 39321600 | tf_op jit(solution)/shard_map/all_to_all | solution.py:97
  522.8 86.8 %copy.71 = bf16[160,4,4,80,48]{3,4,2,1,0:T(8,128)(2,1)} copy(bf16[160,4,4,80,48]{0,1,4,3,2:T(4,128)(2,1)} %bitcast.104) | data formatting | bytes 39321600 | tf_op jit(solution)/shard_map/all_to_all | solution.py:97
  609.6 0.0 copy-start.4
  609.6 0.0 copy-start.5
  609.6 0.0 copy-start.6
  609.6 7.2 all-to-all-start.1
  616.8 0.0 copy-done.4
  616.8 0.1 copy.67
  616.9 0.1 reduce
  617.1 0.0 copy-done.5
  617.1 0.1 mul.237
  617.2 0.1 convert_reduce_fusion
  617.3 0.0 copy-done.6
  617.3 0.1 select_reduce_fusion
  617.4 0.1 add_select_fusion.2
  617.5 0.1 add_compare_fusion
  617.6 0.1 fusion.61
  617.7 0.5 add_divide_fusion
  618.2 672.8 %all-to-all-done.1 = bf16[160,16,80,48]{2,3,1,0:T(8,128)(2,1)} async-done(((bf16[160,16,80,48]{2,3,1,0:T(8,128)(2,1)}), bf16[160,16,80,48]{2,3,1,0:T(8,128)(2,1)}, u32[]{:S(2)}, u32[]{:S(2)}) %all-to-all-start.1) | async-done | bytes 19660832 | tf_op jit(solution)/shard_map/all_to_all | solution.py:96
  1291.0 62.8 %copy.101 = bf16[8,20,16,80,48]{3,0,4,2,1:T(8,128)(2,1)} copy(bf16[8,20,16,80,48]{3,4,2,1,0:T(8,128)(2,1)} %bitcast.11) | data formatting | bytes 39321600 | tf_op jit(solution)/shard_map/all_to_all | solution.py:96
  1353.8 44.8 %all_to_all.57 = bf16[20,16,640,48]{2,3,1,0:T(8,128)(2,1)} reshape(bf16[20,16,8,80,48]{3,2,4,1,0:T(8,128)(2,1)} %bitcast.105) | data formatting | bytes 39321600 | tf_op jit(solution)/shard_map/all_to_all | solution.py:96
  1398.7 15.1 gather_fusion
  1413.8 10.3 fusion.23
  1424.1 0.0 copy-start
  1424.1 7.1 copy-done
  1431.2 7.9 slice.21
  1439.1 0.0 copy-start.3
  1439.1 30.7 %reverse = bf16[20,16,384,48]{2,3,1,0:T(8,128)(2,1)} reverse(bf16[20,16,384,48]{2,3,1,0:T(8,128)(2,1)} %bitcast.111), dimensions={2} | reverse | bytes 23592960
  1469.8 0.0 copy-done.3
  1469.8 0.0 copy-start.1
  1469.8 19.1 fusion.34
  1489.0 0.0 copy-done.1
  1489.0 6.4 fusion.33
  1495.3 40.8 %fusion.27 = f32[20,2,16,320,48]{3,4,2,1,0:T(8,128)} fusion(f32[20,2,320,48]{2,3,1,0:T(8,128)S(1)} %add_divide_fusion, pred[20,2,320]{2,1,0:T(4,128)(4,1)S(1)} %add_compare_fusion, bf16[20,1,16,320,48]{3,4,2,1,0:T(8,128)(2,1)} %fusion.33, bf16[20,1,16,320,48]{3,4,2,1,0:T(8,128)(2,1)} %get-tuple-element.5, bf16[20,2,320,320]{3,2,1,0:T(8,128)(2,1)} %param.9), kind=kOutput, calls=%fused_computation.32 | convolution fusion | flops 12622233600 | bytes 69644800 | tf_op jit(solution)/shard_map/mpkl,mpksc->mpslc/dot_general | solution.py:67
  1536.2 20.2 subtract_bitcast_fusion
  1556.4 20.2 fusion.32
  1576.6 30.7 %reverse.1 = bf16[20,16,384,48]{2,3,1,0:T(8,128)(2,1)} reverse(bf16[20,16,384,48]{2,3,1,0:T(8,128)(2,1)} %bitcast.110), dimensions={2} | reverse | bytes 23592960
  1607.2 0.0 copy-start.2
  1607.2 13.4 slice.35
  1620.6 0.0 copy-done.2
  1620.6 13.1 pad_maximum_fusion
  1633.8 6.0 copy.78
  1639.8 217.7 %all_to_all.70 = bf16[20,16,640,48]{2,3,0,1:T(8,128)(2,1)S(1)} all-to-all(bf16[20,16,640,48]{2,3,0,1:T(8,128)(2,1)S(1)} %copy.78), channel_id=1, replica_groups=mesh['traj'=4,'grid'=8] {'traj'}, dimensions={1} | all-to-all | bytes 39321600 | tf_op jit(solution)/shard_map/all_to_all | solution.py:110
  1857.5 7.0 copy.80
  1864.4 40.1 %copy.81 = bf16[80,4,640,48]{0,3,1,2:T(8,128)(2,1)} copy(bf16[80,4,640,48]{2,3,1,0:T(8,128)(2,1)} %bitcast.108) | data formatting | bytes 39321600 | tf_op jit(solution)/shard_map/all_to_all | solution.py:110
  1904.5 10.2 all-to-all-start.3
  1914.8 14.9 fusion.56
  1929.7 658.4 %all-to-all-done.3 = bf16[80,4,640,48]{0,3,1,2:T(8,128)(2,1)} async-done(((bf16[80,4,640,48]{0,3,1,2:T(8,128)(2,1)}), bf16[80,4,640,48]{0,3,1,2:T(8,128)(2,1)}, u32[]{:S(2)}, u32[]{:S(2)}) %all-to-all-start.3) | async-done | bytes 19660832 | tf_op jit(solution)/shard_map/all_to_all | solution.py:109
  2588.1 53.8 %copy.100 = bf16[80,4,8,80,48]{0,2,4,3,1:T(8,128)(2,1)} copy(bf16[80,4,8,80,48]{0,4,1,3,2:T(8,128)(2,1)} %bitcast.31) | data formatting | bytes 39321600 | tf_op jit(solution)/shard_map/all_to_all | solution.py:109
  2641.9 44.9 %reshape.326 = bf16[640,4,80,2,24]{0,4,3,2,1:T(8,128)(2,1)} reshape(bf16[8,80,4,80,48]{1,0,4,3,2:T(8,128)(2,1)} %bitcast.106) | data formatting | bytes 39321600 | tf_op jit(solution)/shard_map/reshape | solution.py:116
  2686.8 33.4 %fusion.24 = bf16[4,24,80,1280]{3,2,1,0:T(8,128)(2,1)} fusion(bf16[640,4,80,2,24]{0,4,3,2,1:T(8,128)(2,1)} %reshape.326, f32[640,1,1280]{2,0,1:T(8,128)} %get-tuple-element.8, f32[640,1,1280]{2,0,1:T(8,128)S(1)} %get-tuple-element.7, f32[640]{0:T(1024)S(1)} %compare_select_fusion), kind=kOutput, calls=%fused_computation.31 | convolution fusion | flops 25180569600 | bytes 45877760 | tf_op jit(solution)/shard_map/mtlrf,mrj->tflj/dot_general | solution.py:118
  (9 shorter events, 0.1 us)
Async XLA Ops:
  609.6 7.2 copy-start.4
  609.6 7.5 copy-start.5
  609.6 7.7 copy-start.6
  609.6 681.4 %all-to-all-start.1 = ((bf16[160,16,80,48]{2,3,1,0:T(8,128)(2,1)}), bf16[160,16,80,48]{2,3,1,0:T(8,128)(2,1)}, u32[]{:S(2)}, u32[]{:S(2)}) async-start(bf16[160,16,80,48]{2,3,1,0:T(8,128)(2,1)} %bitcast.102), calls=%async_computation.1 | async-start | bytes 62914560 | tf_op jit(solution)/shard_map/all_to_all | solution.py:96
  1424.1 7.1 copy-start
  1439.1 30.7 %copy-start.3 = (f32[320]{0:T(512)S(1)}, f32[320]{0:T(512)}, u32[]{:S(2)}) copy-start(f32[320]{0:T(512)} %param.10) | copy-start | bytes 3844
  1469.8 19.2 copy-start.1
  1607.2 13.4 copy-start.2
  1904.5 683.6 %all-to-all-start.3 = ((bf16[80,4,640,48]{0,3,1,2:T(8,128)(2,1)}), bf16[80,4,640,48]{0,3,1,2:T(8,128)(2,1)}, u32[]{:S(2)}, u32[]{:S(2)}) async-start(bf16[80,4,640,48]{0,3,1,2:T(8,128)(2,1)} %copy.81), calls=%async_computation.3 | async-start | bytes 62914560 | tf_op jit(solution)/shard_map/all_to_all | solution.py:109
where the time goes:
time: 2740 us; the launch traced here: 2720 us
  waiting for transfers between devices  1330 us (49%)
  blocking collectives  575 us (21%)
  local copies, waits for them, and re-layouts  572 us (21%)
  other arithmetic  120 us (4%)
  matrix products  105 us (4%)
    all_to_all x1, waiting for transfers between devices, on_device(): lax.all_to_all(lax.all_to_all(wave_rows, 'traj', split_axis=0, concat_axi...  673 us
    all_to_all x1, waiting for transfers between devices, on_device(): lax.all_to_all(lax.all_to_all(filtered, 'traj', split_axis=1, concat_axis...  658 us
    all_to_all x1, blocking collectives, on_device(): lax.all_to_all(wave_rows, 'traj', split_axis=0, concat_axis=1, tiled=True)  357 us
    all_to_all x1, blocking collectives, on_device(): lax.all_to_all(filtered, 'traj', split_axis=1, concat_axis=0, tiled=True)  218 us
    all_to_all x2, local copies, waits for them, and re-layouts, on_device(): lax.all_to_all(wave_rows, 'traj', split_axis=0, concat_axis=1, tiled=True)  156 us
    all_to_all x2, local copies, waits for them, and re-layouts, on_device(): lax.all_to_all(lax.all_to_all(wave_rows, 'traj', split_axis=0, concat_axi...  108 us
    unnamed x17, local copies, waits for them, and re-layouts  81.8 us
  transfers between devices with their start and end apart: 2, of which 2 were waited for; matrix products, arithmetic and copies ran while one was open for 1% of the time, Pallas kernels for 0%

commit v1 on v0

v1 whole, which is shorter than its diff:
```python
import math

import jax
import jax.numpy as jnp
import numpy as np
from jax import lax
from jax.sharding import PartitionSpec as P

FIELD_PARTS = 3
MOST_COPIES = 4


def parent_slots(counts, slot_perm):
    member_count = counts.shape[0]
    position = jnp.arange(member_count, dtype=jnp.int32)
    copy_end = jnp.cumsum(counts)
    copy_parent = jnp.sum((copy_end[None, :] <= position[:, None]).astype(jnp.int32), axis=1)
    landing = (slot_perm[:, None] == position[None, :]).astype(jnp.int32)
    return jnp.sum(landing * copy_parent[:, None], axis=0)


def survivor_lists(counts, slot_perm):
    member_count = counts.shape[0]
    position = jnp.arange(member_count, dtype=jnp.int32)
    alive = counts > 0
    rank = jnp.sum((position[None, :] < position[:, None]) & alive[None, :], axis=1).astype(jnp.int32)
    hit = alive[None, :] & (rank[None, :] == position[:, None])
    survivors = jnp.sum(hit * position[None, :], axis=1).astype(jnp.int32)
    parents = parent_slots(counts, slot_perm)
    slot_source = jnp.sum((parents[:, None] == position[None, :]) * rank[None, :], axis=1)
    return survivors, slot_source.astype(jnp.int32)


def trig_tables(lon_count):
    wave_count = lon_count // 2
    turn = np.arange(wave_count)[:, None] * np.arange(lon_count)[None, :] % lon_count
    phase = (turn.astype(np.float32) * np.float32(2.0 * math.pi / lon_count)).astype(np.float64)
    pair = np.stack([np.cos(phase), -np.sin(phase)], axis=1).astype(np.float32)
    doubled = np.where(np.arange(wave_count) == 0, 1.0, 2.0).astype(np.float32)
    forward = (pair / np.float32(lon_count)).astype(jnp.bfloat16)
    inverse = (pair * doubled[:, None, None]).astype(jnp.bfloat16)
    return forward.reshape(2 * wave_count, lon_count), inverse.reshape(2 * wave_count, lon_count)


def exchange(pieces, axis):
    size = lax.axis_size(axis)
    out = [pieces[0]]
    for s in range(1, size):
        out.append(lax.ppermute(pieces[s], axis, [(i, i ^ s) for i in range(size)]))
    return out


def whole_globe(legendre, quad_weight, slab_index, slab_count):
    wave_here, _, degree_count, hemisphere = legendre.shape
    mirror = np.eye(hemisphere, dtype=np.float32)[::-1].astype(jnp.bfloat16)
    weighted = (legendre.astype(jnp.float32) * quad_weight).astype(jnp.bfloat16)
    sign = jnp.array([1.0, -1.0], jnp.bfloat16)[None, :, None, None]

    def both(table):
        south = jnp.einsum("mpkl,lh->mpkh", table, mirror, preferred_element_type=jnp.float32)
        south = south.astype(jnp.bfloat16) * sign
        full = jnp.concatenate([table, south], axis=-1)
        full = full.reshape(wave_here, 2 * degree_count, slab_count, 2 * hemisphere // slab_count)
        order = slab_index ^ jnp.arange(slab_count, dtype=jnp.int32)
        full = jnp.take(full, order, axis=2)
        return full.reshape(wave_here, 2 * degree_count, 2 * hemisphere)

    return both(weighted), both(legendre)


def run(survivor_count, state, survivors, slot_source, legendre, quad_weight, diffusion):
    group_count = lax.axis_size("traj")
    slab_count = lax.axis_size("grid")
    group_index = lax.axis_index("traj")
    slab_index = lax.axis_index("grid")
    member_here, field_count, lat_here, lon_count = state.shape
    wave_count = lon_count // 2
    wave_here = wave_count // (group_count * slab_count)
    row_here = 2 * wave_here
    lat_count = lat_here * slab_count
    hemisphere = lat_count // 2
    field_here = field_count // FIELD_PARTS
    point_here = field_here * lat_here

    forward, inverse = trig_tables(lon_count)
    forward = jnp.asarray(forward)
    inverse = jnp.asarray(inverse).reshape(group_count, slab_count, row_here, lon_count)
    group_order = group_index ^ jnp.arange(group_count, dtype=jnp.int32)
    slab_order = slab_index ^ jnp.arange(slab_count, dtype=jnp.int32)
    inverse = jnp.take(jnp.take(inverse, group_order, axis=0), slab_order, axis=1)
    inverse = inverse.reshape(group_count * slab_count * row_here, lon_count)
    analysis, synthesis = whole_globe(legendre, quad_weight, slab_index, slab_count)

    wave_ids = (group_index * slab_count + slab_index) * wave_here + jnp.arange(
        wave_here, dtype=jnp.int32
    )
    parity = jnp.arange(2, dtype=jnp.int32)
    degree = (
        2 * jnp.arange(hemisphere, dtype=jnp.int32)[None, None, :]
        + (wave_ids[:, None, None] + parity[None, :, None]) % 2
    )
    degree_ratio = (degree * (degree + 1)).astype(jnp.float32) / float(lat_count * (lat_count - 1))
    ratio_square = (degree_ratio * degree_ratio).reshape(wave_here, 2 * hemisphere)
    retained = (degree >= wave_ids[:, None, None]).reshape(wave_here, 2 * hemisphere)

    survivor_at = (survivors // member_here ^ group_index) * member_here + survivors % member_here
    survivor_at = survivor_at[:survivor_count]
    slot_rows = slot_source.reshape(group_count, member_here)

    parts = []
    for part in range(FIELD_PARTS):
        block = state[:, part * field_here : (part + 1) * field_here].reshape(
            member_here, point_here, lon_count
        )
        fourier = jnp.einsum("wj,tcj->twc", forward, block, preferred_element_type=jnp.float32)
        fourier = fourier.astype(jnp.bfloat16).reshape(
            member_here, group_count, slab_count * row_here, point_here
        )
        pieces = [
            lax.dynamic_index_in_dim(fourier, group_index ^ s, 1, keepdims=False)
            for s in range(group_count)
        ]
        members = jnp.concatenate(exchange(pieces, "traj"), axis=0)
        kept = jnp.take(members, survivor_at, axis=0).reshape(
            survivor_count, slab_count, row_here, point_here
        )
        pieces = [
            lax.dynamic_index_in_dim(kept, slab_index ^ s, 1, keepdims=False)
            for s in range(slab_count)
        ]
        rows = jnp.stack(exchange(pieces, "grid"), axis=0)
        rows = rows.reshape(slab_count, survivor_count, wave_here, 2, field_here, lat_here)
        rows = rows.transpose(2, 1, 3, 4, 0, 5).reshape(wave_here, -1, lat_count)
        spectrum = jnp.einsum(
            "mql,mcl->mqc", analysis, rows, preferred_element_type=jnp.float32
        )
        rate = diffusion[part * field_here : (part + 1) * field_here]
        rate_cols = jnp.broadcast_to(rate, (survivor_count, 2, field_here)).reshape(-1)
        damping = 1.0 / (1.0 + rate_cols[None, None, :] * ratio_square[..., None])
        filtered = jnp.where(retained[..., None], spectrum * damping, 0.0).astype(jnp.bfloat16)
        waves = jnp.einsum(
            "mql,mqc->mcl", synthesis, filtered, preferred_element_type=jnp.float32
        ).astype(jnp.bfloat16)
        waves = waves.reshape(wave_here, survivor_count, 2, field_here, slab_count, lat_here)
        waves = waves.transpose(4, 1, 0, 2, 3, 5).reshape(
            slab_count, survivor_count, row_here, point_here
        )
        back = jnp.stack(exchange([waves[s] for s in range(slab_count)], "grid"), axis=1)
        pieces = [
            jnp.take(
                back, lax.dynamic_index_in_dim(slot_rows, group_index ^ s, 0, keepdims=False), axis=0
            )
            for s in range(group_count)
        ]
        slots = jnp.stack(exchange(pieces, "traj"), axis=1).reshape(
            member_here, -1, point_here
        )
        smoothed = jnp.einsum(
            "twc,wj->tcj", slots, inverse, preferred_element_type=jnp.float32
        )
        parts.append(
            smoothed.astype(jnp.bfloat16).reshape(member_here, field_here, lat_here, lon_count)
        )
    return jnp.concatenate(parts, axis=1)


def on_device(state, counts, slot_perm, legendre, quad_weight, diffusion):
    survivors, slot_source = survivor_lists(counts, slot_perm)
    most = counts.shape[0] - MOST_COPIES + 1
    return run(most, state, survivors, slot_source, legendre, quad_weight, diffusion)


def solution(mesh):
    return jax.shard_map(
        on_device,
        mesh=mesh,
        in_specs=(
            P("traj", None, "grid", None),
            P(),
            P(),
            P(("traj", "grid"), None, None, None),
            P(),
            P(),
        ),
        out_specs=P("traj", None, "grid", None),
        check_vma=False,
    )
```

time: 2740 us -> 1620 us (0.59)
  waiting for transfers between devices: 1330 us -> 521 us
  blocking collectives: 575 us -> 0 us
  local copies, waits for them, and re-layouts: 572 us -> 734 us
  starting transfers between devices: 17.4 us -> 83.7 us
  matrix products: 105 us -> 145 us
    all_to_all x2 -> x0, waiting for transfers between devices: 1330 us -> none  [the longest x1 673 us: on_device(): lax.all_to_all(lax.all_to_all(wave_rows, 'traj', split_axis=0, concat_axi...]
    all_to_all x2 -> x0, blocking collectives: 575 us -> none  [the longest x1 357 us: on_device(): lax.all_to_all(wave_rows, 'traj', split_axis=0, concat_axis=1, tiled=True)]
    ppermute x0 -> x60, waiting for transfers between devices: none -> 521 us  [exchange(): out.append(lax.ppermute(pieces[s], axis, [(i, i ^ s) for i in range(size)]))]
    all_to_all x7 -> x0, local copies, waits for them, and re-layouts: 364 us -> none  [the longest x2 156 us: on_device(): lax.all_to_all(wave_rows, 'traj', split_axis=0, concat_axis=1, tiled=True)]
    gather x1 -> x25, local copies, waits for them, and re-layouts: 15.1 us -> 155 us  [the longest x8 78 us: both(): full = jnp.take(full, order, axis=2)]
    reshape x2 -> x12, local copies, waits for them, and re-layouts: 85 us -> 190 us  [the longest x2 80.5 us: both(): full.reshape(wave_here, 2 * degree_count, slab_count, 2 * hemisphere // s...]
    ppermute x0 -> x60, starting transfers between devices: none -> 83.7 us  [exchange(): out.append(lax.ppermute(pieces[s], axis, [(i, i ^ s) for i in range(size)]))]
    another operation x1 -> x34, local copies, waits for them, and re-layouts: 0.08 us -> 76.1 us  [the longest x27 65 us: run(): rows = jnp.stack(exchange(pieces, 'grid'), axis=0)]
  transfers between devices with their start and end apart: 2 -> 60, of which waited for: 2 -> 25; matrix products, arithmetic and copies ran while one was open for 1% -> 55% of each run, Pallas kernels for 0% -> 0%
where the time goes in v1:
time: 1620 us; the launch traced here: 1600 us
  local copies, waits for them, and re-layouts  734 us (45%)
  waiting for transfers between devices  521 us (32%)
  matrix products  145 us (9%)
  other arithmetic  115 us (7%)
  starting transfers between devices  83.7 us (5%)
    ppermute x60, waiting for transfers between devices, exchange(): out.append(lax.ppermute(pieces[s], axis, [(i, i ^ s) for i in range(size)]))  521 us
    unnamed x160, local copies, waits for them, and re-layouts  139 us
    ppermute x60, starting transfers between devices, exchange(): out.append(lax.ppermute(pieces[s], axis, [(i, i ^ s) for i in range(size)]))  83.7 us
    reshape x2, local copies, waits for them, and re-layouts, both(): full.reshape(wave_here, 2 * degree_count, slab_count, 2 * hemisphere // s...  80.5 us
    gather x8, local copies, waits for them, and re-layouts, both(): full = jnp.take(full, order, axis=2)  78 us
    reshape x6, local copies, waits for them, and re-layouts, run(): waves.reshape(wave_here, survivor_count, 2, field_here, slab_count, lat_h...  69.5 us
    another operation x27, local copies, waits for them, and re-layouts, run(): rows = jnp.stack(exchange(pieces, 'grid'), axis=0)  65 us
    dot_general x3, matrix products, run(): jnp.einsum('mql,mqc->mcl', synthesis, filtered, preferred_element_type=jn...  56.9 us
  transfers between devices with their start and end apart: 60, of which 25 were waited for; matrix products, arithmetic and copies ran while one was open for 55% of the time, Pallas kernels for 0%

profile of v1, /device:TPU:17, one launch (start us, length us, event | category | flops | bytes accessed | tf_op | source)
XLA Modules:
  0.0 1600.6 jit_solution(12601459689001138537)
XLA Ops:
  0.0 11.2 fusion.76
  11.6 12.2 convolution_convert_fusion.2
  32.1 8.9 convolution_convert_fusion.1
  45.6 10.1 multiply_convert_fusion
  55.7 9.0 convert_multiply_fusion
  64.7 10.9 pad_maximum_fusion.1
  75.6 40.3 %reshape.618 = bf16[20,640,8,80]{3,2,1,0:T(8,128)(2,1)} reshape(bf16[20,2,320,640]{3,2,1,0:T(8,128)(2,1)} %pad_maximum_fusion.1) | data formatting | bytes 32768000 | tf_op jit(solution)/shard_map/reshape | solution.py:63
  115.9 9.0 mini-gather-slice.9
  124.9 13.9 mini-gather-slice.8
  138.8 11.2 multiply_bitcast_fusion
  150.1 14.5 pad_maximum_fusion.2
  164.6 40.3 %reshape.619 = bf16[20,640,8,80]{3,2,1,0:T(8,128)(2,1)} reshape(bf16[20,2,320,640]{3,2,1,0:T(8,128)(2,1)} %pad_maximum_fusion.2) | data formatting | bytes 32768000 | tf_op jit(solution)/shard_map/reshape | solution.py:63
  204.8 9.0 mini-gather-slice.11
  213.8 13.9 mini-gather-slice.10
  227.7 13.6 copy.127
  241.3 19.1 %copy.126 = bf16[20,384,8,80]{1,3,0,2:T(8,128)(2,1)} copy(bf16[20,384,8,80]{3,2,1,0:T(8,128)(2,1)} %mini-gather-slice.8) | data formatting | bytes 19660800
  267.5 9.6 gather_fusion.2
  277.1 13.6 copy.129
  297.2 19.5 %copy.128 = bf16[20,384,8,80]{1,3,0,2:T(8,128)(2,1)} copy(bf16[20,384,8,80]{3,2,1,0:T(8,128)(2,1)} %mini-gather-slice.10) | data formatting | bytes 19660800
  316.7 9.5 gather_fusion.5
  327.2 25.0 %maximum_select_fusion = (bf16[20,640,8,80]{1,3,0,2:T(8,128)(2,1)}, bf16[20,640,8,80]{1,3,0,2:T(8,128)(2,1)}) fusion(bf16[20,256,8,80]{1,3,0,2:T(8,128)(2,1)} %bitcast.299, bf16[20,384,8,80]{1,3,0,2:T(8,128)(2,1)} %bitcast.297, pred[8]{0:T(512)(128)(4,1)S(1)} %compare_and_fusion.5, bf16[20,256,8,80]{1,3,0,2:T(8,128)(2,1)} %bitcast.300, ...), kind=kLoop, calls=%fused_computation.24 | loop fusion | flops 81920000 | bytes 65536008 | tf_op jit(solution)/shard_map/jit(_take)/select_n | solution.py:65
  352.2 13.5 convolution_convert_fusion
  366.2 14.7 copy.89
  424.6 11.0 collective-permute-done.42
  435.6 34.2 %collective-permute-done.41 = bf16[4,320,640]{2,1,0:T(8,128)(2,1)} collective-permute-done((bf16[4,320,640]{2,1,0:T(8,128)(2,1)}, bf16[4,320,640]{2,1,0:T(8,128)(2,1)}, u32[]{:S(2)}, u32[]{:S(2)}) %collective-permute-start.41) | collective-permute-done | bytes 1638432 | tf_op jit(solution)/shard_map/ppermute | solution.py:49
  482.3 9.3 broadcast_select_fusion.2
  521.0 15.7 collective-permute-done.4
  559.7 26.1 %collective-permute-start.25 = (bf16[13,40,640]{2,1,0:T(8,128)(2,1)}, bf16[13,40,640]{2,1,0:T(8,128)(2,1)}, u32[]{:S(2)}, u32[]{:S(2)}) collective-permute-start(bf16[13,40,640]{2,1,0:T(8,128)(2,1)} %get-tuple-element.71), channel_id=1, source_target_pairs={{0,3},{1,2},{2,1},{3,0},{4,7},{5,6},{6,5},{7,4},{8,11},{9,10},{10,... | collective-permute-start | bytes 1996808 | tf_op jit(solution)/shard_map/ppermute | solution.py:49
  588.7 10.7 collective-permute-done.8
  604.8 31.8 %collective-permute-done.9 = bf16[13,40,640]{2,1,0:T(8,128)(2,1)} collective-permute-done((bf16[13,40,640]{2,1,0:T(8,128)(2,1)}, bf16[13,40,640]{2,1,0:T(8,128)(2,1)}, u32[]{:S(2)}, u32[]{:S(2)}) %collective-permute-start.9) | collective-permute-done | bytes 665632 | tf_op jit(solution)/shard_map/ppermute | solution.py:49
  645.7 16.6 %copy.84 = bf16[20,13,2,8,8,80]{5,4,3,2,1,0:T(8,128)(2,1)} copy(bf16[20,13,2,8,8,80]{5,3,2,0,1,4:T(8,128)(2,1)} %bitcast.319) | data formatting | bytes 10649600 | tf_op jit(solution)/shard_map/transpose | solution.py:133
  662.4 13.6 reshape.364
  676.1 18.9 %fusion.47 = bf16[20,208,640]{2,1,0:T(8,128)(2,1)} fusion(bf16[20,640,640]{1,2,0:T(8,128)(2,1)} %bitcast.311, bf16[20,208,640]{2,1,0:T(8,128)(2,1)} %reshape.364, bf16[20,640,640]{1,2,0:T(8,128)(2,1)} %bitcast.314, f32[20,640]{1,0:T(8,128)S(1)} %fusion.53, f32[208]{0:T(256)S(1)} %mul.136, pred[20,640]{1,0:T(8,128)(4,1)S(1)} %add_compare_fusion), kind=kOutput, calls=%fused_computation.93 | convolution fusion | flops 6834380800 | bytes 43482432 | tf_op jit(solution)/shard_map/mql,mqc->mcl/dot_general | solution.py:141
  727.1 18.7 %collective-permute-done.29 = bf16[13,40,640]{2,1,0:T(8,128)(2,1)} collective-permute-done((bf16[13,40,640]{2,1,0:T(8,128)(2,1)}, bf16[13,40,640]{2,1,0:T(8,128)(2,1)}, u32[]{:S(2)}, u32[]{:S(2)}) %collective-permute-start.29) | collective-permute-done | bytes 665632 | tf_op jit(solution)/shard_map/ppermute | solution.py:49
  754.9 16.7 %copy.93 = bf16[20,13,2,8,8,80]{5,4,3,2,1,0:T(8,128)(2,1)} copy(bf16[20,13,2,8,8,80]{5,3,2,0,1,4:T(8,128)(2,1)} %bitcast.318) | data formatting | bytes 10649600 | tf_op jit(solution)/shard_map/transpose | solution.py:133
  771.6 13.4 reshape.376
  785.0 18.9 %fusion.46 = bf16[20,208,640]{2,1,0:T(8,128)(2,1)} fusion(bf16[20,640,640]{1,2,0:T(8,128)(2,1)} %bitcast.312, bf16[20,208,640]{2,1,0:T(8,128)(2,1)} %reshape.376, bf16[20,640,640]{1,2,0:T(8,128)(2,1)} %bitcast.315, f32[208]{0:T(256)S(1)} %mul.147, f32[20,640]{1,0:T(8,128)S(1)} %fusion.53, pred[20,640]{1,0:T(8,128)(4,1)S(1)} %add_compare_fusion), kind=kOutput, calls=%fused_computation.92 | convolution fusion | flops 6834380800 | bytes 43482432 | tf_op jit(solution)/shard_map/mql,mqc->mcl/dot_general | solution.py:141
  803.9 14.1 reshape.367
  818.1 8.9 copy.141
  848.0 14.5 reshape.377
  862.5 8.9 copy.140
  913.9 16.7 %copy.98 = bf16[20,13,2,8,8,80]{5,4,3,2,1,0:T(8,128)(2,1)} copy(bf16[20,13,2,8,8,80]{5,3,2,0,1,4:T(8,128)(2,1)} %bitcast.317) | data formatting | bytes 10649600 | tf_op jit(solution)/shard_map/transpose | solution.py:133
  930.5 13.2 reshape.382
  943.7 19.1 %fusion.45 = bf16[20,208,640]{2,1,0:T(8,128)(2,1)} fusion(bf16[20,640,640]{1,2,0:T(8,128)(2,1)} %bitcast.313, bf16[20,208,640]{2,1,0:T(8,128)(2,1)} %reshape.382, bf16[20,640,640]{1,2,0:T(8,128)(2,1)} %bitcast.316, f32[208]{0:T(256)S(1)} %copy-done.40, f32[20,640]{1,0:T(8,128)S(1)} %fusion.53, pred[20,640]{1,0:T(8,128)(4,1)S(1)} %add_compare_fusion), kind=kOutput, calls=%fused_computation.91 | convolution fusion | flops 6834380800 | bytes 43482432 | tf_op jit(solution)/shard_map/mql,mqc->mcl/dot_general | solution.py:141
  962.8 14.1 reshape.383
  976.9 9.0 copy.139
  1062.1 29.5 %collective-permute-done.15 = bf16[13,40,640]{2,1,0:T(8,128)(2,1)S(1)} collective-permute-done((bf16[13,40,640]{2,1,0:T(8,128)(2,1)}, bf16[13,40,640]{2,1,0:T(8,128)(2,1)S(1)}, u32[]{:S(2)}, u32[]{:S(2)}) %collective-permute-start.15) | collective-permute-done | bytes 665632 | tf_op jit(solution)/shard_map/ppermute | solution.py:49
  1092.4 30.2 %collective-permute-done.16 = bf16[13,40,640]{2,1,0:T(8,128)(2,1)S(1)} collective-permute-done((bf16[13,40,640]{2,1,0:T(8,128)(2,1)}, bf16[13,40,640]{2,1,0:T(8,128)(2,1)S(1)}, u32[]{:S(2)}, u32[]{:S(2)}) %collective-permute-start.16) | collective-permute-done | bytes 665632 | tf_op jit(solution)/shard_map/ppermute | solution.py:49
  1135.7 41.6 %collective-permute-done.33 = bf16[13,40,640]{2,1,0:T(8,128)(2,1)} collective-permute-done((bf16[13,40,640]{2,1,0:T(8,128)(2,1)}, bf16[13,40,640]{2,1,0:T(8,128)(2,1)}, u32[]{:S(2)}, u32[]{:S(2)}) %collective-permute-start.33) | collective-permute-done | bytes 665632 | tf_op jit(solution)/shard_map/ppermute | solution.py:49
  1182.5 9.1 collective-permute-done.34
  1197.8 10.2 collective-permute-done.35
  1208.9 28.6 %collective-permute-done.36 = bf16[13,40,640]{2,1,0:T(8,128)(2,1)S(1)} collective-permute-done((bf16[13,40,640]{2,1,0:T(8,128)(2,1)S(1)}, bf16[13,40,640]{2,1,0:T(8,128)(2,1)S(1)}, u32[]{:S(2)}, u32[]{:S(2)}) %collective-permute-start.36) | collective-permute-done | bytes 665632 | tf_op jit(solution)/shard_map/ppermute | solution.py:49
  1258.9 32.6 %collective-permute-done.53 = bf16[13,40,640]{2,1,0:T(8,128)(2,1)} collective-permute-done((bf16[13,40,640]{2,1,0:T(8,128)(2,1)}, bf16[13,40,640]{2,1,0:T(8,128)(2,1)}, u32[]{:S(2)}, u32[]{:S(2)}) %collective-permute-start.53) | collective-permute-done | bytes 665632 | tf_op jit(solution)/shard_map/ppermute | solution.py:49
  1293.5 12.3 collective-permute-done.54
  1307.8 14.8 collective-permute-done.55
  1323.4 13.9 collective-permute-done.56
  1405.7 34.5 %collective-permute-done.58 = bf16[4,8,40,640]{3,2,1,0:T(8,128)(2,1)} collective-permute-done((bf16[4,8,40,640]{3,2,1,0:T(8,128)(2,1)}, bf16[4,8,40,640]{3,2,1,0:T(8,128)(2,1)}, u32[]{:S(2)}, u32[]{:S(2)}) %collective-permute-start.58) | collective-permute-done | bytes 1638432 | tf_op jit(solution)/shard_map/ppermute | solution.py:49
  1442.3 11.0 bitcast_convert_fusion
  1453.4 21.9 %collective-permute-done.39 = bf16[4,8,40,640]{3,2,1,0:T(8,128)(2,1)S(1)} collective-permute-done((bf16[4,8,40,640]{3,2,1,0:T(8,128)(2,1)}, bf16[4,8,40,640]{3,2,1,0:T(8,128)(2,1)S(1)}, u32[]{:S(2)}, u32[]{:S(2)}) %collective-permute-start.39) | collective-permute-done | bytes 1638432 | tf_op jit(solution)/shard_map/ppermute | solution.py:49
  1475.6 34.7 %collective-permute-done.38 = bf16[4,8,40,640]{3,2,1,0:T(8,128)(2,1)S(1)} collective-permute-done((bf16[4,8,40,640]{3,2,1,0:T(8,128)(2,1)}, bf16[4,8,40,640]{3,2,1,0:T(8,128)(2,1)S(1)}, u32[]{:S(2)}, u32[]{:S(2)}) %collective-permute-start.38) | collective-permute-done | bytes 1638432 | tf_op jit(solution)/shard_map/ppermute | solution.py:49
  1512.0 11.3 bitcast_convert_fusion.1
  1523.3 22.3 %collective-permute-done.19 = bf16[4,8,40,640]{3,2,1,0:T(8,128)(2,1)} collective-permute-done((bf16[4,8,40,640]{3,2,1,0:T(8,128)(2,1)S(1)}, bf16[4,8,40,640]{3,2,1,0:T(8,128)(2,1)}, u32[]{:S(2)}, u32[]{:S(2)}) %collective-permute-start.19) | collective-permute-done | bytes 1638432 | tf_op jit(solution)/shard_map/ppermute | solution.py:49
  1545.6 35.1 %collective-permute-done.18 = bf16[4,8,40,640]{3,2,1,0:T(8,128)(2,1)} collective-permute-done((bf16[4,8,40,640]{3,2,1,0:T(8,128)(2,1)S(1)}, bf16[4,8,40,640]{3,2,1,0:T(8,128)(2,1)}, u32[]{:S(2)}, u32[]{:S(2)}) %collective-permute-start.18) | collective-permute-done | bytes 1638432 | tf_op jit(solution)/shard_map/ppermute | solution.py:49
  1580.7 11.4 bitcast_convert_fusion.2
  (387 shorter events, 468.0 us)
Async XLA Ops:
  29.9 335.8 %collective-permute-start.2 = (bf16[4,320,640]{2,1,0:T(8,128)(2,1)}, bf16[4,320,640]{2,1,0:T(8,128)(2,1)}, u32[]{:S(2)}, u32[]{:S(2)}) collective-permute-start(bf16[4,320,640]{2,1,0:T(8,128)(2,1)} %get-tuple-element.48), channel_id=1, source_target_pairs={{0,24},{8,16},{16,8},{24,0},{1,25},{9,17},{17,9},{25,1},{2,26},{10... | collective-permute-start | bytes 4915208 | tf_op jit(solution)/shard_map/ppermute | solution.py:49
  31.7 365.5 %collective-permute-start.1 = (bf16[4,320,640]{2,1,0:T(8,128)(2,1)}, bf16[4,320,640]{2,1,0:T(8,128)(2,1)}, u32[]{:S(2)}, u32[]{:S(2)}) collective-permute-start(bf16[4,320,640]{2,1,0:T(8,128)(2,1)} %get-tuple-element.49), channel_id=1, source_target_pairs={{0,16},{8,24},{16,0},{24,8},{1,17},{9,25},{17,1},{25,9},{2,18},{10... | collective-permute-start | bytes 4915208 | tf_op jit(solution)/shard_map/ppermute | solution.py:49
  31.9 366.5 %collective-permute-start = (bf16[4,320,640]{2,1,0:T(8,128)(2,1)}, bf16[4,320,640]{2,1,0:T(8,128)(2,1)}, u32[]{:S(2)}, u32[]{:S(2)}) collective-permute-start(bf16[4,320,640]{2,1,0:T(8,128)(2,1)} %get-tuple-element.50), channel_id=1, source_target_pairs={{0,8},{8,0},{16,24},{24,16},{1,9},{9,1},{17,25},{25,17},{2,10},{10... | collective-permute-start | bytes 4915208 | tf_op jit(solution)/shard_map/ppermute | solution.py:49
  43.9 354.7 %collective-permute-start.22 = (bf16[4,320,640]{2,1,0:T(8,128)(2,1)}, bf16[4,320,640]{2,1,0:T(8,128)(2,1)}, u32[]{:S(2)}, u32[]{:S(2)}) collective-permute-start(bf16[4,320,640]{2,1,0:T(8,128)(2,1)} %get-tuple-element.52), channel_id=1, source_target_pairs={{0,24},{8,16},{16,8},{24,0},{1,25},{9,17},{17,9},{25,1},{2,26},{10... | collective-permute-start | bytes 4915208 | tf_op jit(solution)/shard_map/ppermute | solution.py:49
  45.3 366.7 %collective-permute-start.21 = (bf16[4,320,640]{2,1,0:T(8,128)(2,1)}, bf16[4,320,640]{2,1,0:T(8,128)(2,1)}, u32[]{:S(2)}, u32[]{:S(2)}) collective-permute-start(bf16[4,320,640]{2,1,0:T(8,128)(2,1)} %get-tuple-element.53), channel_id=1, source_target_pairs={{0,16},{8,24},{16,0},{24,8},{1,17},{9,25},{17,1},{25,9},{2,18},{10... | collective-permute-start | bytes 4915208 | tf_op jit(solution)/shard_map/ppermute | solution.py:49
  138.8 188.4 %copy-start.41 = (pred[8]{0:T(512)(128)(4,1)}, pred[8]{0:T(512)(128)(4,1)S(1)}, u32[]{:S(2)}) copy-start(pred[8]{0:T(512)(128)(4,1)S(1)} %compare_and_fusion.5) | copy-start | bytes 28
  365.7 46.4 %collective-permute-start.20 = (bf16[4,320,640]{2,1,0:T(8,128)(2,1)}, bf16[4,320,640]{2,1,0:T(8,128)(2,1)}, u32[]{:S(2)}, u32[]{:S(2)}) collective-permute-start(bf16[4,320,640]{2,1,0:T(8,128)(2,1)} %get-tuple-element.54), channel_id=1, source_target_pairs={{0,8},{8,0},{16,24},{24,16},{1,9},{9,1},{17,25},{25,17},{2,10},{10... | collective-permute-start | bytes 4915208 | tf_op jit(solution)/shard_map/ppermute | solution.py:49
  397.2 38.4 %collective-permute-start.42 = (bf16[4,320,640]{2,1,0:T(8,128)(2,1)}, bf16[4,320,640]{2,1,0:T(8,128)(2,1)}, u32[]{:S(2)}, u32[]{:S(2)}) collective-permute-start(bf16[4,320,640]{2,1,0:T(8,128)(2,1)} %get-tuple-element.56), channel_id=1, source_target_pairs={{0,24},{8,16},{16,8},{24,0},{1,25},{9,17},{17,9},{25,1},{2,26},{10... | collective-permute-start | bytes 4915208 | tf_op jit(solution)/shard_map/ppermute | solution.py:49
  398.4 71.4 %collective-permute-start.41 = (bf16[4,320,640]{2,1,0:T(8,128)(2,1)}, bf16[4,320,640]{2,1,0:T(8,128)(2,1)}, u32[]{:S(2)}, u32[]{:S(2)}) collective-permute-start(bf16[4,320,640]{2,1,0:T(8,128)(2,1)} %get-tuple-element.57), channel_id=1, source_target_pairs={{0,16},{8,24},{16,0},{24,8},{1,17},{9,25},{17,1},{25,9},{2,18},{10... | collective-permute-start | bytes 4915208 | tf_op jit(solution)/shard_map/ppermute | solution.py:49
  398.6 71.2 %collective-permute-start.40 = (bf16[4,320,640]{2,1,0:T(8,128)(2,1)}, bf16[4,320,640]{2,1,0:T(8,128)(2,1)}, u32[]{:S(2)}, u32[]{:S(2)}) collective-permute-start(bf16[4,320,640]{2,1,0:T(8,128)(2,1)} %get-tuple-element.58), channel_id=1, source_target_pairs={{0,8},{8,0},{16,24},{24,16},{1,9},{9,1},{17,25},{25,17},{2,10},{10... | collective-permute-start | bytes 4915208 | tf_op jit(solution)/shard_map/ppermute | solution.py:49
  493.7 15.6 collective-permute-start.3
  496.1 40.6 %collective-permute-start.4 = (bf16[13,40,640]{2,1,0:T(8,128)(2,1)}, bf16[13,40,640]{2,1,0:T(8,128)(2,1)}, u32[]{:S(2)}, u32[]{:S(2)}) collective-permute-start(bf16[13,40,640]{2,1,0:T(8,128)(2,1)} %get-tuple-element.64), channel_id=1, source_target_pairs={{0,2},{1,3},{2,0},{3,1},{4,6},{5,7},{6,4},{7,5},{8,10},{9,11},{10,... | collective-permute-start | bytes 1996808 | tf_op jit(solution)/shard_map/ppermute | solution.py:49
  497.6 53.4 %collective-permute-start.5 = (bf16[13,40,640]{2,1,0:T(8,128)(2,1)}, bf16[13,40,640]{2,1,0:T(8,128)(2,1)}, u32[]{:S(2)}, u32[]{:S(2)}) collective-permute-start(bf16[13,40,640]{2,1,0:T(8,128)(2,1)} %get-tuple-element.63), channel_id=1, source_target_pairs={{0,3},{1,2},{2,1},{3,0},{4,7},{5,6},{6,5},{7,4},{8,11},{9,10},{10,... | collective-permute-start | bytes 1996808 | tf_op jit(solution)/shard_map/ppermute | solution.py:49
  497.8 55.5 %collective-permute-start.6 = (bf16[13,40,640]{2,1,0:T(8,128)(2,1)}, bf16[13,40,640]{2,1,0:T(8,128)(2,1)}, u32[]{:S(2)}, u32[]{:S(2)}) collective-permute-start(bf16[13,40,640]{2,1,0:T(8,128)(2,1)} %get-tuple-element.62), channel_id=1, source_target_pairs={{0,4},{1,5},{2,6},{3,7},{4,0},{5,1},{6,2},{7,3},{8,12},{9,13},{10,... | collective-permute-start | bytes 1996808 | tf_op jit(solution)/shard_map/ppermute | solution.py:49
  497.9 61.8 %collective-permute-start.7 = (bf16[13,40,640]{2,1,0:T(8,128)(2,1)}, bf16[13,40,640]{2,1,0:T(8,128)(2,1)}, u32[]{:S(2)}, u32[]{:S(2)}) collective-permute-start(bf16[13,40,640]{2,1,0:T(8,128)(2,1)} %get-tuple-element.61), channel_id=1, source_target_pairs={{0,5},{1,4},{2,7},{3,6},{4,1},{5,0},{6,3},{7,2},{8,13},{9,12},{10,... | collective-permute-start | bytes 1996808 | tf_op jit(solution)/shard_map/ppermute | solution.py:49
  509.3 90.1 %collective-permute-start.8 = (bf16[13,40,640]{2,1,0:T(8,128)(2,1)}, bf16[13,40,640]{2,1,0:T(8,128)(2,1)}, u32[]{:S(2)}, u32[]{:S(2)}) collective-permute-start(bf16[13,40,640]{2,1,0:T(8,128)(2,1)} %get-tuple-element.60), channel_id=1, source_target_pairs={{0,6},{1,7},{2,4},{3,5},{4,2},{5,3},{6,0},{7,1},{8,14},{9,15},{10,... | collective-permute-start | bytes 1996808 | tf_op jit(solution)/shard_map/ppermute | solution.py:49
  536.8 99.8 %collective-permute-start.9 = (bf16[13,40,640]{2,1,0:T(8,128)(2,1)}, bf16[13,40,640]{2,1,0:T(8,128)(2,1)}, u32[]{:S(2)}, u32[]{:S(2)}) collective-permute-start(bf16[13,40,640]{2,1,0:T(8,128)(2,1)} %get-tuple-element.59), channel_id=1, source_target_pairs={{0,7},{1,6},{2,5},{3,4},{4,3},{5,2},{6,1},{7,0},{8,15},{9,14},{10,... | collective-permute-start | bytes 1996808 | tf_op jit(solution)/shard_map/ppermute | solution.py:49
  551.0 124.9 %collective-permute-start.23 = (bf16[13,40,640]{2,1,0:T(8,128)(2,1)}, bf16[13,40,640]{2,1,0:T(8,128)(2,1)}, u32[]{:S(2)}, u32[]{:S(2)}) collective-permute-start(bf16[13,40,640]{2,1,0:T(8,128)(2,1)} %get-tuple-element.73), channel_id=1, source_target_pairs={{0,1},{1,0},{2,3},{3,2},{4,5},{5,4},{6,7},{7,6},{8,9},{9,8},{10,11... | collective-permute-start | bytes 1996808 | tf_op jit(solution)/shard_map/ppermute | solution.py:49
  553.3 122.8 %collective-permute-start.24 = (bf16[13,40,640]{2,1,0:T(8,128)(2,1)}, bf16[13,40,640]{2,1,0:T(8,128)(2,1)}, u32[]{:S(2)}, u32[]{:S(2)}) collective-permute-start(bf16[13,40,640]{2,1,0:T(8,128)(2,1)} %get-tuple-element.72), channel_id=1, source_target_pairs={{0,2},{1,3},{2,0},{3,1},{4,6},{5,7},{6,4},{7,5},{8,10},{9,11},{10,... | collective-permute-start | bytes 1996808 | tf_op jit(solution)/shard_map/ppermute | solution.py:49
  559.7 139.8 %collective-permute-start.25 = (bf16[13,40,640]{2,1,0:T(8,128)(2,1)}, bf16[13,40,640]{2,1,0:T(8,128)(2,1)}, u32[]{:S(2)}, u32[]{:S(2)}) collective-permute-start(bf16[13,40,640]{2,1,0:T(8,128)(2,1)} %get-tuple-element.71), channel_id=1, source_target_pairs={{0,3},{1,2},{2,1},{3,0},{4,7},{5,6},{6,5},{7,4},{8,11},{9,10},{10,... | collective-permute-start | bytes 1996808 | tf_op jit(solution)/shard_map/ppermute | solution.py:49
  599.4 104.9 %collective-permute-start.26 = (bf16[13,40,640]{2,1,0:T(8,128)(2,1)}, bf16[13,40,640]{2,1,0:T(8,128)(2,1)}, u32[]{:S(2)}, u32[]{:S(2)}) collective-permute-start(bf16[13,40,640]{2,1,0:T(8,128)(2,1)} %get-tuple-element.70), channel_id=1, source_target_pairs={{0,4},{1,5},{2,6},{3,7},{4,0},{5,1},{6,2},{7,3},{8,12},{9,13},{10,... | collective-permute-start | bytes 1996808 | tf_op jit(solution)/shard_map/ppermute | solution.py:49
  636.6 72.9 %collective-permute-start.27 = (bf16[13,40,640]{2,1,0:T(8,128)(2,1)}, bf16[13,40,640]{2,1,0:T(8,128)(2,1)}, u32[]{:S(2)}, u32[]{:S(2)}) collective-permute-start(bf16[13,40,640]{2,1,0:T(8,128)(2,1)} %get-tuple-element.69), channel_id=1, source_target_pairs={{0,5},{1,4},{2,7},{3,6},{4,1},{5,0},{6,3},{7,2},{8,13},{9,12},{10,... | collective-permute-start | bytes 1996808 | tf_op jit(solution)/shard_map/ppermute | solution.py:49
  675.9 45.8 %collective-permute-start.28 = (bf16[13,40,640]{2,1,0:T(8,128)(2,1)}, bf16[13,40,640]{2,1,0:T(8,128)(2,1)}, u32[]{:S(2)}, u32[]{:S(2)}) collective-permute-start(bf16[13,40,640]{2,1,0:T(8,128)(2,1)} %get-tuple-element.68), channel_id=1, source_target_pairs={{0,6},{1,7},{2,4},{3,5},{4,2},{5,3},{6,0},{7,1},{8,14},{9,15},{10,... | collective-permute-start | bytes 1996808 | tf_op jit(solution)/shard_map/ppermute | solution.py:49
  676.0 69.8 %collective-permute-start.29 = (bf16[13,40,640]{2,1,0:T(8,128)(2,1)}, bf16[13,40,640]{2,1,0:T(8,128)(2,1)}, u32[]{:S(2)}, u32[]{:S(2)}) collective-permute-start(bf16[13,40,640]{2,1,0:T(8,128)(2,1)} %get-tuple-element.67), channel_id=1, source_target_pairs={{0,7},{1,6},{2,5},{3,4},{4,3},{5,2},{6,1},{7,0},{8,15},{9,14},{10,... | collective-permute-start | bytes 1996808 | tf_op jit(solution)/shard_map/ppermute | solution.py:49
  699.5 85.4 %collective-permute-start.43 = (bf16[13,40,640]{2,1,0:T(8,128)(2,1)}, bf16[13,40,640]{2,1,0:T(8,128)(2,1)}, u32[]{:S(2)}, u32[]{:S(2)}) collective-permute-start(bf16[13,40,640]{2,1,0:T(8,128)(2,1)} %get-tuple-element.81), channel_id=1, source_target_pairs={{0,1},{1,0},{2,3},{3,2},{4,5},{5,4},{6,7},{7,6},{8,9},{9,8},{10,11... | collective-permute-start | bytes 1996808 | tf_op jit(solution)/shard_map/ppermute | solution.py:49
  704.3 170.1 %collective-permute-start.44 = (bf16[13,40,640]{2,1,0:T(8,128)(2,1)}, bf16[13,40,640]{2,1,0:T(8,128)(2,1)}, u32[]{:S(2)}, u32[]{:S(2)}) collective-permute-start(bf16[13,40,640]{2,1,0:T(8,128)(2,1)} %get-tuple-element.80), channel_id=1, source_target_pairs={{0,2},{1,3},{2,0},{3,1},{4,6},{5,7},{6,4},{7,5},{8,10},{9,11},{10,... | collective-permute-start | bytes 1996808 | tf_op jit(solution)/shard_map/ppermute | solution.py:49
  709.5 170.1 %collective-permute-start.45 = (bf16[13,40,640]{2,1,0:T(8,128)(2,1)}, bf16[13,40,640]{2,1,0:T(8,128)(2,1)}, u32[]{:S(2)}, u32[]{:S(2)}) collective-permute-start(bf16[13,40,640]{2,1,0:T(8,128)(2,1)} %get-tuple-element.79), channel_id=1, source_target_pairs={{0,3},{1,2},{2,1},{3,0},{4,7},{5,6},{6,5},{7,4},{8,11},{9,10},{10,... | collective-permute-start | bytes 1996808 | tf_op jit(solution)/shard_map/ppermute | solution.py:49
  721.8 160.9 %collective-permute-start.46 = (bf16[13,40,640]{2,1,0:T(8,128)(2,1)}, bf16[13,40,640]{2,1,0:T(8,128)(2,1)}, u32[]{:S(2)}, u32[]{:S(2)}) collective-permute-start(bf16[13,40,640]{2,1,0:T(8,128)(2,1)} %get-tuple-element.78), channel_id=1, source_target_pairs={{0,4},{1,5},{2,6},{3,7},{4,0},{5,1},{6,2},{7,3},{8,12},{9,13},{10,... | collective-permute-start | bytes 1996808 | tf_op jit(solution)/shard_map/ppermute | solution.py:49
  745.9 143.4 %collective-permute-start.47 = (bf16[13,40,640]{2,1,0:T(8,128)(2,1)}, bf16[13,40,640]{2,1,0:T(8,128)(2,1)}, u32[]{:S(2)}, u32[]{:S(2)}) collective-permute-start(bf16[13,40,640]{2,1,0:T(8,128)(2,1)} %get-tuple-element.77), channel_id=1, source_target_pairs={{0,5},{1,4},{2,7},{3,6},{4,1},{5,0},{6,3},{7,2},{8,13},{9,12},{10,... | collective-permute-start | bytes 1996808 | tf_op jit(solution)/shard_map/ppermute | solution.py:49
  785.0 109.7 %collective-permute-start.48 = (bf16[13,40,640]{2,1,0:T(8,128)(2,1)}, bf16[13,40,640]{2,1,0:T(8,128)(2,1)}, u32[]{:S(2)}, u32[]{:S(2)}) collective-permute-start(bf16[13,40,640]{2,1,0:T(8,128)(2,1)} %get-tuple-element.76), channel_id=1, source_target_pairs={{0,6},{1,7},{2,4},{3,5},{4,2},{5,3},{6,0},{7,1},{8,14},{9,15},{10,... | collective-permute-start | bytes 1996808 | tf_op jit(solution)/shard_map/ppermute | solution.py:49
  874.4 34.7 %collective-permute-start.49 = (bf16[13,40,640]{2,1,0:T(8,128)(2,1)}, bf16[13,40,640]{2,1,0:T(8,128)(2,1)}, u32[]{:S(2)}, u32[]{:S(2)}) collective-permute-start(bf16[13,40,640]{2,1,0:T(8,128)(2,1)} %get-tuple-element.75), channel_id=1, source_target_pairs={{0,7},{1,6},{2,5},{3,4},{4,3},{5,2},{6,1},{7,0},{8,15},{9,14},{10,... | collective-permute-start | bytes 1996808 | tf_op jit(solution)/shard_map/ppermute | solution.py:49
  879.6 167.5 %collective-permute-start.10 = (bf16[13,40,640]{2,1,0:T(8,128)(2,1)}, bf16[13,40,640]{2,1,0:T(8,128)(2,1)}, u32[]{:S(2)}, u32[]{:S(2)}) collective-permute-start(bf16[13,40,640]{2,1,0:T(8,128)(2,1)} %squeeze.199), channel_id=1, source_target_pairs={{0,1},{1,0},{2,3},{3,2},{4,5},{5,4},{6,7},{7,6},{8,9},{9,8},{10,11... | collective-permute-start | bytes 1996808 | tf_op jit(solution)/shard_map/ppermute | solution.py:49
  882.7 167.6 %collective-permute-start.11 = (bf16[13,40,640]{2,1,0:T(8,128)(2,1)}, bf16[13,40,640]{2,1,0:T(8,128)(2,1)}, u32[]{:S(2)}, u32[]{:S(2)}) collective-permute-start(bf16[13,40,640]{2,1,0:T(8,128)(2,1)} %squeeze.200), channel_id=1, source_target_pairs={{0,2},{1,3},{2,0},{3,1},{4,6},{5,7},{6,4},{7,5},{8,10},{9,11},{10,... | collective-permute-start | bytes 1996808 | tf_op jit(solution)/shard_map/ppermute | solution.py:49
  889.2 163.3 %collective-permute-start.12 = (bf16[13,40,640]{2,1,0:T(8,128)(2,1)}, bf16[13,40,640]{2,1,0:T(8,128)(2,1)}, u32[]{:S(2)}, u32[]{:S(2)}) collective-permute-start(bf16[13,40,640]{2,1,0:T(8,128)(2,1)} %squeeze.201), channel_id=1, source_target_pairs={{0,3},{1,2},{2,1},{3,0},{4,7},{5,6},{6,5},{7,4},{8,11},{9,10},{10,... | collective-permute-start | bytes 1996808 | tf_op jit(solution)/shard_map/ppermute | solution.py:49
  894.6 161.0 %collective-permute-start.13 = (bf16[13,40,640]{2,1,0:T(8,128)(2,1)}, bf16[13,40,640]{2,1,0:T(8,128)(2,1)}, u32[]{:S(2)}, u32[]{:S(2)}) collective-permute-start(bf16[13,40,640]{2,1,0:T(8,128)(2,1)} %squeeze.202), channel_id=1, source_target_pairs={{0,4},{1,5},{2,6},{3,7},{4,0},{5,1},{6,2},{7,3},{8,12},{9,13},{10,... | collective-permute-start | bytes 1996808 | tf_op jit(solution)/shard_map/ppermute | solution.py:49
  909.1 151.0 %collective-permute-start.14 = (bf16[13,40,640]{2,1,0:T(8,128)(2,1)}, bf16[13,40,640]{2,1,0:T(8,128)(2,1)}, u32[]{:S(2)}, u32[]{:S(2)}) collective-permute-start(bf16[13,40,640]{2,1,0:T(8,128)(2,1)} %squeeze.203), channel_id=1, source_target_pairs={{0,5},{1,4},{2,7},{3,6},{4,1},{5,0},{6,3},{7,2},{8,13},{9,12},{10,... | collective-permute-start | bytes 1996808 | tf_op jit(solution)/shard_map/ppermute | solution.py:49
  1047.1 44.5 %collective-permute-start.15 = (bf16[13,40,640]{2,1,0:T(8,128)(2,1)}, bf16[13,40,640]{2,1,0:T(8,128)(2,1)S(1)}, u32[]{:S(2)}, u32[]{:S(2)}) collective-permute-start(bf16[13,40,640]{2,1,0:T(8,128)(2,1)} %squeeze.204), channel_id=1, source_target_pairs={{0,6},{1,7},{2,4},{3,5},{4,2},{5,3},{6,0},{7,1},{8,14},{9,15},{10,... | collective-permute-start | bytes 1996808 | tf_op jit(solution)/shard_map/ppermute | solution.py:49
  1050.2 76.8 %copy-start.31 = (bf16[13,40,640]{2,1,0:T(8,128)(2,1)S(1)}, bf16[13,40,640]{2,1,0:T(8,128)(2,1)}, u32[]{:S(2)}) copy-start(bf16[13,40,640]{2,1,0:T(8,128)(2,1)} %squeeze.226) | copy-start | bytes 1996804
  1050.2 72.4 %collective-permute-start.16 = (bf16[13,40,640]{2,1,0:T(8,128)(2,1)}, bf16[13,40,640]{2,1,0:T(8,128)(2,1)S(1)}, u32[]{:S(2)}, u32[]{:S(2)}) collective-permute-start(bf16[13,40,640]{2,1,0:T(8,128)(2,1)} %squeeze.205), channel_id=1, source_target_pairs={{0,7},{1,6},{2,5},{3,4},{4,3},{5,2},{6,1},{7,0},{8,15},{9,14},{10,... | collective-permute-start | bytes 1996808 | tf_op jit(solution)/shard_map/ppermute | solution.py:49
  1052.5 76.6 %copy-start.30 = (bf16[13,40,640]{2,1,0:T(8,128)(2,1)S(1)}, bf16[13,40,640]{2,1,0:T(8,128)(2,1)}, u32[]{:S(2)}) copy-start(bf16[13,40,640]{2,1,0:T(8,128)(2,1)} %squeeze.227) | copy-start | bytes 1996804
  1052.5 74.5 %collective-permute-start.30 = (bf16[13,40,640]{2,1,0:T(8,128)(2,1)}, bf16[13,40,640]{2,1,0:T(8,128)(2,1)}, u32[]{:S(2)}, u32[]{:S(2)}) collective-permute-start(bf16[13,40,640]{2,1,0:T(8,128)(2,1)} %squeeze.221), channel_id=1, source_target_pairs={{0,1},{1,0},{2,3},{3,2},{4,5},{5,4},{6,7},{7,6},{8,9},{9,8},{10,11... | collective-permute-start | bytes 1996808 | tf_op jit(solution)/shard_map/ppermute | solution.py:49
  1055.7 73.4 %collective-permute-start.31 = (bf16[13,40,640]{2,1,0:T(8,128)(2,1)}, bf16[13,40,640]{2,1,0:T(8,128)(2,1)}, u32[]{:S(2)}, u32[]{:S(2)}) collective-permute-start(bf16[13,40,640]{2,1,0:T(8,128)(2,1)} %squeeze.222), channel_id=1, source_target_pairs={{0,2},{1,3},{2,0},{3,1},{4,6},{5,7},{6,4},{7,5},{8,10},{9,11},{10,... | collective-permute-start | bytes 1996808 | tf_op jit(solution)/shard_map/ppermute | solution.py:49
  1060.1 71.1 %collective-permute-start.32 = (bf16[13,40,640]{2,1,0:T(8,128)(2,1)}, bf16[13,40,640]{2,1,0:T(8,128)(2,1)}, u32[]{:S(2)}, u32[]{:S(2)}) collective-permute-start(bf16[13,40,640]{2,1,0:T(8,128)(2,1)} %squeeze.223), channel_id=1, source_target_pairs={{0,3},{1,2},{2,1},{3,0},{4,7},{5,6},{6,5},{7,4},{8,11},{9,10},{10,... | collective-permute-start | bytes 1996808 | tf_op jit(solution)/shard_map/ppermute | solution.py:49
  1091.5 85.8 %collective-permute-start.33 = (bf16[13,40,640]{2,1,0:T(8,128)(2,1)}, bf16[13,40,640]{2,1,0:T(8,128)(2,1)}, u32[]{:S(2)}, u32[]{:S(2)}) collective-permute-start(bf16[13,40,640]{2,1,0:T(8,128)(2,1)} %squeeze.224), channel_id=1, source_target_pairs={{0,4},{1,5},{2,6},{3,7},{4,0},{5,1},{6,2},{7,3},{8,12},{9,13},{10,... | collective-permute-start | bytes 1996808 | tf_op jit(solution)/shard_map/ppermute | solution.py:49
  1122.6 69.0 %collective-permute-start.34 = (bf16[13,40,640]{2,1,0:T(8,128)(2,1)}, bf16[13,40,640]{2,1,0:T(8,128)(2,1)}, u32[]{:S(2)}, u32[]{:S(2)}) collective-permute-start(bf16[13,40,640]{2,1,0:T(8,128)(2,1)} %squeeze.225), channel_id=1, source_target_pairs={{0,5},{1,4},{2,7},{3,6},{4,1},{5,0},{6,3},{7,2},{8,13},{9,12},{10,... | collective-permute-start | bytes 1996808 | tf_op jit(solution)/shard_map/ppermute | solution.py:49
  1127.0 80.9 %collective-permute-start.35 = (bf16[13,40,640]{2,1,0:T(8,128)(2,1)S(1)}, bf16[13,40,640]{2,1,0:T(8,128)(2,1)S(1)}, u32[]{:S(2)}, u32[]{:S(2)}) collective-permute-start(bf16[13,40,640]{2,1,0:T(8,128)(2,1)S(1)} %copy-done.31), channel_id=1, source_target_pairs={{0,6},{1,7},{2,4},{3,5},{4,2},{5,3},{6,0},{7,1},{8,14},{9,15},{10,... | collective-permute-start | bytes 1996808 | tf_op jit(solution)/shard_map/ppermute | solution.py:49
  1129.1 108.4 %collective-permute-start.36 = (bf16[13,40,640]{2,1,0:T(8,128)(2,1)S(1)}, bf16[13,40,640]{2,1,0:T(8,128)(2,1)S(1)}, u32[]{:S(2)}, u32[]{:S(2)}) collective-permute-start(bf16[13,40,640]{2,1,0:T(8,128)(2,1)S(1)} %copy-done.30), channel_id=1, source_target_pairs={{0,7},{1,6},{2,5},{3,4},{4,3},{5,2},{6,1},{7,0},{8,15},{9,14},{10,... | collective-permute-start | bytes 1996808 | tf_op jit(solution)/shard_map/ppermute | solution.py:49
  1131.1 119.9 %collective-permute-start.50 = (bf16[13,40,640]{2,1,0:T(8,128)(2,1)}, bf16[13,40,640]{2,1,0:T(8,128)(2,1)}, u32[]{:S(2)}, u32[]{:S(2)}) collective-permute-start(bf16[13,40,640]{2,1,0:T(8,128)(2,1)} %squeeze.239), channel_id=1, source_target_pairs={{0,1},{1,0},{2,3},{3,2},{4,5},{5,4},{6,7},{7,6},{8,9},{9,8},{10,11... | collective-permute-start | bytes 1996808 | tf_op jit(solution)/shard_map/ppermute | solution.py:49
  1177.3 75.8 %collective-permute-start.51 = (bf16[13,40,640]{2,1,0:T(8,128)(2,1)}, bf16[13,40,640]{2,1,0:T(8,128)(2,1)}, u32[]{:S(2)}, u32[]{:S(2)}) collective-permute-start(bf16[13,40,640]{2,1,0:T(8,128)(2,1)} %squeeze.240), channel_id=1, source_target_pairs={{0,2},{1,3},{2,0},{3,1},{4,6},{5,7},{6,4},{7,5},{8,10},{9,11},{10,... | collective-permute-start | bytes 1996808 | tf_op jit(solution)/shard_map/ppermute | solution.py:49
  1191.7 65.3 %collective-permute-start.52 = (bf16[13,40,640]{2,1,0:T(8,128)(2,1)}, bf16[13,40,640]{2,1,0:T(8,128)(2,1)}, u32[]{:S(2)}, u32[]{:S(2)}) collective-permute-start(bf16[13,40,640]{2,1,0:T(8,128)(2,1)} %squeeze.241), channel_id=1, source_target_pairs={{0,3},{1,2},{2,1},{3,0},{4,7},{5,6},{6,5},{7,4},{8,11},{9,10},{10,... | collective-permute-start | bytes 1996808 | tf_op jit(solution)/shard_map/ppermute | solution.py:49
  1208.0 83.5 %collective-permute-start.53 = (bf16[13,40,640]{2,1,0:T(8,128)(2,1)}, bf16[13,40,640]{2,1,0:T(8,128)(2,1)}, u32[]{:S(2)}, u32[]{:S(2)}) collective-permute-start(bf16[13,40,640]{2,1,0:T(8,128)(2,1)} %squeeze.242), channel_id=1, source_target_pairs={{0,4},{1,5},{2,6},{3,7},{4,0},{5,1},{6,2},{7,3},{8,12},{9,13},{10,... | collective-permute-start | bytes 1996808 | tf_op jit(solution)/shard_map/ppermute | solution.py:49
  1237.5 68.3 %collective-permute-start.54 = (bf16[13,40,640]{2,1,0:T(8,128)(2,1)}, bf16[13,40,640]{2,1,0:T(8,128)(2,1)}, u32[]{:S(2)}, u32[]{:S(2)}) collective-permute-start(bf16[13,40,640]{2,1,0:T(8,128)(2,1)} %squeeze.243), channel_id=1, source_target_pairs={{0,5},{1,4},{2,7},{3,6},{4,1},{5,0},{6,3},{7,2},{8,13},{9,12},{10,... | collective-permute-start | bytes 1996808 | tf_op jit(solution)/shard_map/ppermute | solution.py:49
  1251.0 71.5 %collective-permute-start.55 = (bf16[13,40,640]{2,1,0:T(8,128)(2,1)}, bf16[13,40,640]{2,1,0:T(8,128)(2,1)S(1)}, u32[]{:S(2)}, u32[]{:S(2)}) collective-permute-start(bf16[13,40,640]{2,1,0:T(8,128)(2,1)} %squeeze.244), channel_id=1, source_target_pairs={{0,6},{1,7},{2,4},{3,5},{4,2},{5,3},{6,0},{7,1},{8,14},{9,15},{10,... | collective-permute-start | bytes 1996808 | tf_op jit(solution)/shard_map/ppermute | solution.py:49
  1253.1 84.2 %collective-permute-start.56 = (bf16[13,40,640]{2,1,0:T(8,128)(2,1)}, bf16[13,40,640]{2,1,0:T(8,128)(2,1)S(1)}, u32[]{:S(2)}, u32[]{:S(2)}) collective-permute-start(bf16[13,40,640]{2,1,0:T(8,128)(2,1)} %squeeze.245), channel_id=1, source_target_pairs={{0,7},{1,6},{2,5},{3,4},{4,3},{5,2},{6,1},{7,0},{8,15},{9,14},{10,... | collective-permute-start | bytes 1996808 | tf_op jit(solution)/shard_map/ppermute | solution.py:49
  1365.7 39.5 %collective-permute-start.59 = (bf16[4,8,40,640]{3,2,1,0:T(8,128)(2,1)}, bf16[4,8,40,640]{3,2,1,0:T(8,128)(2,1)}, u32[]{:S(2)}, u32[]{:S(2)}) collective-permute-start(bf16[4,8,40,640]{3,2,1,0:T(8,128)(2,1)} %get-tuple-element.100), channel_id=1, source_target_pairs={{0,24},{8,16},{16,8},{24,0},{1,25},{9,17},{17,9},{25,1},{2,26},{10... | collective-permute-start | bytes 4915208 | tf_op jit(solution)/shard_map/ppermute | solution.py:49
  1370.9 69.3 %collective-permute-start.58 = (bf16[4,8,40,640]{3,2,1,0:T(8,128)(2,1)}, bf16[4,8,40,640]{3,2,1,0:T(8,128)(2,1)}, u32[]{:S(2)}, u32[]{:S(2)}) collective-permute-start(bf16[4,8,40,640]{3,2,1,0:T(8,128)(2,1)} %get-tuple-element.97), channel_id=1, source_target_pairs={{0,16},{8,24},{16,0},{24,8},{1,17},{9,25},{17,1},{25,9},{2,18},{10... | collective-permute-start | bytes 4915208 | tf_op jit(solution)/shard_map/ppermute | solution.py:49
  1373.5 66.7 %collective-permute-start.57 = (bf16[4,8,40,640]{3,2,1,0:T(8,128)(2,1)}, bf16[4,8,40,640]{3,2,1,0:T(8,128)(2,1)}, u32[]{:S(2)}, u32[]{:S(2)}) collective-permute-start(bf16[4,8,40,640]{3,2,1,0:T(8,128)(2,1)} %get-tuple-element.94), channel_id=1, source_target_pairs={{0,8},{8,0},{16,24},{24,16},{1,9},{9,1},{17,25},{25,17},{2,10},{10... | collective-permute-start | bytes 4915208 | tf_op jit(solution)/shard_map/ppermute | solution.py:49
  1394.6 80.7 %collective-permute-start.39 = (bf16[4,8,40,640]{3,2,1,0:T(8,128)(2,1)}, bf16[4,8,40,640]{3,2,1,0:T(8,128)(2,1)S(1)}, u32[]{:S(2)}, u32[]{:S(2)}) collective-permute-start(bf16[4,8,40,640]{3,2,1,0:T(8,128)(2,1)} %get-tuple-element.99), channel_id=1, source_target_pairs={{0,24},{8,16},{16,8},{24,0},{1,25},{9,17},{17,9},{25,1},{2,26},{10... | collective-permute-start | bytes 4915208 | tf_op jit(solution)/shard_map/ppermute | solution.py:49
  1395.8 114.6 %collective-permute-start.38 = (bf16[4,8,40,640]{3,2,1,0:T(8,128)(2,1)}, bf16[4,8,40,640]{3,2,1,0:T(8,128)(2,1)S(1)}, u32[]{:S(2)}, u32[]{:S(2)}) collective-permute-start(bf16[4,8,40,640]{3,2,1,0:T(8,128)(2,1)} %get-tuple-element.96), channel_id=1, source_target_pairs={{0,16},{8,24},{16,0},{24,8},{1,17},{9,25},{17,1},{25,9},{2,18},{10... | collective-permute-start | bytes 4915208 | tf_op jit(solution)/shard_map/ppermute | solution.py:49
  1405.2 105.2 %collective-permute-start.37 = (bf16[4,8,40,640]{3,2,1,0:T(8,128)(2,1)S(1)}, bf16[4,8,40,640]{3,2,1,0:T(8,128)(2,1)S(1)}, u32[]{:S(2)}, u32[]{:S(2)}) collective-permute-start(bf16[4,8,40,640]{3,2,1,0:T(8,128)(2,1)S(1)} %copy-done.29), channel_id=1, source_target_pairs={{0,8},{8,0},{16,24},{24,16},{1,9},{9,1},{17,25},{25,17},{2,10},{10... | collective-permute-start | bytes 4915208 | tf_op jit(solution)/shard_map/ppermute | solution.py:49
  1440.2 105.4 %collective-permute-start.19 = (bf16[4,8,40,640]{3,2,1,0:T(8,128)(2,1)S(1)}, bf16[4,8,40,640]{3,2,1,0:T(8,128)(2,1)}, u32[]{:S(2)}, u32[]{:S(2)}) collective-permute-start(bf16[4,8,40,640]{3,2,1,0:T(8,128)(2,1)S(1)} %copy-done.26), channel_id=1, source_target_pairs={{0,24},{8,16},{16,8},{24,0},{1,25},{9,17},{17,9},{25,1},{2,26},{10... | collective-permute-start | bytes 4915208 | tf_op jit(solution)/shard_map/ppermute | solution.py:49
  1440.2 140.4 %collective-permute-start.18 = (bf16[4,8,40,640]{3,2,1,0:T(8,128)(2,1)S(1)}, bf16[4,8,40,640]{3,2,1,0:T(8,128)(2,1)}, u32[]{:S(2)}, u32[]{:S(2)}) collective-permute-start(bf16[4,8,40,640]{3,2,1,0:T(8,128)(2,1)S(1)} %copy-done.27), channel_id=1, source_target_pairs={{0,16},{8,24},{16,0},{24,8},{1,17},{9,25},{17,1},{25,9},{2,18},{10... | collective-permute-start | bytes 4915208 | tf_op jit(solution)/shard_map/ppermute | solution.py:49
  1475.3 105.4 %collective-permute-start.17 = (bf16[4,8,40,640]{3,2,1,0:T(8,128)(2,1)S(1)}, bf16[4,8,40,640]{3,2,1,0:T(8,128)(2,1)}, u32[]{:S(2)}, u32[]{:S(2)}) collective-permute-start(bf16[4,8,40,640]{3,2,1,0:T(8,128)(2,1)S(1)} %copy-done.28), channel_id=1, source_target_pairs={{0,8},{8,0},{16,24},{24,16},{1,9},{9,1},{17,25},{25,17},{2,10},{10... | collective-permute-start | bytes 4915208 | tf_op jit(solution)/shard_map/ppermute | solution.py:49
  1512.0 68.7 %copy-start.25 = (bf16[8,4,40,1280]{3,2,1,0:T(8,128)(2,1)S(1)}, bf16[8,4,40,1280]{3,2,1,0:T(8,128)(2,1)}, u32[]{:S(2)}) copy-start(bf16[8,4,40,1280]{3,2,1,0:T(8,128)(2,1)} %gather_fusion.1) | copy-start | bytes 9830404
  (53 other events, 748.2 us)

commit v2 on v1

v2 whole, which is shorter than its diff:
```python
import math

import jax
import jax.numpy as jnp
import numpy as np
from jax import lax
from jax.experimental import pallas as pl
from jax.experimental.pallas import tpu as pltpu
from jax.sharding import PartitionSpec as P

FIELD_PARTS = 3
MOST_COPIES = 4
VMEM_BYTES = 60 * 2**20
NT = (((1,), (1,)), ((), ()))
TN = (((0,), (0,)), ((), ()))


def parent_slots(counts, slot_perm):
    member_count = counts.shape[0]
    position = jnp.arange(member_count, dtype=jnp.int32)
    copy_end = jnp.cumsum(counts)
    copy_parent = jnp.sum((copy_end[None, :] <= position[:, None]).astype(jnp.int32), axis=1)
    landing = (slot_perm[:, None] == position[None, :]).astype(jnp.int32)
    return jnp.sum(landing * copy_parent[:, None], axis=0)


def survivor_lists(counts, slot_perm):
    member_count = counts.shape[0]
    position = jnp.arange(member_count, dtype=jnp.int32)
    alive = counts > 0
    rank = jnp.sum((position[None, :] < position[:, None]) & alive[None, :], axis=1).astype(jnp.int32)
    hit = alive[None, :] & (rank[None, :] == position[:, None])
    survivors = jnp.sum(hit * position[None, :], axis=1).astype(jnp.int32)
    parents = parent_slots(counts, slot_perm)
    slot_source = jnp.sum((parents[:, None] == position[None, :]) * rank[None, :], axis=1)
    return survivors, slot_source.astype(jnp.int32)


def trig_tables(lon_count):
    wave_count = lon_count // 2
    turn = np.arange(wave_count)[:, None] * np.arange(lon_count)[None, :] % lon_count
    phase = (turn.astype(np.float32) * np.float32(2.0 * math.pi / lon_count)).astype(np.float64)
    pair = np.stack([np.cos(phase), -np.sin(phase)], axis=1).astype(np.float32)
    doubled = np.where(np.arange(wave_count) == 0, 1.0, 2.0).astype(np.float32)
    forward = (pair / np.float32(lon_count)).astype(jnp.bfloat16)
    inverse = (pair * doubled[:, None, None]).astype(jnp.bfloat16)
    return forward.reshape(2 * wave_count, lon_count), inverse.reshape(2 * wave_count, lon_count)


def exchange(pieces, axis):
    size = lax.axis_size(axis)
    out = [pieces[0]]
    for s in range(1, size):
        out.append(lax.ppermute(pieces[s], axis, [(i, i ^ s) for i in range(size)]))
    return out


def params():
    return pltpu.CompilerParams(vmem_limit_bytes=VMEM_BYTES)


def cost(flops, bytes_accessed):
    return pl.CostEstimate(flops=flops, bytes_accessed=bytes_accessed, transcendentals=0)


def dot(a, b, dims=(((1,), (0,)), ((), ()))):
    return lax.dot_general(a, b, dims, preferred_element_type=jnp.float32)


def analyse(table, state, part):
    group_count, rows, lon_count = table.shape
    member_here, _, points, _ = state.shape

    def kernel(table_ref, state_ref, *out_refs):
        block = state_ref[0, 0]
        for s in range(group_count):
            out_refs[s][0] = dot(table_ref[s], block, NT).astype(jnp.bfloat16)

    return pl.pallas_call(
        kernel,
        name="analyse",
        grid=(member_here,),
        in_specs=[
            pl.BlockSpec((group_count, rows, lon_count), lambda t: (0, 0, 0)),
            pl.BlockSpec((1, 1, points, lon_count), lambda t: (t, part, 0, 0)),
        ],
        out_specs=[pl.BlockSpec((1, rows, points), lambda t: (t, 0, 0))] * group_count,
        out_shape=[jax.ShapeDtypeStruct((member_here, rows, points), jnp.bfloat16)] * group_count,
        compiler_params=params(),
        cost_estimate=cost(
            2 * member_here * group_count * rows * lon_count * points,
            2 * member_here * points * (lon_count + group_count * rows),
        ),
    )(table, state)


def keep(place, survivors, sources, survivor_count):
    group_count = len(sources)
    member_here, slab_count, rows, points = sources[0].shape

    def kernel(place_ref, survivor_ref, *refs):
        source_refs = refs[:group_count]
        out_refs = refs[group_count : group_count + slab_count]
        sems = refs[-1]
        group, slab = place_ref[0], place_ref[1]
        for d in range(survivor_count):
            parent = survivor_ref[d]
            offset = lax.bitwise_xor(parent // member_here, group)
            member = parent % member_here
            for k in range(group_count):

                @pl.when(offset == k)
                def _(k=k, d=d, member=member):
                    for s in range(slab_count):
                        pltpu.make_async_copy(
                            source_refs[k].at[member, lax.bitwise_xor(slab, s)],
                            out_refs[s].at[d],
                            sems.at[s],
                        ).start()

        for s in range(slab_count):
            pltpu.make_async_copy(out_refs[s], out_refs[s], sems.at[s]).wait()

    return pl.pallas_call(
        kernel,
        name="keep",
        in_specs=[pl.BlockSpec(memory_space=pltpu.SMEM)] * 2
        + [pl.BlockSpec(memory_space=pl.ANY)] * group_count,
        out_specs=[pl.BlockSpec(memory_space=pl.ANY)] * slab_count,
        out_shape=[jax.ShapeDtypeStruct((survivor_count, rows, points), jnp.bfloat16)] * slab_count,
        scratch_shapes=[pltpu.SemaphoreType.DMA((slab_count,))],
        compiler_params=params(),
        cost_estimate=cost(0, 4 * survivor_count * slab_count * rows * points),
    )(place, survivors, *sources)


def spread(place, slot_source, sources, member_here, group_count):
    slab_count = len(sources)
    _, rows, points = sources[0].shape

    def kernel(place_ref, slot_ref, *refs):
        source_refs = refs[:slab_count]
        out_refs = refs[slab_count : slab_count + group_count]
        sems = refs[-1]
        group, slab = place_ref[0], place_ref[1]
        for k in range(group_count):
            for t in range(member_here):
                origin = slot_ref[lax.bitwise_xor(group, k) * member_here + t]
                for s in range(slab_count):
                    pltpu.make_async_copy(
                        source_refs[s].at[origin],
                        out_refs[k].at[t, lax.bitwise_xor(slab, s)],
                        sems.at[k],
                    ).start()
        for k in range(group_count):
            pltpu.make_async_copy(out_refs[k], out_refs[k], sems.at[k]).wait()

    return pl.pallas_call(
        kernel,
        name="spread",
        in_specs=[pl.BlockSpec(memory_space=pltpu.SMEM)] * 2
        + [pl.BlockSpec(memory_space=pl.ANY)] * slab_count,
        out_specs=[pl.BlockSpec(memory_space=pl.ANY)] * group_count,
        out_shape=[
            jax.ShapeDtypeStruct((member_here, slab_count, rows, points), jnp.bfloat16)
        ]
        * group_count,
        scratch_shapes=[pltpu.SemaphoreType.DMA((group_count,))],
        compiler_params=params(),
        cost_estimate=cost(0, 4 * group_count * member_here * slab_count * rows * points),
    )(place, slot_source, *sources)


def synthesise(place, table, sources, part, part_count, earlier):
    group_count, rows, lon_count = table.shape
    member_here, _, points = sources[0].shape

    def kernel(place_ref, table_ref, *refs):
        group = place_ref[0]
        total = dot(refs[0][0], table_ref[group], TN)
        for s in range(1, group_count):
            total += dot(refs[s][0], table_ref[lax.bitwise_xor(group, s)], TN)
        refs[-1][0, 0] = total.astype(jnp.bfloat16)

    given = [place, table, *sources]
    specs = [
        pl.BlockSpec(memory_space=pltpu.SMEM),
        pl.BlockSpec((group_count, rows, lon_count), lambda t: (0, 0, 0)),
    ] + [pl.BlockSpec((1, rows, points), lambda t: (t, 0, 0))] * group_count
    aliases = {}
    if earlier is not None:
        aliases = {len(given): 0}
        given.append(earlier)
        specs.append(pl.BlockSpec(memory_space=pl.ANY))
    return pl.pallas_call(
        kernel,
        name="synthesise",
        grid=(member_here,),
        in_specs=specs,
        out_specs=pl.BlockSpec((1, 1, points, lon_count), lambda t: (t, part, 0, 0)),
        out_shape=jax.ShapeDtypeStruct((member_here, part_count, points, lon_count), jnp.bfloat16),
        input_output_aliases=aliases,
        compiler_params=params(),
        cost_estimate=cost(
            2 * member_here * group_count * rows * lon_count * points,
            2 * member_here * points * (lon_count + group_count * rows),
        ),
    )(*given)


def spectral_filter(place, legendre, quad_weight, rates, sources, survivor_count, field_here):
    slab_count = len(sources)
    points = sources[0].shape[1]
    lat_here = points // field_here
    wave_here, _, degree_count, hemisphere = legendre.shape
    lat_count = 2 * hemisphere
    half_slabs = slab_count // 2
    row_here = 2 * wave_here
    used = 2 * survivor_count
    padded = -(-used // 16) * 16

    shuffle = np.zeros((wave_here, padded, survivor_count, wave_here, 2), np.float32)
    for m in range(wave_here):
        for d in range(survivor_count):
            for r in range(2):
                shuffle[m, 2 * d + r, d, m, r] = 1.0
    shuffle = shuffle.reshape(wave_here * padded, survivor_count * row_here)
    gather = jnp.asarray(shuffle.astype(jnp.bfloat16))
    scatter = jnp.asarray(shuffle.T.astype(jnp.bfloat16))
    mirror = jnp.asarray(np.eye(hemisphere, dtype=np.float32)[::-1].astype(jnp.bfloat16))

    def kernel(place_ref, gather_ref, scatter_ref, mirror_ref, weight_ref, rate_ref, table_ref, *refs):
        source_refs = refs[:slab_count]
        out_refs = refs[slab_count : 2 * slab_count]
        held, north_rows, south_rows = refs[2 * slab_count :]
        m = pl.program_id(0)
        group, slab = place_ref[0], place_ref[1]

        @pl.when(m == 0)
        def _():
            for s in range(slab_count):
                held[s] = dot(gather_ref[...], source_refs[s][...]).astype(jnp.bfloat16)

        here = pl.ds(pl.multiple_of(m * padded, 16), padded)
        for side, rows_ref in ((0, north_rows), (half_slabs, south_rows)):
            for g in range(half_slabs):
                row = held[lax.bitwise_xor(slab, side + g), here, :]
                for f in range(field_here):
                    rows_ref[f * padded : (f + 1) * padded, g * lat_here : (g + 1) * lat_here] = row[
                        :, f * lat_here : (f + 1) * lat_here
                    ]
        north = north_rows[...].astype(jnp.float32)
        south = dot(south_rows[...], mirror_ref[...])
        weight = weight_ref[...]
        wave = (group * slab_count + slab) * wave_here + m
        degree_index = lax.broadcasted_iota(jnp.int32, (1, degree_count), 1)
        returned = []
        for p in range(2):
            both = (north + south) if p == 0 else (north - south)
            paired = (both * weight).astype(jnp.bfloat16)
            spectrum = dot(paired, table_ref[0, p], NT)
            degree = 2 * degree_index + (wave + p) % 2
            ratio = (degree * (degree + 1)).astype(jnp.float32) / float(lat_count * (lat_count - 1))
            damping = 1.0 / (1.0 + rate_ref[...] * (ratio * ratio))
            damping = jnp.where(degree >= wave, damping, 0.0)
            filtered = jnp.concatenate(
                [
                    (spectrum[f * padded : (f + 1) * padded] * damping[f : f + 1]).astype(jnp.bfloat16)
                    for f in range(field_here)
                ],
                axis=0,
            )
            returned.append(dot(filtered, table_ref[0, p]))
        north_rows[...] = (returned[0] + returned[1]).astype(jnp.bfloat16)
        south_rows[...] = dot(
            (returned[0] - returned[1]).astype(jnp.bfloat16), mirror_ref[...]
        ).astype(jnp.bfloat16)
        for side, rows_ref in ((0, north_rows), (half_slabs, south_rows)):
            for g in range(half_slabs):
                at = lax.bitwise_xor(slab, side + g)
                for f in range(field_here):
                    held[at, here, f * lat_here : (f + 1) * lat_here] = rows_ref[
                        f * padded : (f + 1) * padded, g * lat_here : (g + 1) * lat_here
                    ]

        @pl.when(m == wave_here - 1)
        def _():
            for s in range(slab_count):
                out_refs[s][...] = dot(scatter_ref[...], held[s]).astype(jnp.bfloat16)

    def fixed(*dims):
        return pl.BlockSpec(dims, lambda m: (0,) * len(dims), pipeline_mode=pl.Buffered(1))

    rows = survivor_count * row_here
    return pl.pallas_call(
        kernel,
        name="spectral",
        grid=(wave_here,),
        in_specs=[
            pl.BlockSpec(memory_space=pltpu.SMEM),
            fixed(*gather.shape),
            fixed(*scatter.shape),
            fixed(hemisphere, hemisphere),
            fixed(1, hemisphere),
            fixed(field_here, 1),
            pl.BlockSpec((1, 2, degree_count, hemisphere), lambda m: (m, 0, 0, 0)),
        ]
        + [fixed(rows, points)] * slab_count,
        out_specs=[fixed(rows, points)] * slab_count,
        out_shape=[jax.ShapeDtypeStruct((rows, points), jnp.bfloat16)] * slab_count,
        scratch_shapes=[
            pltpu.VMEM((slab_count, wave_here * padded, points), jnp.bfloat16),
            pltpu.VMEM((field_here * padded, hemisphere), jnp.bfloat16),
            pltpu.VMEM((field_here * padded, hemisphere), jnp.bfloat16),
        ],
        compiler_params=params(),
        cost_estimate=cost(
            20 * 10**9, 2 * wave_here * 2 * degree_count * hemisphere + 4 * slab_count * rows * points
        ),
    )(place, gather, scatter, mirror, quad_weight[None, :], rates[:, None], legendre, *sources)


def run(survivor_count, state, survivors, slot_source, legendre, quad_weight, diffusion):
    group_count = lax.axis_size("traj")
    slab_count = lax.axis_size("grid")
    group_index = lax.axis_index("traj")
    slab_index = lax.axis_index("grid")
    member_here, field_count, lat_here, lon_count = state.shape
    wave_count = lon_count // 2
    row_here = 2 * wave_count // (group_count * slab_count)
    field_here = field_count // FIELD_PARTS
    points = field_here * lat_here
    place = jnp.stack([group_index, slab_index]).astype(jnp.int32)

    forward, inverse = trig_tables(lon_count)
    forward = jnp.asarray(forward).reshape(group_count, slab_count * row_here, lon_count)
    inverse = jnp.asarray(inverse).reshape(group_count, slab_count * row_here, lon_count)
    forward = jnp.stack(
        [
            lax.dynamic_index_in_dim(forward, group_index ^ s, 0, keepdims=False)
            for s in range(group_count)
        ]
    )
    state = state.reshape(member_here, FIELD_PARTS, points, lon_count)

    smoothed = None
    for part in range(FIELD_PARTS):
        waves = exchange(analyse(forward, state, part), "traj")
        waves = [w.reshape(member_here, slab_count, row_here, points) for w in waves]
        kept = exchange(keep(place, survivors, waves, survivor_count), "grid")
        kept = [w.reshape(survivor_count * row_here, points) for w in kept]
        rates = diffusion[part * field_here : (part + 1) * field_here]
        back = spectral_filter(
            place, legendre, quad_weight, rates, kept, survivor_count, field_here
        )
        back = exchange([w.reshape(survivor_count, row_here, points) for w in back], "grid")
        slots = exchange(spread(place, slot_source, back, member_here, group_count), "traj")
        slots = [w.reshape(member_here, slab_count * row_here, points) for w in slots]
        smoothed = synthesise(place, inverse, slots, part, FIELD_PARTS, smoothed)
    return smoothed.reshape(member_here, field_count, lat_here, lon_count)


def on_device(state, counts, slot_perm, legendre, quad_weight, diffusion):
    survivors, slot_source = survivor_lists(counts, slot_perm)
    most = counts.shape[0] - MOST_COPIES + 1
    return run(most, state, survivors, slot_source, legendre, quad_weight, diffusion)


def solution(mesh):
    return jax.shard_map(
        on_device,
        mesh=mesh,
        in_specs=(
            P("traj", None, "grid", None),
            P(),
            P(),
            P(("traj", "grid"), None, None, None),
            P(),
            P(),
        ),
        out_specs=P("traj", None, "grid", None),
        check_vma=False,
    )
```

time: 1620 us -> 1780 us (1.099)
  Pallas kernels: 0 us -> 1340 us
  local copies, waits for them, and re-layouts: 734 us -> 12.5 us
  waiting for transfers between devices: 521 us -> 332 us
  matrix products: 145 us -> 0 us
  other arithmetic: 115 us -> 3.64 us
    pallas_call x0 -> x15, Pallas kernels: none -> 1340 us  [the longest x3 601 us: spread(): pl.pallas_call(kernel, name='spread', in_specs=[pl.BlockSpec(memory_space...]
    reshape x12 -> x0, local copies, waits for them, and re-layouts: 190 us -> none  [the longest x2 80.5 us: both(): full.reshape(wave_here, 2 * degree_count, slab_count, 2 * hemisphere // s...]
    ppermute x60, waiting for transfers between devices: 521 us -> 332 us  [exchange(): out.append(lax.ppermute(pieces[s], axis, [(i, i ^ s) for i in range(size)]))]
    gather x25 -> x0, local copies, waits for them, and re-layouts: 155 us -> none  [the longest x8 78 us: both(): full = jnp.take(full, order, axis=2)]
    dot_general x11 -> x0, matrix products: 145 us -> none  [the longest x3 56.9 us: run(): jnp.einsum('mql,mqc->mcl', synthesis, filtered, preferred_element_type=jn...]
    unnamed x160 -> x70, local copies, waits for them, and re-layouts: 139 us -> 7.66 us
    another operation x34 -> x1, local copies, waits for them, and re-layouts: 76.1 us -> 0.08 us  [the longest x27 65 us: run(): rows = jnp.stack(exchange(pieces, 'grid'), axis=0)]
    squeeze x27 -> x0, local copies, waits for them, and re-layouts: 73 us -> none  [the longest x21 49.3 us: run(): waves[s]]
  transfers between devices with their start and end apart: 60 -> 60, of which waited for: 25 -> 14; matrix products, arithmetic and copies ran while one was open for 55% -> 0% of each run, Pallas kernels for 0% -> 74%
where the time goes in v2:
time: 1780 us; the launch traced here: 1770 us
  Pallas kernels  1340 us (75%)
  waiting for transfers between devices  332 us (19%)
  starting transfers between devices  79.8 us (4%)
    pallas_call x3, Pallas kernels, spread(): pl.pallas_call(kernel, name='spread', in_specs=[pl.BlockSpec(memory_space...  601 us
    pallas_call x3, Pallas kernels, keep(): pl.pallas_call(kernel, name='keep', in_specs=[pl.BlockSpec(memory_space=p...  490 us
    ppermute x60, waiting for transfers between devices, exchange(): out.append(lax.ppermute(pieces[s], axis, [(i, i ^ s) for i in range(size)]))  332 us
    pallas_call x3, Pallas kernels, spectral_filter(): pl.pallas_call(kernel, name='spectral', grid=(wave_here,), in_specs=[pl.B...  155 us
    ppermute x60, starting transfers between devices, exchange(): out.append(lax.ppermute(pieces[s], axis, [(i, i ^ s) for i in range(size)]))  79.8 us
    pallas_call x3, Pallas kernels, synthesise(): pl.pallas_call(kernel, name='synthesise', grid=(member_here,), in_specs=s...  55.1 us
    pallas_call x3, Pallas kernels, analyse(): pl.pallas_call(kernel, name='analyse', grid=(member_here,), in_specs=[pl....  42.7 us
  transfers between devices with their start and end apart: 60, of which 14 were waited for; matrix products, arithmetic and copies ran while one was open for 0% of the time, Pallas kernels for 74%

profile of v2, /device:TPU:17, one launch (start us, length us, event | category | flops | bytes accessed | tf_op | source)
XLA Modules:
  0.0 1772.1 jit_solution(15574719011986910362)
XLA Ops:
  0.0 2.1 constant_dynamic-slice_fusion.3
  2.1 1.9 pad_maximum_fusion.table_ref
  4.0 14.4 analyse.5
  19.1 1.2 collective-permute-start.41
  20.7 14.2 analyse.4
  35.1 1.2 collective-permute-start.21
  36.3 14.2 analyse.3
  51.3 5.4 collective-permute-done.41
  56.7 1.2 copy-done.3
  57.9 1.2 collective-permute-start
  59.1 33.3 %collective-permute-done.42 = bf16[4,320,640]{2,1,0:T(8,128)(2,1)} collective-permute-done((bf16[4,320,640]{2,1,0:T(8,128)(2,1)}, bf16[4,320,640]{2,1,0:T(8,128)(2,1)}, u32[]{:S(2)}, u32[]{:S(2)}) %collective-permute-start.42) | collective-permute-done | bytes 1638432 | tf_op jit(solution)/shard_map/ppermute | solution.py:54
  92.4 1.2 collective-permute-start.1
  95.7 163.2 %keep.5 = (bf16[13,40,640]{2,1,0:T(8,128)(2,1)}, bf16[13,40,640]{2,1,0:T(8,128)(2,1)}, bf16[13,40,640]{2,1,0:T(8,128)(2,1)}, bf16[13,40,640]{2,1,0:T(8,128)(2,1)...) custom-call(s32[2]{0:T(128)} %pad_add_fusion.place_ref, ...), custom_call_target="tpu_custom_call" | custom-call | bytes 10649600 | tf_op jit(solution)/shard_map/keep/pallas_call | solution.py:124
  259.0 1.3 collective-permute-start.43
  260.2 1.3 collective-permute-start.44
  261.7 3.3 collective-permute-start.47
  265.0 163.2 %keep.4 = (bf16[13,40,640]{2,1,0:T(8,128)(2,1)}, bf16[13,40,640]{2,1,0:T(8,128)(2,1)}, bf16[13,40,640]{2,1,0:T(8,128)(2,1)}, bf16[13,40,640]{2,1,0:T(8,128)(2,1)...) custom-call(s32[2]{0:T(128)} %pad_add_fusion.place_ref, ...), custom_call_target="tpu_custom_call" | custom-call | bytes 10649600 | tf_op jit(solution)/shard_map/keep/pallas_call | solution.py:124
  428.5 1.2 collective-permute-start.49
  429.7 1.2 collective-permute-start.23
  430.9 3.1 collective-permute-start.24
  434.1 163.3 %keep.3 = (bf16[13,40,640]{2,1,0:T(8,128)(2,1)}, bf16[13,40,640]{2,1,0:T(8,128)(2,1)}, bf16[13,40,640]{2,1,0:T(8,128)(2,1)}, bf16[13,40,640]{2,1,0:T(8,128)(2,1)...) custom-call(s32[2]{0:T(128)} %pad_add_fusion.place_ref, ...), custom_call_target="tpu_custom_call" | custom-call | bytes 10649600 | tf_op jit(solution)/shard_map/keep/pallas_call | solution.py:124
  599.5 3.0 collective-permute-start.27
  602.8 1.2 collective-permute-start.29
  604.8 1.2 collective-permute-start.3
  607.3 62.4 %collective-permute-done.26 = bf16[13,40,640]{2,1,0:T(8,128)(2,1)S(1)} collective-permute-done((bf16[13,40,640]{2,1,0:T(8,128)(2,1)}, bf16[13,40,640]{2,1,0:T(8,128)(2,1)S(1)}, u32[]{:S(2)}, u32[]{:S(2)}) %collective-permute-start.26) | collective-permute-done | bytes 665632 | tf_op jit(solution)/shard_map/ppermute | solution.py:54
  669.8 4.7 collective-permute-start.4
  674.5 9.6 collective-permute-done.27
  684.1 5.6 collective-permute-start.5
  689.7 12.3 collective-permute-done.28
  702.0 30.9 %collective-permute-done.29 = bf16[13,40,640]{2,1,0:T(8,128)(2,1)} collective-permute-done((bf16[13,40,640]{2,1,0:T(8,128)(2,1)}, bf16[13,40,640]{2,1,0:T(8,128)(2,1)}, u32[]{:S(2)}, u32[]{:S(2)}) %collective-permute-start.29) | collective-permute-done | bytes 665632 | tf_op jit(solution)/shard_map/ppermute | solution.py:54
  733.1 51.8 %spectral.5 = (bf16[520,640]{1,0:T(8,128)(2,1)}, bf16[520,640]{1,0:T(8,128)(2,1)}, bf16[520,640]{1,0:T(8,128)(2,1)}, bf16[520,640]{1,0:T(8,128)(2,1)}, bf16[520,...) custom-call(s32[2]{0:T(128)} %pad_add_fusion.place_ref, ...), custom_call_target="tpu_custom_call" | custom-call | flops 20000000000 | bytes 18841600 | tf_op jit(solution)/shard_map/spectral/pallas_call | solution.py:295
  784.9 1.5 collective-permute-start.9
  787.3 1.2 collective-permute-start.50
  788.4 2.4 collective-permute-start.51
  792.8 24.8 %collective-permute-done.8 = bf16[13,40,640]{2,1,0:T(8,128)(2,1)} collective-permute-done((bf16[13,40,640]{2,1,0:T(8,128)(2,1)}, bf16[13,40,640]{2,1,0:T(8,128)(2,1)}, u32[]{:S(2)}, u32[]{:S(2)}) %collective-permute-start.8) | collective-permute-done | bytes 665632 | tf_op jit(solution)/shard_map/ppermute | solution.py:54
  817.7 28.0 %collective-permute-done.9 = bf16[13,40,640]{2,1,0:T(8,128)(2,1)} collective-permute-done((bf16[13,40,640]{2,1,0:T(8,128)(2,1)}, bf16[13,40,640]{2,1,0:T(8,128)(2,1)}, u32[]{:S(2)}, u32[]{:S(2)}) %collective-permute-start.9) | collective-permute-done | bytes 665632 | tf_op jit(solution)/shard_map/ppermute | solution.py:54
  845.8 1.5 collective-permute-start.56
  847.3 51.4 %spectral.4 = (bf16[520,640]{1,0:T(8,128)(2,1)}, bf16[520,640]{1,0:T(8,128)(2,1)}, bf16[520,640]{1,0:T(8,128)(2,1)}, bf16[520,640]{1,0:T(8,128)(2,1)}, bf16[520,...) custom-call(s32[2]{0:T(128)} %pad_add_fusion.place_ref, ...), custom_call_target="tpu_custom_call" | custom-call | flops 20000000000 | bytes 18841600 | tf_op jit(solution)/shard_map/spectral/pallas_call | solution.py:295
  898.7 1.2 collective-permute-start.30
  899.9 10.0 collective-permute-done.53.refs_4_
  909.9 6.6 collective-permute-start.31
  916.5 7.8 collective-permute-done.54.refs_5_
  924.3 7.5 collective-permute-start.32
  931.8 12.3 collective-permute-done.55.refs_6_
  944.0 31.4 %collective-permute-done.56.refs_7_ = bf16[13,40,640]{2,1,0:T(8,128)(2,1)} collective-permute-done((bf16[13,40,640]{2,1,0:T(8,128)(2,1)}, bf16[13,40,640]{2,1,0:T(8,128)(2,1)}, u32[]{:S(2)}, u32[]{:S(2)}) %collective-permute-start.56) | collective-permute-done | bytes 665632 | tf_op jit(solution)/shard_map/ppermute | solution.py:54
  975.5 51.6 %spectral.3 = (bf16[520,640]{1,0:T(8,128)(2,1)}, bf16[520,640]{1,0:T(8,128)(2,1)}, bf16[520,640]{1,0:T(8,128)(2,1)}, bf16[520,640]{1,0:T(8,128)(2,1)}, bf16[520,...) custom-call(s32[2]{0:T(128)} %pad_add_fusion.place_ref, ...), custom_call_target="tpu_custom_call" | custom-call | flops 20000000000 | bytes 18841600 | tf_op jit(solution)/shard_map/spectral/pallas_call | solution.py:295
  1027.2 1.4 collective-permute-start.36
  1028.6 1.2 collective-permute-start.10
  1029.8 2.2 collective-permute-start.11
  1032.1 200.4 %spread.5 = (bf16[4,8,40,640]{3,2,1,0:T(8,128)(2,1)}, bf16[4,8,40,640]{3,2,1,0:T(8,128)(2,1)}, bf16[4,8,40,640]{3,2,1,0:T(8,128)(2,1)}, bf16[4,8,40,640]{3,2,1,0:T(8,128)(2,1)}) custom-call(s32[2]{0:T(128)} %pad_add_fusion.place_ref, s32[16]{0:T(128)} %get-tuple-element.150.slot_ref, bf16[13,40,640]{2,1,0:T(8,128)(2,1)} %bitcast.94, ...), custom_call_target="tpu_custom_call" | custom-call | bytes 13107200 | tf_op jit(solution)/shard_map/spread/pallas_call | solution.py:158
  1232.5 2.2 collective-permute-start.57
  1235.6 4.0 collective-permute-start.13
  1239.7 1.2 collective-permute-start.15
  1240.8 200.4 %spread.4 = (bf16[4,8,40,640]{3,2,1,0:T(8,128)(2,1)}, bf16[4,8,40,640]{3,2,1,0:T(8,128)(2,1)}, bf16[4,8,40,640]{3,2,1,0:T(8,128)(2,1)}, bf16[4,8,40,640]{3,2,1,0:T(8,128)(2,1)}) custom-call(s32[2]{0:T(128)} %pad_add_fusion.place_ref, s32[16]{0:T(128)} %get-tuple-element.150.slot_ref, bf16[13,40,640]{2,1,0:T(8,128)(2,1)} %bitcast.96, ...), custom_call_target="tpu_custom_call" | custom-call | bytes 13107200 | tf_op jit(solution)/shard_map/spread/pallas_call | solution.py:158
  1441.2 1.4 collective-permute-start.58
  1445.5 1.3 collective-permute-start.16
  1446.8 30.7 %collective-permute-done.16.refs_7_ = bf16[13,40,640]{2,1,0:T(8,128)(2,1)S(1)} collective-permute-done((bf16[13,40,640]{2,1,0:T(8,128)(2,1)}, bf16[13,40,640]{2,1,0:T(8,128)(2,1)S(1)}, u32[]{:S(2)}, u32[]{:S(2)}) %collective-permute-start.16) | collective-permute-done | bytes 665632 | tf_op jit(solution)/shard_map/ppermute | solution.py:54
  1477.5 2.4 collective-permute-start.39
  1479.9 200.4 %spread.3 = (bf16[4,8,40,640]{3,2,1,0:T(8,128)(2,1)}, bf16[4,8,40,640]{3,2,1,0:T(8,128)(2,1)}, bf16[4,8,40,640]{3,2,1,0:T(8,128)(2,1)}, bf16[4,8,40,640]{3,2,1,0:T(8,128)(2,1)}) custom-call(s32[2]{0:T(128)} %pad_add_fusion.place_ref, s32[16]{0:T(128)} %get-tuple-element.150.slot_ref, bf16[13,40,640]{2,1,0:T(8,128)(2,1)} %bitcast.95, ...), custom_call_target="tpu_custom_call" | custom-call | bytes 13107200 | tf_op jit(solution)/shard_map/spread/pallas_call | solution.py:158
  1680.9 1.6 collective-permute-start.19
  1682.5 18.5 %synthesise.3.refs_4_ = bf16[4,3,640,1280]{3,2,1,0:T(8,128)(2,1)} custom-call(s32[2]{0:T(128)} %pad_add_fusion.place_ref, bf16[4,320,1280]{2,1,0:T(8,128)(2,1)} %constant.50.table_ref, bf16[4,320,640]{2,1,0:T(8,128)(2,1)} %bitcast.101, bf16[4,320,640]{2,1,0:T(8,128)(2,1)} %bitcast.76.refs_1_, bf16[4,320,640]{2,1,0:T(8,128)(2,1)} %bitcast.77.refs_2_, ...), custom_call_target="tpu_custom_call" | custom-call | flops 8388608000 | bytes 13107200 | tf_op jit(solution)/shard_map/synthesise/pallas_call | solution.py:195
  1702.2 18.3 %synthesise.4.refs_4_ = bf16[4,3,640,1280]{3,2,1,0:T(8,128)(2,1)} custom-call(s32[2]{0:T(128)} %pad_add_fusion.place_ref, bf16[4,320,1280]{2,1,0:T(8,128)(2,1)} %constant.50.table_ref, bf16[4,320,640]{2,1,0:T(8,128)(2,1)} %bitcast.90, bf16[4,320,640]{2,1,0:T(8,128)(2,1)} %bitcast.91, bf16[4,320,640]{2,1,0:T(8,128)(2,1)} %bitcast.93, ...), custom_call_target="tpu_custom_call", output_to_operand_aliasing={{}: (6, {})} | custom-call | flops 8388608000 | bytes 13107200 | tf_op jit(solution)/shard_map/synthesise/pallas_call | solution.py:195
  1720.5 32.9 %collective-permute-done.19 = bf16[4,8,40,640]{3,2,1,0:T(8,128)(2,1)} collective-permute-done((bf16[4,8,40,640]{3,2,1,0:T(8,128)(2,1)}, bf16[4,8,40,640]{3,2,1,0:T(8,128)(2,1)}, u32[]{:S(2)}, u32[]{:S(2)}) %collective-permute-start.19) | collective-permute-done | bytes 1638432 | tf_op jit(solution)/shard_map/ppermute | solution.py:54
  1753.4 18.3 %synthesise.5 = bf16[4,3,640,1280]{3,2,1,0:T(8,128)(2,1)} custom-call(s32[2]{0:T(128)} %pad_add_fusion.place_ref, bf16[4,320,1280]{2,1,0:T(8,128)(2,1)} %constant.50.table_ref, bf16[4,320,640]{2,1,0:T(8,128)(2,1)} %bitcast.92, bf16[4,320,640]{2,1,0:T(8,128)(2,1)} %bitcast.26.refs_1_, ...), custom_call_target="tpu_custom_call", output_to_operand_aliasing={{}: (6, {})} | custom-call | flops 8388608000 | bytes 13107200 | tf_op jit(solution)/shard_map/synthesise/pallas_call | solution.py:195
  (156 shorter events, 18.0 us)
Async XLA Ops:
  18.4 32.2 %collective-permute-start.40 = (bf16[4,320,640]{2,1,0:T(8,128)(2,1)}, bf16[4,320,640]{2,1,0:T(8,128)(2,1)S(1)}, u32[]{:S(2)}, u32[]{:S(2)}) collective-permute-start(bf16[4,320,640]{2,1,0:T(8,128)(2,1)} %get-tuple-element.126), channel_id=1, source_target_pairs={{0,8},{8,0},{16,24},{24,16},{1,9},{9,1},{17,25},{25,17},{2,10},{10... | collective-permute-start | bytes 4915208 | tf_op jit(solution)/shard_map/ppermute | solution.py:54
  19.1 37.6 %collective-permute-start.41 = (bf16[4,320,640]{2,1,0:T(8,128)(2,1)}, bf16[4,320,640]{2,1,0:T(8,128)(2,1)S(1)}, u32[]{:S(2)}, u32[]{:S(2)}) collective-permute-start(bf16[4,320,640]{2,1,0:T(8,128)(2,1)} %get-tuple-element.127), channel_id=1, source_target_pairs={{0,16},{8,24},{16,0},{24,8},{1,17},{9,25},{17,1},{25,9},{2,18},{10... | collective-permute-start | bytes 4915208 | tf_op jit(solution)/shard_map/ppermute | solution.py:54
  20.3 72.1 %collective-permute-start.42 = (bf16[4,320,640]{2,1,0:T(8,128)(2,1)}, bf16[4,320,640]{2,1,0:T(8,128)(2,1)}, u32[]{:S(2)}, u32[]{:S(2)}) collective-permute-start(bf16[4,320,640]{2,1,0:T(8,128)(2,1)} %get-tuple-element.128), channel_id=1, source_target_pairs={{0,24},{8,16},{16,8},{24,0},{1,25},{9,17},{17,9},{25,1},{2,26},{10... | collective-permute-start | bytes 4915208 | tf_op jit(solution)/shard_map/ppermute | solution.py:54
  34.9 58.8 %collective-permute-start.20 = (bf16[4,320,640]{2,1,0:T(8,128)(2,1)}, bf16[4,320,640]{2,1,0:T(8,128)(2,1)}, u32[]{:S(2)}, u32[]{:S(2)}) collective-permute-start(bf16[4,320,640]{2,1,0:T(8,128)(2,1)} %get-tuple-element.102), channel_id=1, source_target_pairs={{0,8},{8,0},{16,24},{24,16},{1,9},{9,1},{17,25},{25,17},{2,10},{10... | collective-permute-start | bytes 4915208 | tf_op jit(solution)/shard_map/ppermute | solution.py:54
  35.1 223.8 %collective-permute-start.21 = (bf16[4,320,640]{2,1,0:T(8,128)(2,1)}, bf16[4,320,640]{2,1,0:T(8,128)(2,1)}, u32[]{:S(2)}, u32[]{:S(2)}) collective-permute-start(bf16[4,320,640]{2,1,0:T(8,128)(2,1)} %get-tuple-element.103), channel_id=1, source_target_pairs={{0,16},{8,24},{16,0},{24,8},{1,17},{9,25},{17,1},{25,9},{2,18},{10... | collective-permute-start | bytes 4915208 | tf_op jit(solution)/shard_map/ppermute | solution.py:54
  50.6 209.7 %collective-permute-start.22 = (bf16[4,320,640]{2,1,0:T(8,128)(2,1)}, bf16[4,320,640]{2,1,0:T(8,128)(2,1)}, u32[]{:S(2)}, u32[]{:S(2)}) collective-permute-start(bf16[4,320,640]{2,1,0:T(8,128)(2,1)} %get-tuple-element.104), channel_id=1, source_target_pairs={{0,24},{8,16},{16,8},{24,0},{1,25},{9,17},{17,9},{25,1},{2,26},{10... | collective-permute-start | bytes 4915208 | tf_op jit(solution)/shard_map/ppermute | solution.py:54
  57.9 203.6 %collective-permute-start = (bf16[4,320,640]{2,1,0:T(8,128)(2,1)}, bf16[4,320,640]{2,1,0:T(8,128)(2,1)S(1)}, u32[]{:S(2)}, u32[]{:S(2)}) collective-permute-start(bf16[4,320,640]{2,1,0:T(8,128)(2,1)} %get-tuple-element.78), channel_id=1, source_target_pairs={{0,8},{8,0},{16,24},{24,16},{1,9},{9,1},{17,25},{25,17},{2,10},{10... | collective-permute-start | bytes 4915208 | tf_op jit(solution)/shard_map/ppermute | solution.py:54
  92.4 169.3 %collective-permute-start.1 = (bf16[4,320,640]{2,1,0:T(8,128)(2,1)}, bf16[4,320,640]{2,1,0:T(8,128)(2,1)S(1)}, u32[]{:S(2)}, u32[]{:S(2)}) collective-permute-start(bf16[4,320,640]{2,1,0:T(8,128)(2,1)} %get-tuple-element.79), channel_id=1, source_target_pairs={{0,16},{8,24},{16,0},{24,8},{1,17},{9,25},{17,1},{25,9},{2,18},{10... | collective-permute-start | bytes 4915208 | tf_op jit(solution)/shard_map/ppermute | solution.py:54
  93.7 168.0 %collective-permute-start.2 = (bf16[4,320,640]{2,1,0:T(8,128)(2,1)}, bf16[4,320,640]{2,1,0:T(8,128)(2,1)}, u32[]{:S(2)}, u32[]{:S(2)}) collective-permute-start(bf16[4,320,640]{2,1,0:T(8,128)(2,1)} %get-tuple-element.80), channel_id=1, source_target_pairs={{0,24},{8,16},{16,8},{24,0},{1,25},{9,17},{17,9},{25,1},{2,26},{10... | collective-permute-start | bytes 4915208 | tf_op jit(solution)/shard_map/ppermute | solution.py:54
  259.0 169.2 %collective-permute-start.43 = (bf16[13,40,640]{2,1,0:T(8,128)(2,1)}, bf16[13,40,640]{2,1,0:T(8,128)(2,1)}, u32[]{:S(2)}, u32[]{:S(2)}) collective-permute-start(bf16[13,40,640]{2,1,0:T(8,128)(2,1)} %get-tuple-element.130), channel_id=1, source_target_pairs={{0,1},{1,0},{2,3},{3,2},{4,5},{5,4},{6,7},{7,6},{8,9},{9,8},{10,11... | collective-permute-start | bytes 1996808 | tf_op jit(solution)/shard_map/ppermute | solution.py:54
  260.2 168.2 %collective-permute-start.44 = (bf16[13,40,640]{2,1,0:T(8,128)(2,1)}, bf16[13,40,640]{2,1,0:T(8,128)(2,1)}, u32[]{:S(2)}, u32[]{:S(2)}) collective-permute-start(bf16[13,40,640]{2,1,0:T(8,128)(2,1)} %get-tuple-element.131), channel_id=1, source_target_pairs={{0,2},{1,3},{2,0},{3,1},{4,6},{5,7},{6,4},{7,5},{8,10},{9,11},{10,... | collective-permute-start | bytes 1996808 | tf_op jit(solution)/shard_map/ppermute | solution.py:54
  261.5 168.2 %collective-permute-start.45 = (bf16[13,40,640]{2,1,0:T(8,128)(2,1)}, bf16[13,40,640]{2,1,0:T(8,128)(2,1)}, u32[]{:S(2)}, u32[]{:S(2)}) collective-permute-start(bf16[13,40,640]{2,1,0:T(8,128)(2,1)} %get-tuple-element.132), channel_id=1, source_target_pairs={{0,3},{1,2},{2,1},{3,0},{4,7},{5,6},{6,5},{7,4},{8,11},{9,10},{10,... | collective-permute-start | bytes 1996808 | tf_op jit(solution)/shard_map/ppermute | solution.py:54
  261.7 169.2 %collective-permute-start.46 = (bf16[13,40,640]{2,1,0:T(8,128)(2,1)}, bf16[13,40,640]{2,1,0:T(8,128)(2,1)}, u32[]{:S(2)}, u32[]{:S(2)}) collective-permute-start(bf16[13,40,640]{2,1,0:T(8,128)(2,1)} %get-tuple-element.133), channel_id=1, source_target_pairs={{0,4},{1,5},{2,6},{3,7},{4,0},{5,1},{6,2},{7,3},{8,12},{9,13},{10,... | collective-permute-start | bytes 1996808 | tf_op jit(solution)/shard_map/ppermute | solution.py:54
  261.7 172.3 %collective-permute-start.47 = (bf16[13,40,640]{2,1,0:T(8,128)(2,1)}, bf16[13,40,640]{2,1,0:T(8,128)(2,1)}, u32[]{:S(2)}, u32[]{:S(2)}) collective-permute-start(bf16[13,40,640]{2,1,0:T(8,128)(2,1)} %get-tuple-element.134), channel_id=1, source_target_pairs={{0,5},{1,4},{2,7},{3,6},{4,1},{5,0},{6,3},{7,2},{8,13},{9,12},{10,... | collective-permute-start | bytes 1996808 | tf_op jit(solution)/shard_map/ppermute | solution.py:54
  428.2 169.2 %collective-permute-start.48 = (bf16[13,40,640]{2,1,0:T(8,128)(2,1)}, bf16[13,40,640]{2,1,0:T(8,128)(2,1)S(1)}, u32[]{:S(2)}, u32[]{:S(2)}) collective-permute-start(bf16[13,40,640]{2,1,0:T(8,128)(2,1)} %get-tuple-element.135), channel_id=1, source_target_pairs={{0,6},{1,7},{2,4},{3,5},{4,2},{5,3},{6,0},{7,1},{8,14},{9,15},{10,... | collective-permute-start | bytes 1996808 | tf_op jit(solution)/shard_map/ppermute | solution.py:54
  428.5 170.2 %collective-permute-start.49 = (bf16[13,40,640]{2,1,0:T(8,128)(2,1)}, bf16[13,40,640]{2,1,0:T(8,128)(2,1)S(1)}, u32[]{:S(2)}, u32[]{:S(2)}) collective-permute-start(bf16[13,40,640]{2,1,0:T(8,128)(2,1)} %get-tuple-element.136), channel_id=1, source_target_pairs={{0,7},{1,6},{2,5},{3,4},{4,3},{5,2},{6,1},{7,0},{8,15},{9,14},{10,... | collective-permute-start | bytes 1996808 | tf_op jit(solution)/shard_map/ppermute | solution.py:54
  429.7 172.8 %collective-permute-start.23 = (bf16[13,40,640]{2,1,0:T(8,128)(2,1)}, bf16[13,40,640]{2,1,0:T(8,128)(2,1)S(1)}, u32[]{:S(2)}, u32[]{:S(2)}) collective-permute-start(bf16[13,40,640]{2,1,0:T(8,128)(2,1)} %get-tuple-element.106), channel_id=1, source_target_pairs={{0,1},{1,0},{2,3},{3,2},{4,5},{5,4},{6,7},{7,6},{8,9},{9,8},{10,11... | collective-permute-start | bytes 1996808 | tf_op jit(solution)/shard_map/ppermute | solution.py:54
  430.9 171.8 %collective-permute-start.24 = (bf16[13,40,640]{2,1,0:T(8,128)(2,1)}, bf16[13,40,640]{2,1,0:T(8,128)(2,1)S(1)}, u32[]{:S(2)}, u32[]{:S(2)}) collective-permute-start(bf16[13,40,640]{2,1,0:T(8,128)(2,1)} %get-tuple-element.107), channel_id=1, source_target_pairs={{0,2},{1,3},{2,0},{3,1},{4,6},{5,7},{6,4},{7,5},{8,10},{9,11},{10,... | collective-permute-start | bytes 1996808 | tf_op jit(solution)/shard_map/ppermute | solution.py:54
  434.0 170.0 %collective-permute-start.25 = (bf16[13,40,640]{2,1,0:T(8,128)(2,1)}, bf16[13,40,640]{2,1,0:T(8,128)(2,1)S(1)}, u32[]{:S(2)}, u32[]{:S(2)}) collective-permute-start(bf16[13,40,640]{2,1,0:T(8,128)(2,1)} %get-tuple-element.108), channel_id=1, source_target_pairs={{0,3},{1,2},{2,1},{3,0},{4,7},{5,6},{6,5},{7,4},{8,11},{9,10},{10,... | collective-permute-start | bytes 1996808 | tf_op jit(solution)/shard_map/ppermute | solution.py:54
  598.3 71.5 %collective-permute-start.26 = (bf16[13,40,640]{2,1,0:T(8,128)(2,1)}, bf16[13,40,640]{2,1,0:T(8,128)(2,1)S(1)}, u32[]{:S(2)}, u32[]{:S(2)}) collective-permute-start(bf16[13,40,640]{2,1,0:T(8,128)(2,1)} %get-tuple-element.109), channel_id=1, source_target_pairs={{0,4},{1,5},{2,6},{3,7},{4,0},{5,1},{6,2},{7,3},{8,12},{9,13},{10,... | collective-permute-start | bytes 1996808 | tf_op jit(solution)/shard_map/ppermute | solution.py:54
  599.5 84.6 %collective-permute-start.27 = (bf16[13,40,640]{2,1,0:T(8,128)(2,1)}, bf16[13,40,640]{2,1,0:T(8,128)(2,1)S(1)}, u32[]{:S(2)}, u32[]{:S(2)}) collective-permute-start(bf16[13,40,640]{2,1,0:T(8,128)(2,1)} %get-tuple-element.110), channel_id=1, source_target_pairs={{0,5},{1,4},{2,7},{3,6},{4,1},{5,0},{6,3},{7,2},{8,13},{9,12},{10,... | collective-permute-start | bytes 1996808 | tf_op jit(solution)/shard_map/ppermute | solution.py:54
  602.5 99.5 %collective-permute-start.28 = (bf16[13,40,640]{2,1,0:T(8,128)(2,1)}, bf16[13,40,640]{2,1,0:T(8,128)(2,1)}, u32[]{:S(2)}, u32[]{:S(2)}) collective-permute-start(bf16[13,40,640]{2,1,0:T(8,128)(2,1)} %get-tuple-element.111), channel_id=1, source_target_pairs={{0,6},{1,7},{2,4},{3,5},{4,2},{5,3},{6,0},{7,1},{8,14},{9,15},{10,... | collective-permute-start | bytes 1996808 | tf_op jit(solution)/shard_map/ppermute | solution.py:54
  602.8 130.2 %collective-permute-start.29 = (bf16[13,40,640]{2,1,0:T(8,128)(2,1)}, bf16[13,40,640]{2,1,0:T(8,128)(2,1)}, u32[]{:S(2)}, u32[]{:S(2)}) collective-permute-start(bf16[13,40,640]{2,1,0:T(8,128)(2,1)} %get-tuple-element.112), channel_id=1, source_target_pairs={{0,7},{1,6},{2,5},{3,4},{4,3},{5,2},{6,1},{7,0},{8,15},{9,14},{10,... | collective-permute-start | bytes 1996808 | tf_op jit(solution)/shard_map/ppermute | solution.py:54
  604.8 128.1 %collective-permute-start.3 = (bf16[13,40,640]{2,1,0:T(8,128)(2,1)}, bf16[13,40,640]{2,1,0:T(8,128)(2,1)S(1)}, u32[]{:S(2)}, u32[]{:S(2)}) collective-permute-start(bf16[13,40,640]{2,1,0:T(8,128)(2,1)} %get-tuple-element.82), channel_id=1, source_target_pairs={{0,1},{1,0},{2,3},{3,2},{4,5},{5,4},{6,7},{7,6},{8,9},{9,8},{10,11... | collective-permute-start | bytes 1996808 | tf_op jit(solution)/shard_map/ppermute | solution.py:54
  669.8 115.1 %collective-permute-start.4 = (bf16[13,40,640]{2,1,0:T(8,128)(2,1)}, bf16[13,40,640]{2,1,0:T(8,128)(2,1)S(1)}, u32[]{:S(2)}, u32[]{:S(2)}) collective-permute-start(bf16[13,40,640]{2,1,0:T(8,128)(2,1)} %get-tuple-element.83), channel_id=1, source_target_pairs={{0,2},{1,3},{2,0},{3,1},{4,6},{5,7},{6,4},{7,5},{8,10},{9,11},{10,... | collective-permute-start | bytes 1996808 | tf_op jit(solution)/shard_map/ppermute | solution.py:54
  684.1 102.3 %collective-permute-start.5 = (bf16[13,40,640]{2,1,0:T(8,128)(2,1)}, bf16[13,40,640]{2,1,0:T(8,128)(2,1)S(1)}, u32[]{:S(2)}, u32[]{:S(2)}) collective-permute-start(bf16[13,40,640]{2,1,0:T(8,128)(2,1)} %get-tuple-element.84), channel_id=1, source_target_pairs={{0,3},{1,2},{2,1},{3,0},{4,7},{5,6},{6,5},{7,4},{8,11},{9,10},{10,... | collective-permute-start | bytes 1996808 | tf_op jit(solution)/shard_map/ppermute | solution.py:54
  702.0 86.4 %collective-permute-start.6 = (bf16[13,40,640]{2,1,0:T(8,128)(2,1)}, bf16[13,40,640]{2,1,0:T(8,128)(2,1)S(1)}, u32[]{:S(2)}, u32[]{:S(2)}) collective-permute-start(bf16[13,40,640]{2,1,0:T(8,128)(2,1)} %get-tuple-element.85), channel_id=1, source_target_pairs={{0,4},{1,5},{2,6},{3,7},{4,0},{5,1},{6,2},{7,3},{8,12},{9,13},{10,... | collective-permute-start | bytes 1996808 | tf_op jit(solution)/shard_map/ppermute | solution.py:54
  733.0 59.2 %collective-permute-start.7 = (bf16[13,40,640]{2,1,0:T(8,128)(2,1)}, bf16[13,40,640]{2,1,0:T(8,128)(2,1)}, u32[]{:S(2)}, u32[]{:S(2)}) collective-permute-start(bf16[13,40,640]{2,1,0:T(8,128)(2,1)} %get-tuple-element.86), channel_id=1, source_target_pairs={{0,5},{1,4},{2,7},{3,6},{4,1},{5,0},{6,3},{7,2},{8,13},{9,12},{10,... | collective-permute-start | bytes 1996808 | tf_op jit(solution)/shard_map/ppermute | solution.py:54
  733.0 84.7 %collective-permute-start.8 = (bf16[13,40,640]{2,1,0:T(8,128)(2,1)}, bf16[13,40,640]{2,1,0:T(8,128)(2,1)}, u32[]{:S(2)}, u32[]{:S(2)}) collective-permute-start(bf16[13,40,640]{2,1,0:T(8,128)(2,1)} %get-tuple-element.87), channel_id=1, source_target_pairs={{0,6},{1,7},{2,4},{3,5},{4,2},{5,3},{6,0},{7,1},{8,14},{9,15},{10,... | collective-permute-start | bytes 1996808 | tf_op jit(solution)/shard_map/ppermute | solution.py:54
  784.9 60.8 %collective-permute-start.9 = (bf16[13,40,640]{2,1,0:T(8,128)(2,1)}, bf16[13,40,640]{2,1,0:T(8,128)(2,1)}, u32[]{:S(2)}, u32[]{:S(2)}) collective-permute-start(bf16[13,40,640]{2,1,0:T(8,128)(2,1)} %get-tuple-element.88), channel_id=1, source_target_pairs={{0,7},{1,6},{2,5},{3,4},{4,3},{5,2},{6,1},{7,0},{8,15},{9,14},{10,... | collective-permute-start | bytes 1996808 | tf_op jit(solution)/shard_map/ppermute | solution.py:54
  787.3 58.4 %collective-permute-start.50 = (bf16[13,40,640]{2,1,0:T(8,128)(2,1)}, bf16[13,40,640]{2,1,0:T(8,128)(2,1)S(1)}, u32[]{:S(2)}, u32[]{:S(2)}) collective-permute-start(bf16[13,40,640]{2,1,0:T(8,128)(2,1)} %bitcast.136), channel_id=1, source_target_pairs={{0,1},{1,0},{2,3},{3,2},{4,5},{5,4},{6,7},{7,6},{8,9},{9,8},{10,11... | collective-permute-start | bytes 1996808 | tf_op jit(solution)/shard_map/ppermute | solution.py:54
  788.4 57.3 %collective-permute-start.51 = (bf16[13,40,640]{2,1,0:T(8,128)(2,1)}, bf16[13,40,640]{2,1,0:T(8,128)(2,1)S(1)}, u32[]{:S(2)}, u32[]{:S(2)}) collective-permute-start(bf16[13,40,640]{2,1,0:T(8,128)(2,1)} %bitcast.135), channel_id=1, source_target_pairs={{0,2},{1,3},{2,0},{3,1},{4,6},{5,7},{6,4},{7,5},{8,10},{9,11},{10,... | collective-permute-start | bytes 1996808 | tf_op jit(solution)/shard_map/ppermute | solution.py:54
  792.2 106.5 %collective-permute-start.52 = (bf16[13,40,640]{2,1,0:T(8,128)(2,1)}, bf16[13,40,640]{2,1,0:T(8,128)(2,1)S(1)}, u32[]{:S(2)}, u32[]{:S(2)}) collective-permute-start(bf16[13,40,640]{2,1,0:T(8,128)(2,1)} %bitcast.128), channel_id=1, source_target_pairs={{0,3},{1,2},{2,1},{3,0},{4,7},{5,6},{6,5},{7,4},{8,11},{9,10},{10,... | collective-permute-start | bytes 1996808 | tf_op jit(solution)/shard_map/ppermute | solution.py:54
  817.7 92.3 %collective-permute-start.53 = (bf16[13,40,640]{2,1,0:T(8,128)(2,1)}, bf16[13,40,640]{2,1,0:T(8,128)(2,1)S(1)}, u32[]{:S(2)}, u32[]{:S(2)}) collective-permute-start(bf16[13,40,640]{2,1,0:T(8,128)(2,1)} %bitcast.127), channel_id=1, source_target_pairs={{0,4},{1,5},{2,6},{3,7},{4,0},{5,1},{6,2},{7,3},{8,12},{9,13},{10,... | collective-permute-start | bytes 1996808 | tf_op jit(solution)/shard_map/ppermute | solution.py:54
  845.7 78.6 %collective-permute-start.54 = (bf16[13,40,640]{2,1,0:T(8,128)(2,1)}, bf16[13,40,640]{2,1,0:T(8,128)(2,1)S(1)}, u32[]{:S(2)}, u32[]{:S(2)}) collective-permute-start(bf16[13,40,640]{2,1,0:T(8,128)(2,1)} %bitcast.126), channel_id=1, source_target_pairs={{0,5},{1,4},{2,7},{3,6},{4,1},{5,0},{6,3},{7,2},{8,13},{9,12},{10,... | collective-permute-start | bytes 1996808 | tf_op jit(solution)/shard_map/ppermute | solution.py:54
  845.7 98.4 %collective-permute-start.55 = (bf16[13,40,640]{2,1,0:T(8,128)(2,1)}, bf16[13,40,640]{2,1,0:T(8,128)(2,1)}, u32[]{:S(2)}, u32[]{:S(2)}) collective-permute-start(bf16[13,40,640]{2,1,0:T(8,128)(2,1)} %bitcast.123), channel_id=1, source_target_pairs={{0,6},{1,7},{2,4},{3,5},{4,2},{5,3},{6,0},{7,1},{8,14},{9,15},{10,... | collective-permute-start | bytes 1996808 | tf_op jit(solution)/shard_map/ppermute | solution.py:54
  845.8 129.7 %collective-permute-start.56 = (bf16[13,40,640]{2,1,0:T(8,128)(2,1)}, bf16[13,40,640]{2,1,0:T(8,128)(2,1)}, u32[]{:S(2)}, u32[]{:S(2)}) collective-permute-start(bf16[13,40,640]{2,1,0:T(8,128)(2,1)} %bitcast.120), channel_id=1, source_target_pairs={{0,7},{1,6},{2,5},{3,4},{4,3},{5,2},{6,1},{7,0},{8,15},{9,14},{10,... | collective-permute-start | bytes 1996808 | tf_op jit(solution)/shard_map/ppermute | solution.py:54
  898.7 128.4 %collective-permute-start.30 = (bf16[13,40,640]{2,1,0:T(8,128)(2,1)}, bf16[13,40,640]{2,1,0:T(8,128)(2,1)S(1)}, u32[]{:S(2)}, u32[]{:S(2)}) collective-permute-start(bf16[13,40,640]{2,1,0:T(8,128)(2,1)} %bitcast.134), channel_id=1, source_target_pairs={{0,1},{1,0},{2,3},{3,2},{4,5},{5,4},{6,7},{7,6},{8,9},{9,8},{10,11... | collective-permute-start | bytes 1996808 | tf_op jit(solution)/shard_map/ppermute | solution.py:54
  909.9 117.2 %collective-permute-start.31 = (bf16[13,40,640]{2,1,0:T(8,128)(2,1)}, bf16[13,40,640]{2,1,0:T(8,128)(2,1)S(1)}, u32[]{:S(2)}, u32[]{:S(2)}) collective-permute-start(bf16[13,40,640]{2,1,0:T(8,128)(2,1)} %bitcast.133), channel_id=1, source_target_pairs={{0,2},{1,3},{2,0},{3,1},{4,6},{5,7},{6,4},{7,5},{8,10},{9,11},{10,... | collective-permute-start | bytes 1996808 | tf_op jit(solution)/shard_map/ppermute | solution.py:54
  924.3 104.3 %collective-permute-start.32 = (bf16[13,40,640]{2,1,0:T(8,128)(2,1)}, bf16[13,40,640]{2,1,0:T(8,128)(2,1)}, u32[]{:S(2)}, u32[]{:S(2)}) collective-permute-start(bf16[13,40,640]{2,1,0:T(8,128)(2,1)} %bitcast.131), channel_id=1, source_target_pairs={{0,3},{1,2},{2,1},{3,0},{4,7},{5,6},{6,5},{7,4},{8,11},{9,10},{10,... | collective-permute-start | bytes 1996808 | tf_op jit(solution)/shard_map/ppermute | solution.py:54
  944.0 85.8 %collective-permute-start.33 = (bf16[13,40,640]{2,1,0:T(8,128)(2,1)}, bf16[13,40,640]{2,1,0:T(8,128)(2,1)}, u32[]{:S(2)}, u32[]{:S(2)}) collective-permute-start(bf16[13,40,640]{2,1,0:T(8,128)(2,1)} %bitcast.129), channel_id=1, source_target_pairs={{0,4},{1,5},{2,6},{3,7},{4,0},{5,1},{6,2},{7,3},{8,12},{9,13},{10,... | collective-permute-start | bytes 1996808 | tf_op jit(solution)/shard_map/ppermute | solution.py:54
  975.5 257.0 %collective-permute-start.34 = (bf16[13,40,640]{2,1,0:T(8,128)(2,1)}, bf16[13,40,640]{2,1,0:T(8,128)(2,1)}, u32[]{:S(2)}, u32[]{:S(2)}) collective-permute-start(bf16[13,40,640]{2,1,0:T(8,128)(2,1)} %bitcast.124), channel_id=1, source_target_pairs={{0,5},{1,4},{2,7},{3,6},{4,1},{5,0},{6,3},{7,2},{8,13},{9,12},{10,... | collective-permute-start | bytes 1996808 | tf_op jit(solution)/shard_map/ppermute | solution.py:54
  1027.1 205.3 %copy-start.10 = (bf16[13,40,640]{2,1,0:T(8,128)(2,1)}, bf16[13,40,640]{2,1,0:T(8,128)(2,1)S(1)}, u32[]{:S(2)}) copy-start(bf16[13,40,640]{2,1,0:T(8,128)(2,1)S(1)} %collective-permute-done.30.refs_1_) | copy-start | bytes 1996804
  1027.1 207.5 %collective-permute-start.35 = (bf16[13,40,640]{2,1,0:T(8,128)(2,1)}, bf16[13,40,640]{2,1,0:T(8,128)(2,1)S(1)}, u32[]{:S(2)}, u32[]{:S(2)}) collective-permute-start(bf16[13,40,640]{2,1,0:T(8,128)(2,1)} %bitcast.121), channel_id=1, source_target_pairs={{0,6},{1,7},{2,4},{3,5},{4,2},{5,3},{6,0},{7,1},{8,14},{9,15},{10,... | collective-permute-start | bytes 1996808 | tf_op jit(solution)/shard_map/ppermute | solution.py:54
  1027.2 205.3 %copy-start.12 = (bf16[13,40,640]{2,1,0:T(8,128)(2,1)}, bf16[13,40,640]{2,1,0:T(8,128)(2,1)S(1)}, u32[]{:S(2)}) copy-start(bf16[13,40,640]{2,1,0:T(8,128)(2,1)S(1)} %collective-permute-done.31.refs_2_) | copy-start | bytes 1996804
  1027.2 208.4 %collective-permute-start.36 = (bf16[13,40,640]{2,1,0:T(8,128)(2,1)}, bf16[13,40,640]{2,1,0:T(8,128)(2,1)}, u32[]{:S(2)}, u32[]{:S(2)}) collective-permute-start(bf16[13,40,640]{2,1,0:T(8,128)(2,1)} %bitcast.118), channel_id=1, source_target_pairs={{0,7},{1,6},{2,5},{3,4},{4,3},{5,2},{6,1},{7,0},{8,15},{9,14},{10,... | collective-permute-start | bytes 1996808 | tf_op jit(solution)/shard_map/ppermute | solution.py:54
  1028.6 211.1 %collective-permute-start.10 = (bf16[13,40,640]{2,1,0:T(8,128)(2,1)}, bf16[13,40,640]{2,1,0:T(8,128)(2,1)S(1)}, u32[]{:S(2)}, u32[]{:S(2)}) collective-permute-start(bf16[13,40,640]{2,1,0:T(8,128)(2,1)} %bitcast.132), channel_id=1, source_target_pairs={{0,1},{1,0},{2,3},{3,2},{4,5},{5,4},{6,7},{7,6},{8,9},{9,8},{10,11... | collective-permute-start | bytes 1996808 | tf_op jit(solution)/shard_map/ppermute | solution.py:54
  1029.8 209.8 %collective-permute-start.11 = (bf16[13,40,640]{2,1,0:T(8,128)(2,1)}, bf16[13,40,640]{2,1,0:T(8,128)(2,1)S(1)}, u32[]{:S(2)}, u32[]{:S(2)}) collective-permute-start(bf16[13,40,640]{2,1,0:T(8,128)(2,1)} %bitcast.130), channel_id=1, source_target_pairs={{0,2},{1,3},{2,0},{3,1},{4,6},{5,7},{6,4},{7,5},{8,10},{9,11},{10,... | collective-permute-start | bytes 1996808 | tf_op jit(solution)/shard_map/ppermute | solution.py:54
  1232.5 245.0 %collective-permute-start.57 = (bf16[4,8,40,640]{3,2,1,0:T(8,128)(2,1)}, bf16[4,8,40,640]{3,2,1,0:T(8,128)(2,1)}, u32[]{:S(2)}, u32[]{:S(2)}) collective-permute-start(bf16[4,8,40,640]{3,2,1,0:T(8,128)(2,1)} %get-tuple-element.146), channel_id=1, source_target_pairs={{0,8},{8,0},{16,24},{24,16},{1,9},{9,1},{17,25},{25,17},{2,10},{10... | collective-permute-start | bytes 4915208 | tf_op jit(solution)/shard_map/ppermute | solution.py:54
  1235.5 205.8 %collective-permute-start.12 = (bf16[13,40,640]{2,1,0:T(8,128)(2,1)}, bf16[13,40,640]{2,1,0:T(8,128)(2,1)S(1)}, u32[]{:S(2)}, u32[]{:S(2)}) collective-permute-start(bf16[13,40,640]{2,1,0:T(8,128)(2,1)} %bitcast.125), channel_id=1, source_target_pairs={{0,3},{1,2},{2,1},{3,0},{4,7},{5,6},{6,5},{7,4},{8,11},{9,10},{10,... | collective-permute-start | bytes 1996808 | tf_op jit(solution)/shard_map/ppermute | solution.py:54
  1235.6 207.0 %collective-permute-start.13 = (bf16[13,40,640]{2,1,0:T(8,128)(2,1)}, bf16[13,40,640]{2,1,0:T(8,128)(2,1)S(1)}, u32[]{:S(2)}, u32[]{:S(2)}) collective-permute-start(bf16[13,40,640]{2,1,0:T(8,128)(2,1)} %bitcast.122), channel_id=1, source_target_pairs={{0,4},{1,5},{2,6},{3,7},{4,0},{5,1},{6,2},{7,3},{8,12},{9,13},{10,... | collective-permute-start | bytes 1996808 | tf_op jit(solution)/shard_map/ppermute | solution.py:54
  1239.7 201.6 %copy-start.13 = (bf16[13,40,640]{2,1,0:T(8,128)(2,1)}, bf16[13,40,640]{2,1,0:T(8,128)(2,1)S(1)}, u32[]{:S(2)}) copy-start(bf16[13,40,640]{2,1,0:T(8,128)(2,1)S(1)} %collective-permute-done.10.refs_1_) | copy-start | bytes 1996804
  1239.7 204.2 %collective-permute-start.14 = (bf16[13,40,640]{2,1,0:T(8,128)(2,1)}, bf16[13,40,640]{2,1,0:T(8,128)(2,1)S(1)}, u32[]{:S(2)}, u32[]{:S(2)}) collective-permute-start(bf16[13,40,640]{2,1,0:T(8,128)(2,1)} %bitcast.119), channel_id=1, source_target_pairs={{0,5},{1,4},{2,7},{3,6},{4,1},{5,0},{6,3},{7,2},{8,13},{9,12},{10,... | collective-permute-start | bytes 1996808 | tf_op jit(solution)/shard_map/ppermute | solution.py:54
  1239.7 201.5 %copy-start.14 = (bf16[13,40,640]{2,1,0:T(8,128)(2,1)}, bf16[13,40,640]{2,1,0:T(8,128)(2,1)S(1)}, u32[]{:S(2)}) copy-start(bf16[13,40,640]{2,1,0:T(8,128)(2,1)S(1)} %collective-permute-done.11.refs_2_) | copy-start | bytes 1996804
  1239.7 205.8 %collective-permute-start.15 = (bf16[13,40,640]{2,1,0:T(8,128)(2,1)}, bf16[13,40,640]{2,1,0:T(8,128)(2,1)}, u32[]{:S(2)}, u32[]{:S(2)}) collective-permute-start(bf16[13,40,640]{2,1,0:T(8,128)(2,1)} %bitcast.117), channel_id=1, source_target_pairs={{0,6},{1,7},{2,4},{3,5},{4,2},{5,3},{6,0},{7,1},{8,14},{9,15},{10,... | collective-permute-start | bytes 1996808 | tf_op jit(solution)/shard_map/ppermute | solution.py:54
  1441.2 239.0 %collective-permute-start.58 = (bf16[4,8,40,640]{3,2,1,0:T(8,128)(2,1)}, bf16[4,8,40,640]{3,2,1,0:T(8,128)(2,1)}, u32[]{:S(2)}, u32[]{:S(2)}) collective-permute-start(bf16[4,8,40,640]{3,2,1,0:T(8,128)(2,1)} %get-tuple-element.147), channel_id=1, source_target_pairs={{0,16},{8,24},{16,0},{24,8},{1,17},{9,25},{17,1},{25,9},{2,18},{10... | collective-permute-start | bytes 4915208 | tf_op jit(solution)/shard_map/ppermute | solution.py:54
  1442.6 237.7 %collective-permute-start.59 = (bf16[4,8,40,640]{3,2,1,0:T(8,128)(2,1)}, bf16[4,8,40,640]{3,2,1,0:T(8,128)(2,1)}, u32[]{:S(2)}, u32[]{:S(2)}) collective-permute-start(bf16[4,8,40,640]{3,2,1,0:T(8,128)(2,1)} %get-tuple-element.148), channel_id=1, source_target_pairs={{0,24},{8,16},{16,8},{24,0},{1,25},{9,17},{17,9},{25,1},{2,26},{10... | collective-permute-start | bytes 4915208 | tf_op jit(solution)/shard_map/ppermute | solution.py:54
  1444.7 236.3 %collective-permute-start.37 = (bf16[4,8,40,640]{3,2,1,0:T(8,128)(2,1)}, bf16[4,8,40,640]{3,2,1,0:T(8,128)(2,1)S(1)}, u32[]{:S(2)}, u32[]{:S(2)}) collective-permute-start(bf16[4,8,40,640]{3,2,1,0:T(8,128)(2,1)} %get-tuple-element.122), channel_id=1, source_target_pairs={{0,8},{8,0},{16,24},{24,16},{1,9},{9,1},{17,25},{25,17},{2,10},{10... | collective-permute-start | bytes 4915208 | tf_op jit(solution)/shard_map/ppermute | solution.py:54
  1445.5 32.0 %collective-permute-start.16 = (bf16[13,40,640]{2,1,0:T(8,128)(2,1)}, bf16[13,40,640]{2,1,0:T(8,128)(2,1)S(1)}, u32[]{:S(2)}, u32[]{:S(2)}) collective-permute-start(bf16[13,40,640]{2,1,0:T(8,128)(2,1)} %bitcast.115), channel_id=1, source_target_pairs={{0,7},{1,6},{2,5},{3,4},{4,3},{5,2},{6,1},{7,0},{8,15},{9,14},{10,... | collective-permute-start | bytes 1996808 | tf_op jit(solution)/shard_map/ppermute | solution.py:54
  1477.5 223.5 %collective-permute-start.38 = (bf16[4,8,40,640]{3,2,1,0:T(8,128)(2,1)}, bf16[4,8,40,640]{3,2,1,0:T(8,128)(2,1)S(1)}, u32[]{:S(2)}, u32[]{:S(2)}) collective-permute-start(bf16[4,8,40,640]{3,2,1,0:T(8,128)(2,1)} %get-tuple-element.123), channel_id=1, source_target_pairs={{0,16},{8,24},{16,0},{24,8},{1,17},{9,25},{17,1},{25,9},{2,18},{10... | collective-permute-start | bytes 4915208 | tf_op jit(solution)/shard_map/ppermute | solution.py:54
  1477.5 223.5 %collective-permute-start.39 = (bf16[4,8,40,640]{3,2,1,0:T(8,128)(2,1)}, bf16[4,8,40,640]{3,2,1,0:T(8,128)(2,1)}, u32[]{:S(2)}, u32[]{:S(2)}) collective-permute-start(bf16[4,8,40,640]{3,2,1,0:T(8,128)(2,1)} %get-tuple-element.124), channel_id=1, source_target_pairs={{0,24},{8,16},{16,8},{24,0},{1,25},{9,17},{17,9},{25,1},{2,26},{10... | collective-permute-start | bytes 4915208 | tf_op jit(solution)/shard_map/ppermute | solution.py:54
  1680.3 40.2 %collective-permute-start.17 = (bf16[4,8,40,640]{3,2,1,0:T(8,128)(2,1)}, bf16[4,8,40,640]{3,2,1,0:T(8,128)(2,1)}, u32[]{:S(2)}, u32[]{:S(2)}) collective-permute-start(bf16[4,8,40,640]{3,2,1,0:T(8,128)(2,1)} %get-tuple-element.98), channel_id=1, source_target_pairs={{0,8},{8,0},{16,24},{24,16},{1,9},{9,1},{17,25},{25,17},{2,10},{10... | collective-permute-start | bytes 4915208 | tf_op jit(solution)/shard_map/ppermute | solution.py:54
  1680.4 40.1 %collective-permute-start.18 = (bf16[4,8,40,640]{3,2,1,0:T(8,128)(2,1)}, bf16[4,8,40,640]{3,2,1,0:T(8,128)(2,1)}, u32[]{:S(2)}, u32[]{:S(2)}) collective-permute-start(bf16[4,8,40,640]{3,2,1,0:T(8,128)(2,1)} %get-tuple-element.99), channel_id=1, source_target_pairs={{0,16},{8,24},{16,0},{24,8},{1,17},{9,25},{17,1},{25,9},{2,18},{10... | collective-permute-start | bytes 4915208 | tf_op jit(solution)/shard_map/ppermute | solution.py:54
  1680.9 72.4 %collective-permute-start.19 = (bf16[4,8,40,640]{3,2,1,0:T(8,128)(2,1)}, bf16[4,8,40,640]{3,2,1,0:T(8,128)(2,1)}, u32[]{:S(2)}, u32[]{:S(2)}) collective-permute-start(bf16[4,8,40,640]{3,2,1,0:T(8,128)(2,1)} %get-tuple-element.100), channel_id=1, source_target_pairs={{0,24},{8,16},{16,8},{24,0},{1,25},{9,17},{17,9},{25,1},{2,26},{10... | collective-permute-start | bytes 4915208 | tf_op jit(solution)/shard_map/ppermute | solution.py:54
  (31 other events, 1572.3 us)

commit v3 on v2

--- a/solution.py
+++ b/solution.py
@@ -97,75 +97,94 @@
 def keep(place, survivors, sources, survivor_count):
     group_count = len(sources)
     member_here, slab_count, rows, points = sources[0].shape
-
-    def kernel(place_ref, survivor_ref, *refs):
+    survivors = survivors[:survivor_count]
+    offset = survivors // member_here ^ place[0]
+    step = jnp.arange(survivor_count, dtype=jnp.int32)
+    seen = (offset[None, None, :] == jnp.arange(group_count, dtype=jnp.int32)[:, None, None]) & (
+        step[None, None, :] <= step[None, :, None]
+    )
+    shown = jnp.max(jnp.where(seen, survivors % member_here, 0), axis=2).reshape(-1)
+
+    def kernel(place_ref, offset_ref, shown_ref, *refs):
         source_refs = refs[:group_count]
-        out_refs = refs[group_count : group_count + slab_count]
-        sems = refs[-1]
-        group, slab = place_ref[0], place_ref[1]
-        for d in range(survivor_count):
-            parent = survivor_ref[d]
-            offset = lax.bitwise_xor(parent // member_here, group)
-            member = parent % member_here
-            for k in range(group_count):
-
-                @pl.when(offset == k)
-                def _(k=k, d=d, member=member):
-                    for s in range(slab_count):
-                        pltpu.make_async_copy(
-                            source_refs[k].at[member, lax.bitwise_xor(slab, s)],
-                            out_refs[s].at[d],
-                            sems.at[s],
-                        ).start()
-
-        for s in range(slab_count):
-            pltpu.make_async_copy(out_refs[s], out_refs[s], sems.at[s]).wait()
+        out_refs = refs[group_count:]
+        slab = place_ref[1]
+        chosen = offset_ref[pl.program_id(0)]
+        for k in range(group_count):
+
+            @pl.when(chosen == k)
+            def _(k=k):
+                for s in range(slab_count):
+                    out_refs[s][0] = source_refs[k][0, lax.bitwise_xor(slab, s)]
 
     return pl.pallas_call(
         kernel,
         name="keep",
-        in_specs=[pl.BlockSpec(memory_space=pltpu.SMEM)] * 2
-        + [pl.BlockSpec(memory_space=pl.ANY)] * group_count,
-        out_specs=[pl.BlockSpec(memory_space=pl.ANY)] * slab_count,
+        grid_spec=pltpu.PrefetchScalarGridSpec(
+            num_scalar_prefetch=3,
+            grid=(survivor_count,),
+            in_specs=[
+                pl.BlockSpec(
+                    (1, slab_count, rows, points),
+                    lambda d, place_ref, offset_ref, shown_ref, k=k: (
+                        shown_ref[k * survivor_count + d],
+                        0,
+                        0,
+                        0,
+                    ),
+                )
+                for k in range(group_count)
+            ],
+            out_specs=[pl.BlockSpec((1, rows, points), lambda d, *_: (d, 0, 0))] * slab_count,
+        ),
         out_shape=[jax.ShapeDtypeStruct((survivor_count, rows, points), jnp.bfloat16)] * slab_count,
-        scratch_shapes=[pltpu.SemaphoreType.DMA((slab_count,))],
         compiler_params=params(),
         cost_estimate=cost(0, 4 * survivor_count * slab_count * rows * points),
-    )(place, survivors, *sources)
+    )(place, offset, shown, *sources)
 
 
 def spread(place, slot_source, sources, member_here, group_count):
     slab_count = len(sources)
     _, rows, points = sources[0].shape
 
+    def source_at(k, t, place_ref, slot_ref):
+        return slot_ref[lax.bitwise_xor(place_ref[0], k) * member_here + t], 0, 0
+
     def kernel(place_ref, slot_ref, *refs):
         source_refs = refs[:slab_count]
-        out_refs = refs[slab_count : slab_count + group_count]
-        sems = refs[-1]
-        group, slab = place_ref[0], place_ref[1]
+        out_refs = refs[slab_count:]
+        slab = place_ref[1]
         for k in range(group_count):
-            for t in range(member_here):
-                origin = slot_ref[lax.bitwise_xor(group, k) * member_here + t]
+
+            @pl.when(pl.program_id(0) == k)
+            def _(k=k):
                 for s in range(slab_count):
-                    pltpu.make_async_copy(
-                        source_refs[s].at[origin],
-                        out_refs[k].at[t, lax.bitwise_xor(slab, s)],
-                        sems.at[k],
-                    ).start()
-        for k in range(group_count):
-            pltpu.make_async_copy(out_refs[k], out_refs[k], sems.at[k]).wait()
+                    out_refs[k][0, lax.bitwise_xor(slab, s)] = source_refs[s][0]
 
     return pl.pallas_call(
         kernel,
         name="spread",
-        in_specs=[pl.BlockSpec(memory_space=pltpu.SMEM)] * 2
-        + [pl.BlockSpec(memory_space=pl.ANY)] * slab_count,
-        out_specs=[pl.BlockSpec(memory_space=pl.ANY)] * group_count,
+        grid_spec=pltpu.PrefetchScalarGridSpec(
+            num_scalar_prefetch=2,
+            grid=(group_count, member_here),
+            in_specs=[pl.BlockSpec((1, rows, points), source_at)] * slab_count,
+            out_specs=[
+                pl.BlockSpec(
+                    (1, slab_count, rows, points),
+                    lambda k, t, *_, own=own: (
+                        jnp.where(k == own, t, jnp.where(k < own, 0, member_here - 1)),
+                        0,
+                        0,
+                        0,
+                    ),
+                )
+                for own in range(group_count)
+            ],
+        ),
         out_shape=[
             jax.ShapeDtypeStruct((member_here, slab_count, rows, points), jnp.bfloat16)
         ]
         * group_count,
-        scratch_shapes=[pltpu.SemaphoreType.DMA((group_count,))],
         compiler_params=params(),
         cost_estimate=cost(0, 4 * group_count * member_here * slab_count * rows * points),
     )(place, slot_source, *sources)

time: 1780 us -> 1110 us (0.62)
  Pallas kernels: 1340 us -> 320 us
  waiting for transfers between devices: 332 us -> 668 us
    pallas_call x6, Pallas kernels: 1090 us -> 66.9 us  [the longest x3 36.8 us: spread(): pl.pallas_call(kernel, name='spread', grid_spec=pltpu.PrefetchScalarGridS...]
    ppermute x60, waiting for transfers between devices: 332 us -> 668 us  [exchange(): out.append(lax.ppermute(pieces[s], axis, [(i, i ^ s) for i in range(size)]))]
  transfers between devices with their start and end apart: 60 -> 60, of which waited for: 14 -> 28; matrix products, arithmetic and copies ran while one was open for 0% -> 1% of each run, Pallas kernels for 74% -> 26%
where the time goes in v3:
time: 1110 us; the launch traced here: 1090 us
  waiting for transfers between devices  668 us (60%)
  Pallas kernels  320 us (29%)
  starting transfers between devices  90 us (8%)
  local copies, waits for them, and re-layouts  12.1 us (1%)
    ppermute x60, waiting for transfers between devices, exchange(): out.append(lax.ppermute(pieces[s], axis, [(i, i ^ s) for i in range(size)]))  668 us
    pallas_call x3, Pallas kernels, spectral_filter(): pl.pallas_call(kernel, name='spectral', grid=(wave_here,), in_specs=[pl.B...  155 us
    ppermute x60, starting transfers between devices, exchange(): out.append(lax.ppermute(pieces[s], axis, [(i, i ^ s) for i in range(size)]))  90 us
    pallas_call x3, Pallas kernels, synthesise(): pl.pallas_call(kernel, name='synthesise', grid=(member_here,), in_specs=s...  55.1 us
    pallas_call x3, Pallas kernels, analyse(): pl.pallas_call(kernel, name='analyse', grid=(member_here,), in_specs=[pl....  42.7 us
    pallas_call x3, Pallas kernels, spread(): pl.pallas_call(kernel, name='spread', grid_spec=pltpu.PrefetchScalarGridS...  36.8 us
    pallas_call x3, Pallas kernels, keep(): pl.pallas_call(kernel, name='keep', grid_spec=pltpu.PrefetchScalarGridSpe...  30.2 us
  transfers between devices with their start and end apart: 60, of which 28 were waited for; matrix products, arithmetic and copies ran while one was open for 1% of the time, Pallas kernels for 26%

profile of v3, /device:TPU:17, one launch (start us, length us, event | category | flops | bytes accessed | tf_op | source)
XLA Modules:
  0.0 1094.9 jit_solution(7465140685801797369)
XLA Ops:
  0.0 2.1 constant_dynamic-slice_fusion.3
  2.1 1.9 pad_maximum_fusion.table_ref
  4.0 14.4 %analyse.5 = (bf16[4,320,640]{2,1,0:T(8,128)(2,1)}, bf16[4,320,640]{2,1,0:T(8,128)(2,1)}, bf16[4,320,640]{2,1,0:T(8,128)(2,1)}, bf16[4,320,640]{2,1,0:T(8,128)(2,1)}) custom-call(bf16[4,320,1280]{2,1,0:T(8,128)(2,1)} %pad_maximum_fusion.table_ref, bf16[4,3,640,1280]{3,2,1,0:T(8,128)(2,1)} %bitcast.98), custom_call_target="tpu_custom_call" | custom-call | flops 8388608000 | bytes 13107200 | tf_op jit(solution)/shard_map/analyse/pallas_call | solution.py:79
  20.7 14.2 %analyse.4 = (bf16[4,320,640]{2,1,0:T(8,128)(2,1)}, bf16[4,320,640]{2,1,0:T(8,128)(2,1)}, bf16[4,320,640]{2,1,0:T(8,128)(2,1)}, bf16[4,320,640]{2,1,0:T(8,128)(2,1)}) custom-call(bf16[4,320,1280]{2,1,0:T(8,128)(2,1)} %pad_maximum_fusion.table_ref, bf16[4,3,640,1280]{3,2,1,0:T(8,128)(2,1)} %bitcast.99), custom_call_target="tpu_custom_call" | custom-call | flops 8388608000 | bytes 13107200 | tf_op jit(solution)/shard_map/analyse/pallas_call | solution.py:79
  36.3 14.2 %analyse.3 = (bf16[4,320,640]{2,1,0:T(8,128)(2,1)}, bf16[4,320,640]{2,1,0:T(8,128)(2,1)}, bf16[4,320,640]{2,1,0:T(8,128)(2,1)}, bf16[4,320,640]{2,1,0:T(8,128)(2,1)}) custom-call(bf16[4,320,1280]{2,1,0:T(8,128)(2,1)} %pad_maximum_fusion.table_ref, bf16[4,3,640,1280]{3,2,1,0:T(8,128)(2,1)} %bitcast.100), custom_call_target="tpu_custom_call" | custom-call | flops 8388608000 | bytes 13107200 | tf_op jit(solution)/shard_map/analyse/pallas_call | solution.py:79
  51.3 5.4 collective-permute-done.41
  59.1 33.3 %collective-permute-done.42 = bf16[4,320,640]{2,1,0:T(8,128)(2,1)} collective-permute-done((bf16[4,320,640]{2,1,0:T(8,128)(2,1)}, bf16[4,320,640]{2,1,0:T(8,128)(2,1)}, u32[]{:S(2)}, u32[]{:S(2)}) %collective-permute-start.42) | collective-permute-done | bytes 1638432 | tf_op jit(solution)/shard_map/ppermute | solution.py:54
  96.9 10.0 keep.5
  106.9 20.1 %collective-permute-done.21 = bf16[4,320,640]{2,1,0:T(8,128)(2,1)} collective-permute-done((bf16[4,320,640]{2,1,0:T(8,128)(2,1)}, bf16[4,320,640]{2,1,0:T(8,128)(2,1)}, u32[]{:S(2)}, u32[]{:S(2)}) %collective-permute-start.21) | collective-permute-done | bytes 1638432 | tf_op jit(solution)/shard_map/ppermute | solution.py:54
  128.2 34.4 %collective-permute-done.22 = bf16[4,320,640]{2,1,0:T(8,128)(2,1)} collective-permute-done((bf16[4,320,640]{2,1,0:T(8,128)(2,1)}, bf16[4,320,640]{2,1,0:T(8,128)(2,1)}, u32[]{:S(2)}, u32[]{:S(2)}) %collective-permute-start.22) | collective-permute-done | bytes 1638432 | tf_op jit(solution)/shard_map/ppermute | solution.py:54
  162.7 1.3 collective-permute-start.44
  165.1 32.1 %collective-permute-done.1 = bf16[4,320,640]{2,1,0:T(8,128)(2,1)S(1)} collective-permute-done((bf16[4,320,640]{2,1,0:T(8,128)(2,1)}, bf16[4,320,640]{2,1,0:T(8,128)(2,1)S(1)}, u32[]{:S(2)}, u32[]{:S(2)}) %collective-permute-start.1) | collective-permute-done | bytes 1638432 | tf_op jit(solution)/shard_map/ppermute | solution.py:54
  197.1 35.3 %collective-permute-done.2 = bf16[4,320,640]{2,1,0:T(8,128)(2,1)} collective-permute-done((bf16[4,320,640]{2,1,0:T(8,128)(2,1)}, bf16[4,320,640]{2,1,0:T(8,128)(2,1)}, u32[]{:S(2)}, u32[]{:S(2)}) %collective-permute-start.2) | collective-permute-done | bytes 1638432 | tf_op jit(solution)/shard_map/ppermute | solution.py:54
  233.4 10.0 keep.4
  243.5 2.5 collective-permute-start.48
  247.2 2.1 collective-permute-start.24
  249.3 41.4 %collective-permute-done.47 = bf16[13,40,640]{2,1,0:T(8,128)(2,1)} collective-permute-done((bf16[13,40,640]{2,1,0:T(8,128)(2,1)}, bf16[13,40,640]{2,1,0:T(8,128)(2,1)}, u32[]{:S(2)}, u32[]{:S(2)}) %collective-permute-start.47) | collective-permute-done | bytes 665632 | tf_op jit(solution)/shard_map/ppermute | solution.py:54
  290.7 5.7 collective-permute-start.25
  296.4 10.2 keep.3
  306.6 1.9 collective-permute-done.48
  309.4 29.6 %collective-permute-done.49 = bf16[13,40,640]{2,1,0:T(8,128)(2,1)S(1)} collective-permute-done((bf16[13,40,640]{2,1,0:T(8,128)(2,1)}, bf16[13,40,640]{2,1,0:T(8,128)(2,1)S(1)}, u32[]{:S(2)}, u32[]{:S(2)}) %collective-permute-start.49) | collective-permute-done | bytes 665632 | tf_op jit(solution)/shard_map/ppermute | solution.py:54
  340.0 2.2 collective-permute-start.29
  344.8 47.7 %collective-permute-done.26 = bf16[13,40,640]{2,1,0:T(8,128)(2,1)S(1)} collective-permute-done((bf16[13,40,640]{2,1,0:T(8,128)(2,1)}, bf16[13,40,640]{2,1,0:T(8,128)(2,1)S(1)}, u32[]{:S(2)}, u32[]{:S(2)}) %collective-permute-start.26) | collective-permute-done | bytes 665632 | tf_op jit(solution)/shard_map/ppermute | solution.py:54
  392.5 4.6 collective-permute-start.4
  397.1 9.7 collective-permute-done.27
  406.8 5.5 collective-permute-start.5
  412.3 12.3 %collective-permute-done.28 = bf16[13,40,640]{2,1,0:T(8,128)(2,1)} collective-permute-done((bf16[13,40,640]{2,1,0:T(8,128)(2,1)}, bf16[13,40,640]{2,1,0:T(8,128)(2,1)}, u32[]{:S(2)}, u32[]{:S(2)}) %collective-permute-start.28) | collective-permute-done | bytes 665632 | tf_op jit(solution)/shard_map/ppermute | solution.py:54
  424.6 30.2 %collective-permute-done.29 = bf16[13,40,640]{2,1,0:T(8,128)(2,1)} collective-permute-done((bf16[13,40,640]{2,1,0:T(8,128)(2,1)}, bf16[13,40,640]{2,1,0:T(8,128)(2,1)}, u32[]{:S(2)}, u32[]{:S(2)}) %collective-permute-start.29) | collective-permute-done | bytes 665632 | tf_op jit(solution)/shard_map/ppermute | solution.py:54
  454.9 51.9 %spectral.5 = (bf16[520,640]{1,0:T(8,128)(2,1)}, bf16[520,640]{1,0:T(8,128)(2,1)}, bf16[520,640]{1,0:T(8,128)(2,1)}, bf16[520,640]{1,0:T(8,128)(2,1)}, bf16[520,...) custom-call(s32[2]{0:T(128)} %pad_add_fusion.place_ref, ...), custom_call_target="tpu_custom_call" | custom-call | flops 20000000000 | bytes 18841600 | tf_op jit(solution)/shard_map/spectral/pallas_call | solution.py:314
  506.8 2.2 collective-permute-start.9
  510.3 2.7 collective-permute-start.51
  515.6 24.6 %collective-permute-done.8 = bf16[13,40,640]{2,1,0:T(8,128)(2,1)} collective-permute-done((bf16[13,40,640]{2,1,0:T(8,128)(2,1)}, bf16[13,40,640]{2,1,0:T(8,128)(2,1)}, u32[]{:S(2)}, u32[]{:S(2)}) %collective-permute-start.8) | collective-permute-done | bytes 665632 | tf_op jit(solution)/shard_map/ppermute | solution.py:54
  540.2 27.4 %collective-permute-done.9 = bf16[13,40,640]{2,1,0:T(8,128)(2,1)} collective-permute-done((bf16[13,40,640]{2,1,0:T(8,128)(2,1)}, bf16[13,40,640]{2,1,0:T(8,128)(2,1)}, u32[]{:S(2)}, u32[]{:S(2)}) %collective-permute-start.9) | collective-permute-done | bytes 665632 | tf_op jit(solution)/shard_map/ppermute | solution.py:54
  567.7 2.1 collective-permute-start.56
  569.8 51.4 %spectral.4 = (bf16[520,640]{1,0:T(8,128)(2,1)}, bf16[520,640]{1,0:T(8,128)(2,1)}, bf16[520,640]{1,0:T(8,128)(2,1)}, bf16[520,640]{1,0:T(8,128)(2,1)}, bf16[520,...) custom-call(s32[2]{0:T(128)} %pad_add_fusion.place_ref, ...), custom_call_target="tpu_custom_call" | custom-call | flops 20000000000 | bytes 18841600 | tf_op jit(solution)/shard_map/spectral/pallas_call | solution.py:314
  621.9 10.4 collective-permute-done.53.refs_4_
  632.3 6.7 collective-permute-start.31
  639.0 7.6 collective-permute-done.54.refs_5_
  646.6 7.6 collective-permute-start.32
  654.2 12.3 %collective-permute-done.55.refs_6_ = bf16[13,40,640]{2,1,0:T(8,128)(2,1)} collective-permute-done((bf16[13,40,640]{2,1,0:T(8,128)(2,1)}, bf16[13,40,640]{2,1,0:T(8,128)(2,1)}, u32[]{:S(2)}, u32[]{:S(2)}) %collective-permute-start.55) | collective-permute-done | bytes 665632 | tf_op jit(solution)/shard_map/ppermute | solution.py:54
  666.5 30.8 %collective-permute-done.56.refs_7_ = bf16[13,40,640]{2,1,0:T(8,128)(2,1)} collective-permute-done((bf16[13,40,640]{2,1,0:T(8,128)(2,1)}, bf16[13,40,640]{2,1,0:T(8,128)(2,1)}, u32[]{:S(2)}, u32[]{:S(2)}) %collective-permute-start.56) | collective-permute-done | bytes 665632 | tf_op jit(solution)/shard_map/ppermute | solution.py:54
  697.3 51.6 %spectral.3 = (bf16[520,640]{1,0:T(8,128)(2,1)}, bf16[520,640]{1,0:T(8,128)(2,1)}, bf16[520,640]{1,0:T(8,128)(2,1)}, bf16[520,640]{1,0:T(8,128)(2,1)}, bf16[520,...) custom-call(s32[2]{0:T(128)} %pad_add_fusion.place_ref, ...), custom_call_target="tpu_custom_call" | custom-call | flops 20000000000 | bytes 18841600 | tf_op jit(solution)/shard_map/spectral/pallas_call | solution.py:314
  749.0 2.1 collective-permute-start.36
  751.6 2.8 collective-permute-start.11
  754.4 12.2 %spread.5 = (bf16[4,8,40,640]{3,2,1,0:T(8,128)(2,1)}, bf16[4,8,40,640]{3,2,1,0:T(8,128)(2,1)}, bf16[4,8,40,640]{3,2,1,0:T(8,128)(2,1)}, bf16[4,8,40,640]{3,2,1,0:T(8,128)(2,1)}) custom-call(s32[2]{0:T(128)} %pad_add_fusion.place_ref, s32[16]{0:T(128)} %get-tuple-element.150.slot_ref, bf16[13,40,640]{2,1,0:T(8,128)(2,1)} %bitcast.94, ...), custom_call_target="tpu_custom_call" | custom-call | bytes 13107200 | tf_op jit(solution)/shard_map/spread/pallas_call | solution.py:164
  766.7 1.6 collective-permute-start.57
  768.3 25.4 %collective-permute-done.35.refs_6_ = bf16[13,40,640]{2,1,0:T(8,128)(2,1)S(1)} collective-permute-done((bf16[13,40,640]{2,1,0:T(8,128)(2,1)}, bf16[13,40,640]{2,1,0:T(8,128)(2,1)S(1)}, u32[]{:S(2)}, u32[]{:S(2)}) %collective-permute-start.35) | collective-permute-done | bytes 665632 | tf_op jit(solution)/shard_map/ppermute | solution.py:54
  794.5 24.0 %collective-permute-done.36.refs_7_ = bf16[13,40,640]{2,1,0:T(8,128)(2,1)} collective-permute-done((bf16[13,40,640]{2,1,0:T(8,128)(2,1)}, bf16[13,40,640]{2,1,0:T(8,128)(2,1)}, u32[]{:S(2)}, u32[]{:S(2)}) %collective-permute-start.36) | collective-permute-done | bytes 665632 | tf_op jit(solution)/shard_map/ppermute | solution.py:54
  818.6 2.3 collective-permute-start.14
  821.2 12.3 %spread.4 = (bf16[4,8,40,640]{3,2,1,0:T(8,128)(2,1)}, bf16[4,8,40,640]{3,2,1,0:T(8,128)(2,1)}, bf16[4,8,40,640]{3,2,1,0:T(8,128)(2,1)}, bf16[4,8,40,640]{3,2,1,0:T(8,128)(2,1)}) custom-call(s32[2]{0:T(128)} %pad_add_fusion.place_ref, s32[16]{0:T(128)} %get-tuple-element.150.slot_ref, bf16[13,40,640]{2,1,0:T(8,128)(2,1)} %bitcast.96, ...), custom_call_target="tpu_custom_call" | custom-call | bytes 13107200 | tf_op jit(solution)/shard_map/spread/pallas_call | solution.py:164
  834.7 39.6 %collective-permute-done.13.refs_4_ = bf16[13,40,640]{2,1,0:T(8,128)(2,1)S(1)} collective-permute-done((bf16[13,40,640]{2,1,0:T(8,128)(2,1)}, bf16[13,40,640]{2,1,0:T(8,128)(2,1)S(1)}, u32[]{:S(2)}, u32[]{:S(2)}) %collective-permute-start.13) | collective-permute-done | bytes 665632 | tf_op jit(solution)/shard_map/ppermute | solution.py:54
  874.3 5.8 collective-permute-start.59
  880.1 8.5 collective-permute-done.14.refs_5_
  889.4 4.7 collective-permute-start.37
  894.1 24.0 %collective-permute-done.15.refs_6_ = bf16[13,40,640]{2,1,0:T(8,128)(2,1)} collective-permute-done((bf16[13,40,640]{2,1,0:T(8,128)(2,1)}, bf16[13,40,640]{2,1,0:T(8,128)(2,1)}, u32[]{:S(2)}, u32[]{:S(2)}) %collective-permute-start.15) | collective-permute-done | bytes 665632 | tf_op jit(solution)/shard_map/ppermute | solution.py:54
  919.2 13.8 %collective-permute-done.16.refs_7_ = bf16[13,40,640]{2,1,0:T(8,128)(2,1)S(1)} collective-permute-done((bf16[13,40,640]{2,1,0:T(8,128)(2,1)}, bf16[13,40,640]{2,1,0:T(8,128)(2,1)S(1)}, u32[]{:S(2)}, u32[]{:S(2)}) %collective-permute-start.16) | collective-permute-done | bytes 665632 | tf_op jit(solution)/shard_map/ppermute | solution.py:54
  934.3 3.9 collective-permute-start.39
  938.2 12.3 %spread.3 = (bf16[4,8,40,640]{3,2,1,0:T(8,128)(2,1)}, bf16[4,8,40,640]{3,2,1,0:T(8,128)(2,1)}, bf16[4,8,40,640]{3,2,1,0:T(8,128)(2,1)}, bf16[4,8,40,640]{3,2,1,0:T(8,128)(2,1)}) custom-call(s32[2]{0:T(128)} %pad_add_fusion.place_ref, s32[16]{0:T(128)} %get-tuple-element.150.slot_ref, bf16[13,40,640]{2,1,0:T(8,128)(2,1)} %bitcast.95, ...), custom_call_target="tpu_custom_call" | custom-call | bytes 13107200 | tf_op jit(solution)/shard_map/spread/pallas_call | solution.py:164
  952.7 18.5 %synthesise.3.refs_4_ = bf16[4,3,640,1280]{3,2,1,0:T(8,128)(2,1)} custom-call(s32[2]{0:T(128)} %pad_add_fusion.place_ref, bf16[4,320,1280]{2,1,0:T(8,128)(2,1)} %constant.85.table_ref, bf16[4,320,640]{2,1,0:T(8,128)(2,1)} %bitcast.101, bf16[4,320,640]{2,1,0:T(8,128)(2,1)} %bitcast.76.refs_1_, bf16[4,320,640]{2,1,0:T(8,128)(2,1)} %bitcast.77.refs_2_, ...), custom_call_target="tpu_custom_call" | custom-call | flops 8388608000 | bytes 13107200 | tf_op jit(solution)/shard_map/synthesise/pallas_call | solution.py:214
  971.2 38.8 %collective-permute-done.39 = bf16[4,8,40,640]{3,2,1,0:T(8,128)(2,1)} collective-permute-done((bf16[4,8,40,640]{3,2,1,0:T(8,128)(2,1)}, bf16[4,8,40,640]{3,2,1,0:T(8,128)(2,1)}, u32[]{:S(2)}, u32[]{:S(2)}) %collective-permute-start.39) | collective-permute-done | bytes 1638432 | tf_op jit(solution)/shard_map/ppermute | solution.py:54
  1010.0 18.3 %synthesise.4.refs_4_ = bf16[4,3,640,1280]{3,2,1,0:T(8,128)(2,1)} custom-call(s32[2]{0:T(128)} %pad_add_fusion.place_ref, bf16[4,320,1280]{2,1,0:T(8,128)(2,1)} %constant.85.table_ref, bf16[4,320,640]{2,1,0:T(8,128)(2,1)} %bitcast.90, bf16[4,320,640]{2,1,0:T(8,128)(2,1)} %bitcast.91, bf16[4,320,640]{2,1,0:T(8,128)(2,1)} %bitcast.93, ...), custom_call_target="tpu_custom_call", output_to_operand_aliasing={{}: (6, {})} | custom-call | flops 8388608000 | bytes 13107200 | tf_op jit(solution)/shard_map/synthesise/pallas_call | solution.py:214
  1028.3 9.0 collective-permute-done.18
  1037.3 38.9 %collective-permute-done.19 = bf16[4,8,40,640]{3,2,1,0:T(8,128)(2,1)} collective-permute-done((bf16[4,8,40,640]{3,2,1,0:T(8,128)(2,1)}, bf16[4,8,40,640]{3,2,1,0:T(8,128)(2,1)}, u32[]{:S(2)}, u32[]{:S(2)}) %collective-permute-start.19) | collective-permute-done | bytes 1638432 | tf_op jit(solution)/shard_map/ppermute | solution.py:54
  1076.2 18.3 %synthesise.5 = bf16[4,3,640,1280]{3,2,1,0:T(8,128)(2,1)} custom-call(s32[2]{0:T(128)} %pad_add_fusion.place_ref, bf16[4,320,1280]{2,1,0:T(8,128)(2,1)} %constant.85.table_ref, bf16[4,320,640]{2,1,0:T(8,128)(2,1)} %bitcast.92, bf16[4,320,640]{2,1,0:T(8,128)(2,1)} %bitcast.26.refs_1_, ...), custom_call_target="tpu_custom_call", output_to_operand_aliasing={{}: (6, {})} | custom-call | flops 8388608000 | bytes 13107200 | tf_op jit(solution)/shard_map/synthesise/pallas_call | solution.py:214
  (165 shorter events, 33.7 us)
Async XLA Ops:
  18.4 32.1 %collective-permute-start.40 = (bf16[4,320,640]{2,1,0:T(8,128)(2,1)}, bf16[4,320,640]{2,1,0:T(8,128)(2,1)S(1)}, u32[]{:S(2)}, u32[]{:S(2)}) collective-permute-start(bf16[4,320,640]{2,1,0:T(8,128)(2,1)} %get-tuple-element.126), channel_id=1, source_target_pairs={{0,8},{8,0},{16,24},{24,16},{1,9},{9,1},{17,25},{25,17},{2,10},{10... | collective-permute-start | bytes 4915208 | tf_op jit(solution)/shard_map/ppermute | solution.py:54
  19.1 37.6 %collective-permute-start.41 = (bf16[4,320,640]{2,1,0:T(8,128)(2,1)}, bf16[4,320,640]{2,1,0:T(8,128)(2,1)S(1)}, u32[]{:S(2)}, u32[]{:S(2)}) collective-permute-start(bf16[4,320,640]{2,1,0:T(8,128)(2,1)} %get-tuple-element.127), channel_id=1, source_target_pairs={{0,16},{8,24},{16,0},{24,8},{1,17},{9,25},{17,1},{25,9},{2,18},{10... | collective-permute-start | bytes 4915208 | tf_op jit(solution)/shard_map/ppermute | solution.py:54
  20.3 72.1 %collective-permute-start.42 = (bf16[4,320,640]{2,1,0:T(8,128)(2,1)}, bf16[4,320,640]{2,1,0:T(8,128)(2,1)}, u32[]{:S(2)}, u32[]{:S(2)}) collective-permute-start(bf16[4,320,640]{2,1,0:T(8,128)(2,1)} %get-tuple-element.128), channel_id=1, source_target_pairs={{0,24},{8,16},{16,8},{24,0},{1,25},{9,17},{17,9},{25,1},{2,26},{10... | collective-permute-start | bytes 4915208 | tf_op jit(solution)/shard_map/ppermute | solution.py:54
  34.9 58.8 %collective-permute-start.20 = (bf16[4,320,640]{2,1,0:T(8,128)(2,1)}, bf16[4,320,640]{2,1,0:T(8,128)(2,1)}, u32[]{:S(2)}, u32[]{:S(2)}) collective-permute-start(bf16[4,320,640]{2,1,0:T(8,128)(2,1)} %get-tuple-element.102), channel_id=1, source_target_pairs={{0,8},{8,0},{16,24},{24,16},{1,9},{9,1},{17,25},{25,17},{2,10},{10... | collective-permute-start | bytes 4915208 | tf_op jit(solution)/shard_map/ppermute | solution.py:54
  35.1 91.9 %collective-permute-start.21 = (bf16[4,320,640]{2,1,0:T(8,128)(2,1)}, bf16[4,320,640]{2,1,0:T(8,128)(2,1)}, u32[]{:S(2)}, u32[]{:S(2)}) collective-permute-start(bf16[4,320,640]{2,1,0:T(8,128)(2,1)} %get-tuple-element.103), channel_id=1, source_target_pairs={{0,16},{8,24},{16,0},{24,8},{1,17},{9,25},{17,1},{25,9},{2,18},{10... | collective-permute-start | bytes 4915208 | tf_op jit(solution)/shard_map/ppermute | solution.py:54
  50.5 112.1 %collective-permute-start.22 = (bf16[4,320,640]{2,1,0:T(8,128)(2,1)}, bf16[4,320,640]{2,1,0:T(8,128)(2,1)}, u32[]{:S(2)}, u32[]{:S(2)}) collective-permute-start(bf16[4,320,640]{2,1,0:T(8,128)(2,1)} %get-tuple-element.104), channel_id=1, source_target_pairs={{0,24},{8,16},{16,8},{24,0},{1,25},{9,17},{17,9},{25,1},{2,26},{10... | collective-permute-start | bytes 4915208 | tf_op jit(solution)/shard_map/ppermute | solution.py:54
  57.9 106.1 %collective-permute-start = (bf16[4,320,640]{2,1,0:T(8,128)(2,1)}, bf16[4,320,640]{2,1,0:T(8,128)(2,1)S(1)}, u32[]{:S(2)}, u32[]{:S(2)}) collective-permute-start(bf16[4,320,640]{2,1,0:T(8,128)(2,1)} %get-tuple-element.78), channel_id=1, source_target_pairs={{0,8},{8,0},{16,24},{24,16},{1,9},{9,1},{17,25},{25,17},{2,10},{10... | collective-permute-start | bytes 4915208 | tf_op jit(solution)/shard_map/ppermute | solution.py:54
  92.4 104.7 %collective-permute-start.1 = (bf16[4,320,640]{2,1,0:T(8,128)(2,1)}, bf16[4,320,640]{2,1,0:T(8,128)(2,1)S(1)}, u32[]{:S(2)}, u32[]{:S(2)}) collective-permute-start(bf16[4,320,640]{2,1,0:T(8,128)(2,1)} %get-tuple-element.79), channel_id=1, source_target_pairs={{0,16},{8,24},{16,0},{24,8},{1,17},{9,25},{17,1},{25,9},{2,18},{10... | collective-permute-start | bytes 4915208 | tf_op jit(solution)/shard_map/ppermute | solution.py:54
  93.7 138.8 %collective-permute-start.2 = (bf16[4,320,640]{2,1,0:T(8,128)(2,1)}, bf16[4,320,640]{2,1,0:T(8,128)(2,1)}, u32[]{:S(2)}, u32[]{:S(2)}) collective-permute-start(bf16[4,320,640]{2,1,0:T(8,128)(2,1)} %get-tuple-element.80), channel_id=1, source_target_pairs={{0,24},{8,16},{16,8},{24,0},{1,25},{9,17},{17,9},{25,1},{2,26},{10... | collective-permute-start | bytes 4915208 | tf_op jit(solution)/shard_map/ppermute | solution.py:54
  127.0 116.5 %collective-permute-start.43 = (bf16[13,40,640]{2,1,0:T(8,128)(2,1)}, bf16[13,40,640]{2,1,0:T(8,128)(2,1)}, u32[]{:S(2)}, u32[]{:S(2)}) collective-permute-start(bf16[13,40,640]{2,1,0:T(8,128)(2,1)} %get-tuple-element.130), channel_id=1, source_target_pairs={{0,1},{1,0},{2,3},{3,2},{4,5},{5,4},{6,7},{7,6},{8,9},{9,8},{10,11... | collective-permute-start | bytes 1996808 | tf_op jit(solution)/shard_map/ppermute | solution.py:54
  162.7 83.3 %collective-permute-start.44 = (bf16[13,40,640]{2,1,0:T(8,128)(2,1)}, bf16[13,40,640]{2,1,0:T(8,128)(2,1)}, u32[]{:S(2)}, u32[]{:S(2)}) collective-permute-start(bf16[13,40,640]{2,1,0:T(8,128)(2,1)} %get-tuple-element.131), channel_id=1, source_target_pairs={{0,2},{1,3},{2,0},{3,1},{4,6},{5,7},{6,4},{7,5},{8,10},{9,11},{10,... | collective-permute-start | bytes 1996808 | tf_op jit(solution)/shard_map/ppermute | solution.py:54
  164.0 82.1 %collective-permute-start.45 = (bf16[13,40,640]{2,1,0:T(8,128)(2,1)}, bf16[13,40,640]{2,1,0:T(8,128)(2,1)}, u32[]{:S(2)}, u32[]{:S(2)}) collective-permute-start(bf16[13,40,640]{2,1,0:T(8,128)(2,1)} %get-tuple-element.132), channel_id=1, source_target_pairs={{0,3},{1,2},{2,1},{3,0},{4,7},{5,6},{6,5},{7,4},{8,11},{9,10},{10,... | collective-permute-start | bytes 1996808 | tf_op jit(solution)/shard_map/ppermute | solution.py:54
  197.1 50.1 %collective-permute-start.46 = (bf16[13,40,640]{2,1,0:T(8,128)(2,1)}, bf16[13,40,640]{2,1,0:T(8,128)(2,1)}, u32[]{:S(2)}, u32[]{:S(2)}) collective-permute-start(bf16[13,40,640]{2,1,0:T(8,128)(2,1)} %get-tuple-element.133), channel_id=1, source_target_pairs={{0,4},{1,5},{2,6},{3,7},{4,0},{5,1},{6,2},{7,3},{8,12},{9,13},{10,... | collective-permute-start | bytes 1996808 | tf_op jit(solution)/shard_map/ppermute | solution.py:54
  232.5 58.2 %collective-permute-start.47 = (bf16[13,40,640]{2,1,0:T(8,128)(2,1)}, bf16[13,40,640]{2,1,0:T(8,128)(2,1)}, u32[]{:S(2)}, u32[]{:S(2)}) collective-permute-start(bf16[13,40,640]{2,1,0:T(8,128)(2,1)} %get-tuple-element.134), channel_id=1, source_target_pairs={{0,5},{1,4},{2,7},{3,6},{4,1},{5,0},{6,3},{7,2},{8,13},{9,12},{10,... | collective-permute-start | bytes 1996808 | tf_op jit(solution)/shard_map/ppermute | solution.py:54
  243.5 65.0 %collective-permute-start.48 = (bf16[13,40,640]{2,1,0:T(8,128)(2,1)}, bf16[13,40,640]{2,1,0:T(8,128)(2,1)S(1)}, u32[]{:S(2)}, u32[]{:S(2)}) collective-permute-start(bf16[13,40,640]{2,1,0:T(8,128)(2,1)} %get-tuple-element.135), channel_id=1, source_target_pairs={{0,6},{1,7},{2,4},{3,5},{4,2},{5,3},{6,0},{7,1},{8,14},{9,15},{10,... | collective-permute-start | bytes 1996808 | tf_op jit(solution)/shard_map/ppermute | solution.py:54
  246.0 93.0 %collective-permute-start.49 = (bf16[13,40,640]{2,1,0:T(8,128)(2,1)}, bf16[13,40,640]{2,1,0:T(8,128)(2,1)S(1)}, u32[]{:S(2)}, u32[]{:S(2)}) collective-permute-start(bf16[13,40,640]{2,1,0:T(8,128)(2,1)} %get-tuple-element.136), channel_id=1, source_target_pairs={{0,7},{1,6},{2,5},{3,4},{4,3},{5,2},{6,1},{7,0},{8,15},{9,14},{10,... | collective-permute-start | bytes 1996808 | tf_op jit(solution)/shard_map/ppermute | solution.py:54
  246.0 93.9 %collective-permute-start.23 = (bf16[13,40,640]{2,1,0:T(8,128)(2,1)}, bf16[13,40,640]{2,1,0:T(8,128)(2,1)S(1)}, u32[]{:S(2)}, u32[]{:S(2)}) collective-permute-start(bf16[13,40,640]{2,1,0:T(8,128)(2,1)} %get-tuple-element.106), channel_id=1, source_target_pairs={{0,1},{1,0},{2,3},{3,2},{4,5},{5,4},{6,7},{7,6},{8,9},{9,8},{10,11... | collective-permute-start | bytes 1996808 | tf_op jit(solution)/shard_map/ppermute | solution.py:54
  247.2 92.7 %collective-permute-start.24 = (bf16[13,40,640]{2,1,0:T(8,128)(2,1)}, bf16[13,40,640]{2,1,0:T(8,128)(2,1)S(1)}, u32[]{:S(2)}, u32[]{:S(2)}) collective-permute-start(bf16[13,40,640]{2,1,0:T(8,128)(2,1)} %get-tuple-element.107), channel_id=1, source_target_pairs={{0,2},{1,3},{2,0},{3,1},{4,6},{5,7},{6,4},{7,5},{8,10},{9,11},{10,... | collective-permute-start | bytes 1996808 | tf_op jit(solution)/shard_map/ppermute | solution.py:54
  290.7 51.5 %collective-permute-start.25 = (bf16[13,40,640]{2,1,0:T(8,128)(2,1)}, bf16[13,40,640]{2,1,0:T(8,128)(2,1)S(1)}, u32[]{:S(2)}, u32[]{:S(2)}) collective-permute-start(bf16[13,40,640]{2,1,0:T(8,128)(2,1)} %get-tuple-element.108), channel_id=1, source_target_pairs={{0,3},{1,2},{2,1},{3,0},{4,7},{5,6},{6,5},{7,4},{8,11},{9,10},{10,... | collective-permute-start | bytes 1996808 | tf_op jit(solution)/shard_map/ppermute | solution.py:54
  309.4 83.1 %collective-permute-start.26 = (bf16[13,40,640]{2,1,0:T(8,128)(2,1)}, bf16[13,40,640]{2,1,0:T(8,128)(2,1)S(1)}, u32[]{:S(2)}, u32[]{:S(2)}) collective-permute-start(bf16[13,40,640]{2,1,0:T(8,128)(2,1)} %get-tuple-element.109), channel_id=1, source_target_pairs={{0,4},{1,5},{2,6},{3,7},{4,0},{5,1},{6,2},{7,3},{8,12},{9,13},{10,... | collective-permute-start | bytes 1996808 | tf_op jit(solution)/shard_map/ppermute | solution.py:54
  339.9 66.9 %collective-permute-start.27 = (bf16[13,40,640]{2,1,0:T(8,128)(2,1)}, bf16[13,40,640]{2,1,0:T(8,128)(2,1)S(1)}, u32[]{:S(2)}, u32[]{:S(2)}) collective-permute-start(bf16[13,40,640]{2,1,0:T(8,128)(2,1)} %get-tuple-element.110), channel_id=1, source_target_pairs={{0,5},{1,4},{2,7},{3,6},{4,1},{5,0},{6,3},{7,2},{8,13},{9,12},{10,... | collective-permute-start | bytes 1996808 | tf_op jit(solution)/shard_map/ppermute | solution.py:54
  339.9 84.7 %collective-permute-start.28 = (bf16[13,40,640]{2,1,0:T(8,128)(2,1)}, bf16[13,40,640]{2,1,0:T(8,128)(2,1)}, u32[]{:S(2)}, u32[]{:S(2)}) collective-permute-start(bf16[13,40,640]{2,1,0:T(8,128)(2,1)} %get-tuple-element.111), channel_id=1, source_target_pairs={{0,6},{1,7},{2,4},{3,5},{4,2},{5,3},{6,0},{7,1},{8,14},{9,15},{10,... | collective-permute-start | bytes 1996808 | tf_op jit(solution)/shard_map/ppermute | solution.py:54
  340.0 114.8 %collective-permute-start.29 = (bf16[13,40,640]{2,1,0:T(8,128)(2,1)}, bf16[13,40,640]{2,1,0:T(8,128)(2,1)}, u32[]{:S(2)}, u32[]{:S(2)}) collective-permute-start(bf16[13,40,640]{2,1,0:T(8,128)(2,1)} %get-tuple-element.112), channel_id=1, source_target_pairs={{0,7},{1,6},{2,5},{3,4},{4,3},{5,2},{6,1},{7,0},{8,15},{9,14},{10,... | collective-permute-start | bytes 1996808 | tf_op jit(solution)/shard_map/ppermute | solution.py:54
  343.1 111.7 %collective-permute-start.3 = (bf16[13,40,640]{2,1,0:T(8,128)(2,1)}, bf16[13,40,640]{2,1,0:T(8,128)(2,1)S(1)}, u32[]{:S(2)}, u32[]{:S(2)}) collective-permute-start(bf16[13,40,640]{2,1,0:T(8,128)(2,1)} %get-tuple-element.82), channel_id=1, source_target_pairs={{0,1},{1,0},{2,3},{3,2},{4,5},{5,4},{6,7},{7,6},{8,9},{9,8},{10,11... | collective-permute-start | bytes 1996808 | tf_op jit(solution)/shard_map/ppermute | solution.py:54
  392.5 114.3 %copy-start.31 = (bf16[13,40,640]{2,1,0:T(8,128)(2,1)}, bf16[13,40,640]{2,1,0:T(8,128)(2,1)S(1)}, u32[]{:S(2)}) copy-start(bf16[13,40,640]{2,1,0:T(8,128)(2,1)S(1)} %collective-permute-done.26) | copy-start | bytes 1996804
  392.5 114.3 %collective-permute-start.4 = (bf16[13,40,640]{2,1,0:T(8,128)(2,1)}, bf16[13,40,640]{2,1,0:T(8,128)(2,1)S(1)}, u32[]{:S(2)}, u32[]{:S(2)}) collective-permute-start(bf16[13,40,640]{2,1,0:T(8,128)(2,1)} %get-tuple-element.83), channel_id=1, source_target_pairs={{0,2},{1,3},{2,0},{3,1},{4,6},{5,7},{6,4},{7,5},{8,10},{9,11},{10,... | collective-permute-start | bytes 1996808 | tf_op jit(solution)/shard_map/ppermute | solution.py:54
  406.8 102.2 %collective-permute-start.5 = (bf16[13,40,640]{2,1,0:T(8,128)(2,1)}, bf16[13,40,640]{2,1,0:T(8,128)(2,1)S(1)}, u32[]{:S(2)}, u32[]{:S(2)}) collective-permute-start(bf16[13,40,640]{2,1,0:T(8,128)(2,1)} %get-tuple-element.84), channel_id=1, source_target_pairs={{0,3},{1,2},{2,1},{3,0},{4,7},{5,6},{6,5},{7,4},{8,11},{9,10},{10,... | collective-permute-start | bytes 1996808 | tf_op jit(solution)/shard_map/ppermute | solution.py:54
  424.6 85.8 %collective-permute-start.6 = (bf16[13,40,640]{2,1,0:T(8,128)(2,1)}, bf16[13,40,640]{2,1,0:T(8,128)(2,1)S(1)}, u32[]{:S(2)}, u32[]{:S(2)}) collective-permute-start(bf16[13,40,640]{2,1,0:T(8,128)(2,1)} %get-tuple-element.85), channel_id=1, source_target_pairs={{0,4},{1,5},{2,6},{3,7},{4,0},{5,1},{6,2},{7,3},{8,12},{9,13},{10,... | collective-permute-start | bytes 1996808 | tf_op jit(solution)/shard_map/ppermute | solution.py:54
  454.8 59.6 %collective-permute-start.7 = (bf16[13,40,640]{2,1,0:T(8,128)(2,1)}, bf16[13,40,640]{2,1,0:T(8,128)(2,1)}, u32[]{:S(2)}, u32[]{:S(2)}) collective-permute-start(bf16[13,40,640]{2,1,0:T(8,128)(2,1)} %get-tuple-element.86), channel_id=1, source_target_pairs={{0,5},{1,4},{2,7},{3,6},{4,1},{5,0},{6,3},{7,2},{8,13},{9,12},{10,... | collective-permute-start | bytes 1996808 | tf_op jit(solution)/shard_map/ppermute | solution.py:54
  454.8 85.4 %collective-permute-start.8 = (bf16[13,40,640]{2,1,0:T(8,128)(2,1)}, bf16[13,40,640]{2,1,0:T(8,128)(2,1)}, u32[]{:S(2)}, u32[]{:S(2)}) collective-permute-start(bf16[13,40,640]{2,1,0:T(8,128)(2,1)} %get-tuple-element.87), channel_id=1, source_target_pairs={{0,6},{1,7},{2,4},{3,5},{4,2},{5,3},{6,0},{7,1},{8,14},{9,15},{10,... | collective-permute-start | bytes 1996808 | tf_op jit(solution)/shard_map/ppermute | solution.py:54
  506.8 60.8 %collective-permute-start.9 = (bf16[13,40,640]{2,1,0:T(8,128)(2,1)}, bf16[13,40,640]{2,1,0:T(8,128)(2,1)}, u32[]{:S(2)}, u32[]{:S(2)}) collective-permute-start(bf16[13,40,640]{2,1,0:T(8,128)(2,1)} %get-tuple-element.88), channel_id=1, source_target_pairs={{0,7},{1,6},{2,5},{3,4},{4,3},{5,2},{6,1},{7,0},{8,15},{9,14},{10,... | collective-permute-start | bytes 1996808 | tf_op jit(solution)/shard_map/ppermute | solution.py:54
  509.8 57.8 %collective-permute-start.50 = (bf16[13,40,640]{2,1,0:T(8,128)(2,1)}, bf16[13,40,640]{2,1,0:T(8,128)(2,1)S(1)}, u32[]{:S(2)}, u32[]{:S(2)}) collective-permute-start(bf16[13,40,640]{2,1,0:T(8,128)(2,1)} %bitcast.136), channel_id=1, source_target_pairs={{0,1},{1,0},{2,3},{3,2},{4,5},{5,4},{6,7},{7,6},{8,9},{9,8},{10,11... | collective-permute-start | bytes 1996808 | tf_op jit(solution)/shard_map/ppermute | solution.py:54
  510.3 57.4 %collective-permute-start.51 = (bf16[13,40,640]{2,1,0:T(8,128)(2,1)}, bf16[13,40,640]{2,1,0:T(8,128)(2,1)S(1)}, u32[]{:S(2)}, u32[]{:S(2)}) collective-permute-start(bf16[13,40,640]{2,1,0:T(8,128)(2,1)} %bitcast.135), channel_id=1, source_target_pairs={{0,2},{1,3},{2,0},{3,1},{4,6},{5,7},{6,4},{7,5},{8,10},{9,11},{10,... | collective-permute-start | bytes 1996808 | tf_op jit(solution)/shard_map/ppermute | solution.py:54
  514.4 106.9 %collective-permute-start.52 = (bf16[13,40,640]{2,1,0:T(8,128)(2,1)}, bf16[13,40,640]{2,1,0:T(8,128)(2,1)S(1)}, u32[]{:S(2)}, u32[]{:S(2)}) collective-permute-start(bf16[13,40,640]{2,1,0:T(8,128)(2,1)} %bitcast.128), channel_id=1, source_target_pairs={{0,3},{1,2},{2,1},{3,0},{4,7},{5,6},{6,5},{7,4},{8,11},{9,10},{10,... | collective-permute-start | bytes 1996808 | tf_op jit(solution)/shard_map/ppermute | solution.py:54
  540.2 92.1 %collective-permute-start.53 = (bf16[13,40,640]{2,1,0:T(8,128)(2,1)}, bf16[13,40,640]{2,1,0:T(8,128)(2,1)S(1)}, u32[]{:S(2)}, u32[]{:S(2)}) collective-permute-start(bf16[13,40,640]{2,1,0:T(8,128)(2,1)} %bitcast.127), channel_id=1, source_target_pairs={{0,4},{1,5},{2,6},{3,7},{4,0},{5,1},{6,2},{7,3},{8,12},{9,13},{10,... | collective-permute-start | bytes 1996808 | tf_op jit(solution)/shard_map/ppermute | solution.py:54
  567.6 79.0 %collective-permute-start.54 = (bf16[13,40,640]{2,1,0:T(8,128)(2,1)}, bf16[13,40,640]{2,1,0:T(8,128)(2,1)S(1)}, u32[]{:S(2)}, u32[]{:S(2)}) collective-permute-start(bf16[13,40,640]{2,1,0:T(8,128)(2,1)} %bitcast.126), channel_id=1, source_target_pairs={{0,5},{1,4},{2,7},{3,6},{4,1},{5,0},{6,3},{7,2},{8,13},{9,12},{10,... | collective-permute-start | bytes 1996808 | tf_op jit(solution)/shard_map/ppermute | solution.py:54
  567.6 98.9 %collective-permute-start.55 = (bf16[13,40,640]{2,1,0:T(8,128)(2,1)}, bf16[13,40,640]{2,1,0:T(8,128)(2,1)}, u32[]{:S(2)}, u32[]{:S(2)}) collective-permute-start(bf16[13,40,640]{2,1,0:T(8,128)(2,1)} %bitcast.123), channel_id=1, source_target_pairs={{0,6},{1,7},{2,4},{3,5},{4,2},{5,3},{6,0},{7,1},{8,14},{9,15},{10,... | collective-permute-start | bytes 1996808 | tf_op jit(solution)/shard_map/ppermute | solution.py:54
  567.7 129.6 %collective-permute-start.56 = (bf16[13,40,640]{2,1,0:T(8,128)(2,1)}, bf16[13,40,640]{2,1,0:T(8,128)(2,1)}, u32[]{:S(2)}, u32[]{:S(2)}) collective-permute-start(bf16[13,40,640]{2,1,0:T(8,128)(2,1)} %bitcast.120), channel_id=1, source_target_pairs={{0,7},{1,6},{2,5},{3,4},{4,3},{5,2},{6,1},{7,0},{8,15},{9,14},{10,... | collective-permute-start | bytes 1996808 | tf_op jit(solution)/shard_map/ppermute | solution.py:54
  621.3 127.6 %copy-start.8 = (bf16[13,40,640]{2,1,0:T(8,128)(2,1)}, bf16[13,40,640]{2,1,0:T(8,128)(2,1)S(1)}, u32[]{:S(2)}) copy-start(bf16[13,40,640]{2,1,0:T(8,128)(2,1)S(1)} %collective-permute-done.52.refs_3_) | copy-start | bytes 1996804
  621.3 127.6 %collective-permute-start.30 = (bf16[13,40,640]{2,1,0:T(8,128)(2,1)}, bf16[13,40,640]{2,1,0:T(8,128)(2,1)S(1)}, u32[]{:S(2)}, u32[]{:S(2)}) collective-permute-start(bf16[13,40,640]{2,1,0:T(8,128)(2,1)} %bitcast.134), channel_id=1, source_target_pairs={{0,1},{1,0},{2,3},{3,2},{4,5},{5,4},{6,7},{7,6},{8,9},{9,8},{10,11... | collective-permute-start | bytes 1996808 | tf_op jit(solution)/shard_map/ppermute | solution.py:54
  632.3 116.6 %copy-start.9 = (bf16[13,40,640]{2,1,0:T(8,128)(2,1)}, bf16[13,40,640]{2,1,0:T(8,128)(2,1)S(1)}, u32[]{:S(2)}) copy-start(bf16[13,40,640]{2,1,0:T(8,128)(2,1)S(1)} %collective-permute-done.53.refs_4_) | copy-start | bytes 1996804
  632.3 116.7 %collective-permute-start.31 = (bf16[13,40,640]{2,1,0:T(8,128)(2,1)}, bf16[13,40,640]{2,1,0:T(8,128)(2,1)S(1)}, u32[]{:S(2)}, u32[]{:S(2)}) collective-permute-start(bf16[13,40,640]{2,1,0:T(8,128)(2,1)} %bitcast.133), channel_id=1, source_target_pairs={{0,2},{1,3},{2,0},{3,1},{4,6},{5,7},{6,4},{7,5},{8,10},{9,11},{10,... | collective-permute-start | bytes 1996808 | tf_op jit(solution)/shard_map/ppermute | solution.py:54
  646.6 102.3 %copy-start.11 = (bf16[13,40,640]{2,1,0:T(8,128)(2,1)}, bf16[13,40,640]{2,1,0:T(8,128)(2,1)S(1)}, u32[]{:S(2)}) copy-start(bf16[13,40,640]{2,1,0:T(8,128)(2,1)S(1)} %collective-permute-done.54.refs_5_) | copy-start | bytes 1996804
  646.6 104.5 %collective-permute-start.32 = (bf16[13,40,640]{2,1,0:T(8,128)(2,1)}, bf16[13,40,640]{2,1,0:T(8,128)(2,1)}, u32[]{:S(2)}, u32[]{:S(2)}) collective-permute-start(bf16[13,40,640]{2,1,0:T(8,128)(2,1)} %bitcast.131), channel_id=1, source_target_pairs={{0,3},{1,2},{2,1},{3,0},{4,7},{5,6},{6,5},{7,4},{8,11},{9,10},{10,... | collective-permute-start | bytes 1996808 | tf_op jit(solution)/shard_map/ppermute | solution.py:54
  666.5 85.1 %collective-permute-start.33 = (bf16[13,40,640]{2,1,0:T(8,128)(2,1)}, bf16[13,40,640]{2,1,0:T(8,128)(2,1)}, u32[]{:S(2)}, u32[]{:S(2)}) collective-permute-start(bf16[13,40,640]{2,1,0:T(8,128)(2,1)} %bitcast.129), channel_id=1, source_target_pairs={{0,4},{1,5},{2,6},{3,7},{4,0},{5,1},{6,2},{7,3},{8,12},{9,13},{10,... | collective-permute-start | bytes 1996808 | tf_op jit(solution)/shard_map/ppermute | solution.py:54
  697.3 69.4 %collective-permute-start.34 = (bf16[13,40,640]{2,1,0:T(8,128)(2,1)}, bf16[13,40,640]{2,1,0:T(8,128)(2,1)}, u32[]{:S(2)}, u32[]{:S(2)}) collective-permute-start(bf16[13,40,640]{2,1,0:T(8,128)(2,1)} %bitcast.124), channel_id=1, source_target_pairs={{0,5},{1,4},{2,7},{3,6},{4,1},{5,0},{6,3},{7,2},{8,13},{9,12},{10,... | collective-permute-start | bytes 1996808 | tf_op jit(solution)/shard_map/ppermute | solution.py:54
  748.9 44.8 %collective-permute-start.35 = (bf16[13,40,640]{2,1,0:T(8,128)(2,1)}, bf16[13,40,640]{2,1,0:T(8,128)(2,1)S(1)}, u32[]{:S(2)}, u32[]{:S(2)}) collective-permute-start(bf16[13,40,640]{2,1,0:T(8,128)(2,1)} %bitcast.121), channel_id=1, source_target_pairs={{0,6},{1,7},{2,4},{3,5},{4,2},{5,3},{6,0},{7,1},{8,14},{9,15},{10,... | collective-permute-start | bytes 1996808 | tf_op jit(solution)/shard_map/ppermute | solution.py:54
  749.0 69.6 %collective-permute-start.36 = (bf16[13,40,640]{2,1,0:T(8,128)(2,1)}, bf16[13,40,640]{2,1,0:T(8,128)(2,1)}, u32[]{:S(2)}, u32[]{:S(2)}) collective-permute-start(bf16[13,40,640]{2,1,0:T(8,128)(2,1)} %bitcast.118), channel_id=1, source_target_pairs={{0,7},{1,6},{2,5},{3,4},{4,3},{5,2},{6,1},{7,0},{8,15},{9,14},{10,... | collective-permute-start | bytes 1996808 | tf_op jit(solution)/shard_map/ppermute | solution.py:54
  751.1 67.5 %collective-permute-start.10 = (bf16[13,40,640]{2,1,0:T(8,128)(2,1)}, bf16[13,40,640]{2,1,0:T(8,128)(2,1)S(1)}, u32[]{:S(2)}, u32[]{:S(2)}) collective-permute-start(bf16[13,40,640]{2,1,0:T(8,128)(2,1)} %bitcast.132), channel_id=1, source_target_pairs={{0,1},{1,0},{2,3},{3,2},{4,5},{5,4},{6,7},{7,6},{8,9},{9,8},{10,11... | collective-permute-start | bytes 1996808 | tf_op jit(solution)/shard_map/ppermute | solution.py:54
  751.6 69.3 %collective-permute-start.11 = (bf16[13,40,640]{2,1,0:T(8,128)(2,1)}, bf16[13,40,640]{2,1,0:T(8,128)(2,1)S(1)}, u32[]{:S(2)}, u32[]{:S(2)}) collective-permute-start(bf16[13,40,640]{2,1,0:T(8,128)(2,1)} %bitcast.130), channel_id=1, source_target_pairs={{0,2},{1,3},{2,0},{3,1},{4,6},{5,7},{6,4},{7,5},{8,10},{9,11},{10,... | collective-permute-start | bytes 1996808 | tf_op jit(solution)/shard_map/ppermute | solution.py:54
  766.7 167.6 %collective-permute-start.57 = (bf16[4,8,40,640]{3,2,1,0:T(8,128)(2,1)}, bf16[4,8,40,640]{3,2,1,0:T(8,128)(2,1)}, u32[]{:S(2)}, u32[]{:S(2)}) collective-permute-start(bf16[4,8,40,640]{3,2,1,0:T(8,128)(2,1)} %get-tuple-element.146), channel_id=1, source_target_pairs={{0,8},{8,0},{16,24},{24,16},{1,9},{9,1},{17,25},{25,17},{2,10},{10... | collective-permute-start | bytes 4915208 | tf_op jit(solution)/shard_map/ppermute | solution.py:54
  794.5 39.0 %collective-permute-start.12 = (bf16[13,40,640]{2,1,0:T(8,128)(2,1)}, bf16[13,40,640]{2,1,0:T(8,128)(2,1)S(1)}, u32[]{:S(2)}, u32[]{:S(2)}) collective-permute-start(bf16[13,40,640]{2,1,0:T(8,128)(2,1)} %bitcast.125), channel_id=1, source_target_pairs={{0,3},{1,2},{2,1},{3,0},{4,7},{5,6},{6,5},{7,4},{8,11},{9,10},{10,... | collective-permute-start | bytes 1996808 | tf_op jit(solution)/shard_map/ppermute | solution.py:54
  818.6 55.7 %collective-permute-start.13 = (bf16[13,40,640]{2,1,0:T(8,128)(2,1)}, bf16[13,40,640]{2,1,0:T(8,128)(2,1)S(1)}, u32[]{:S(2)}, u32[]{:S(2)}) collective-permute-start(bf16[13,40,640]{2,1,0:T(8,128)(2,1)} %bitcast.122), channel_id=1, source_target_pairs={{0,4},{1,5},{2,6},{3,7},{4,0},{5,1},{6,2},{7,3},{8,12},{9,13},{10,... | collective-permute-start | bytes 1996808 | tf_op jit(solution)/shard_map/ppermute | solution.py:54
  818.6 70.0 %collective-permute-start.14 = (bf16[13,40,640]{2,1,0:T(8,128)(2,1)}, bf16[13,40,640]{2,1,0:T(8,128)(2,1)S(1)}, u32[]{:S(2)}, u32[]{:S(2)}) collective-permute-start(bf16[13,40,640]{2,1,0:T(8,128)(2,1)} %bitcast.119), channel_id=1, source_target_pairs={{0,5},{1,4},{2,7},{3,6},{4,1},{5,0},{6,3},{7,2},{8,13},{9,12},{10,... | collective-permute-start | bytes 1996808 | tf_op jit(solution)/shard_map/ppermute | solution.py:54
  820.9 97.2 %collective-permute-start.15 = (bf16[13,40,640]{2,1,0:T(8,128)(2,1)}, bf16[13,40,640]{2,1,0:T(8,128)(2,1)}, u32[]{:S(2)}, u32[]{:S(2)}) collective-permute-start(bf16[13,40,640]{2,1,0:T(8,128)(2,1)} %bitcast.117), channel_id=1, source_target_pairs={{0,6},{1,7},{2,4},{3,5},{4,2},{5,3},{6,0},{7,1},{8,14},{9,15},{10,... | collective-permute-start | bytes 1996808 | tf_op jit(solution)/shard_map/ppermute | solution.py:54
  833.5 116.9 %collective-permute-start.58 = (bf16[4,8,40,640]{3,2,1,0:T(8,128)(2,1)}, bf16[4,8,40,640]{3,2,1,0:T(8,128)(2,1)}, u32[]{:S(2)}, u32[]{:S(2)}) collective-permute-start(bf16[4,8,40,640]{3,2,1,0:T(8,128)(2,1)} %get-tuple-element.147), channel_id=1, source_target_pairs={{0,16},{8,24},{16,0},{24,8},{1,17},{9,25},{17,1},{25,9},{2,18},{10... | collective-permute-start | bytes 4915208 | tf_op jit(solution)/shard_map/ppermute | solution.py:54
  874.3 76.2 %collective-permute-start.59 = (bf16[4,8,40,640]{3,2,1,0:T(8,128)(2,1)}, bf16[4,8,40,640]{3,2,1,0:T(8,128)(2,1)}, u32[]{:S(2)}, u32[]{:S(2)}) collective-permute-start(bf16[4,8,40,640]{3,2,1,0:T(8,128)(2,1)} %get-tuple-element.148), channel_id=1, source_target_pairs={{0,24},{8,16},{16,8},{24,0},{1,25},{9,17},{17,9},{25,1},{2,26},{10... | collective-permute-start | bytes 4915208 | tf_op jit(solution)/shard_map/ppermute | solution.py:54
  889.4 62.4 %collective-permute-start.37 = (bf16[4,8,40,640]{3,2,1,0:T(8,128)(2,1)}, bf16[4,8,40,640]{3,2,1,0:T(8,128)(2,1)S(1)}, u32[]{:S(2)}, u32[]{:S(2)}) collective-permute-start(bf16[4,8,40,640]{3,2,1,0:T(8,128)(2,1)} %get-tuple-element.122), channel_id=1, source_target_pairs={{0,8},{8,0},{16,24},{24,16},{1,9},{9,1},{17,25},{25,17},{2,10},{10... | collective-permute-start | bytes 4915208 | tf_op jit(solution)/shard_map/ppermute | solution.py:54
  918.1 14.9 %collective-permute-start.16 = (bf16[13,40,640]{2,1,0:T(8,128)(2,1)}, bf16[13,40,640]{2,1,0:T(8,128)(2,1)S(1)}, u32[]{:S(2)}, u32[]{:S(2)}) collective-permute-start(bf16[13,40,640]{2,1,0:T(8,128)(2,1)} %bitcast.115), channel_id=1, source_target_pairs={{0,7},{1,6},{2,5},{3,4},{4,3},{5,2},{6,1},{7,0},{8,15},{9,14},{10,... | collective-permute-start | bytes 1996808 | tf_op jit(solution)/shard_map/ppermute | solution.py:54
  933.0 38.2 %collective-permute-start.38 = (bf16[4,8,40,640]{3,2,1,0:T(8,128)(2,1)}, bf16[4,8,40,640]{3,2,1,0:T(8,128)(2,1)S(1)}, u32[]{:S(2)}, u32[]{:S(2)}) collective-permute-start(bf16[4,8,40,640]{3,2,1,0:T(8,128)(2,1)} %get-tuple-element.123), channel_id=1, source_target_pairs={{0,16},{8,24},{16,0},{24,8},{1,17},{9,25},{17,1},{25,9},{2,18},{10... | collective-permute-start | bytes 4915208 | tf_op jit(solution)/shard_map/ppermute | solution.py:54
  934.3 75.7 %collective-permute-start.39 = (bf16[4,8,40,640]{3,2,1,0:T(8,128)(2,1)}, bf16[4,8,40,640]{3,2,1,0:T(8,128)(2,1)}, u32[]{:S(2)}, u32[]{:S(2)}) collective-permute-start(bf16[4,8,40,640]{3,2,1,0:T(8,128)(2,1)} %get-tuple-element.124), channel_id=1, source_target_pairs={{0,24},{8,16},{16,8},{24,0},{1,25},{9,17},{17,9},{25,1},{2,26},{10... | collective-permute-start | bytes 4915208 | tf_op jit(solution)/shard_map/ppermute | solution.py:54
  950.5 77.8 %collective-permute-start.17 = (bf16[4,8,40,640]{3,2,1,0:T(8,128)(2,1)}, bf16[4,8,40,640]{3,2,1,0:T(8,128)(2,1)}, u32[]{:S(2)}, u32[]{:S(2)}) collective-permute-start(bf16[4,8,40,640]{3,2,1,0:T(8,128)(2,1)} %get-tuple-element.98), channel_id=1, source_target_pairs={{0,8},{8,0},{16,24},{24,16},{1,9},{9,1},{17,25},{25,17},{2,10},{10... | collective-permute-start | bytes 4915208 | tf_op jit(solution)/shard_map/ppermute | solution.py:54
  950.6 86.7 %collective-permute-start.18 = (bf16[4,8,40,640]{3,2,1,0:T(8,128)(2,1)}, bf16[4,8,40,640]{3,2,1,0:T(8,128)(2,1)}, u32[]{:S(2)}, u32[]{:S(2)}) collective-permute-start(bf16[4,8,40,640]{3,2,1,0:T(8,128)(2,1)} %get-tuple-element.99), channel_id=1, source_target_pairs={{0,16},{8,24},{16,0},{24,8},{1,17},{9,25},{17,1},{25,9},{2,18},{10... | collective-permute-start | bytes 4915208 | tf_op jit(solution)/shard_map/ppermute | solution.py:54
  951.8 124.4 %collective-permute-start.19 = (bf16[4,8,40,640]{3,2,1,0:T(8,128)(2,1)}, bf16[4,8,40,640]{3,2,1,0:T(8,128)(2,1)}, u32[]{:S(2)}, u32[]{:S(2)}) collective-permute-start(bf16[4,8,40,640]{3,2,1,0:T(8,128)(2,1)} %get-tuple-element.100), channel_id=1, source_target_pairs={{0,24},{8,16},{16,8},{24,0},{1,25},{9,17},{17,9},{25,1},{2,26},{10... | collective-permute-start | bytes 4915208 | tf_op jit(solution)/shard_map/ppermute | solution.py:54
  (32 other events, 835.8 us)
